TPU v7x, 32 devices: a whole 2x2x4 slice. The times are simulated.
32 devices in a mesh: example: 4 (over x, core), seq: 8 (over z, y).
Axes of the slice: x: 2, y: 2, z: 4, core: 2. Of those that a mesh axis runs over, the one named last changes fastest.
Arguments:
- activations: bfloat16 [4, 2048, 4096], P('example', 'seq'), may hold values from -6 to 6
- gate_weight: bfloat16 [4096, 256], P('seq'), may hold values from -0.09375 to 0.09375
- seeds: bfloat16 [4, 2048, 256], P('example', 'seq'), may hold values from -6 to 6
Outputs:
- fisher: float32 [4096, 256], P('seq', 'example')
All inputs are finite; a program needn't handle non-finite values.
Results may differ from a plain program's by a relative error of at most 0.0024.
Values may be sent and summed in bfloat16 or wider, within the bound.
No kernel may reach another device: no remote copies, remote signals or barrier semaphores. Data moves between devices by JAX's collectives and lax.ppermute only.
A program may use at most 64 MiB of HBM per device.

v0:
```python
import jax
import jax.numpy as jnp
from jax import lax
from jax.sharding import PartitionSpec as P


def local_terms(cotangent, pre):
    sigma = jax.nn.sigmoid(pre)
    return (cotangent.astype(jnp.float32) * sigma * (1.0 + pre * (1.0 - sigma))).astype(
        jnp.bfloat16
    )


def body(activations, gate_weight, seeds):
    inputs = activations[0]
    cotangent = seeds[0]
    tokens_here = inputs.shape[0]
    seq_count = lax.axis_size("seq")
    scale = 1.0 / jnp.sqrt(jnp.float32(tokens_here * seq_count))
    columns = inputs
    pre = jnp.dot(
        columns,
        lax.all_gather(gate_weight, "seq", axis=0, tiled=True),
        preferred_element_type=jnp.float32,
    )
    local = local_terms(cotangent, pre)
    columns = inputs
    product = lax.dot_general(
        columns, local, (((0,), (0,)), ((), ())), preferred_element_type=jnp.float32
    )
    grad = lax.psum_scatter(product * scale, "seq", scatter_dimension=0, tiled=True)
    squared = grad * grad
    total = lax.psum_scatter(squared, "example", scatter_dimension=1, tiled=True)
    return total / jnp.float32(lax.axis_size("example"))


def solution(mesh):
    return jax.shard_map(
        body,
        mesh=mesh,
        in_specs=(P("example", "seq", None), P("seq", None), P("example", "seq", None)),
        out_specs=P("seq", "example"),
        check_vma=False,
    )
```

profile of v0, /device:TPU:0, one launch (start us, length us, event | category | flops | bytes accessed | tf_op | source)
XLA Modules:
  0.0 186.8 jit_solution(13366943485582377419)
XLA Ops:
  6.5 0.0 copy-start
  6.5 0.0 all-gather.2.cloned.1.call-start
  6.5 0.7 all-gather.2.cloned.1.call-update
  7.3 0.0 reduce-scatter.3.cloned.1.call-start
  7.3 54.2 %all-gather.2.cloned.1.call-done = bf16[4096,256]{1,0:T(8,128)(2,1)} async-done(((bf16[512,256]{1,0:T(8,128)(2,1)}), bf16[4096,256]{1,0:T(8,128)(2,1)}) %all-gather.2.cloned.1.call-update) | async-done | bytes 2097168 | tf_op jit(solution)/shard_map/all_gather | solution.py:23
  61.5 0.0 copy-done
  61.5 6.0 %fusion = f32[4096,256]{0,1:T(8,128)} fusion(bf16[1,256,4096]{2,1,0:T(8,128)(2,1)S(1)} %copy-done, bf16[4096,256]{1,0:T(8,128)(2,1)} %all-gather.2.cloned.1.call-done, bf16[1,256,256]{2,1,0:T(8,128)(2,1)} %param.5), kind=kOutput, calls=%fused_computation.1 | convolution fusion | flops 1075445760 | bytes 8519680 | tf_op jit(solution)/shard_map/dot_general | solution.py:28
  67.6 0.0 reduce-scatter.3.cloned.1.call-update
  67.6 0.0 reduce-scatter.5.cloned.1.call-start
  67.6 87.0 %reduce-scatter.3.cloned.1.call-done = f32[512,256]{0,1:T(8,128)} async-done(((f32[4096,256]{0,1:T(8,128)}), f32[512,256]{0,1:T(8,128)}) %reduce-scatter.3.cloned.1.call-update) | async-done | bytes 524304 | tf_op jit(solution)/shard_map/reduce_scatter | solution.py:31
  154.7 2.1 %mul.27 = f32[512,256]{0,1:T(8,128)} multiply(f32[512,256]{0,1:T(8,128)} %reduce-scatter.3.cloned.1.call-done, f32[512,256]{0,1:T(8,128)} %reduce-scatter.3.cloned.1.call-done) | non-fusion elementwise | flops 131072 | bytes 1572864 | tf_op jit(solution)/shard_map/mul | solution.py:32
  156.7 0.0 reduce-scatter.5.cloned.1.call-update
  156.8 22.0 %reduce-scatter.5.cloned.1.call-done = f32[512,64]{0,1:T(8,128)} async-done(((f32[512,256]{0,1:T(8,128)}), f32[512,64]{0,1:T(8,128)}) %reduce-scatter.5.cloned.1.call-update) | async-done | bytes 131088 | tf_op jit(solution)/shard_map/reduce_scatter | solution.py:33
  178.7 1.6 broadcast_multiply_fusion
Async XLA Ops:
  6.5 55.0 %copy-start = (bf16[1,256,4096]{2,1,0:T(8,128)(2,1)S(1)}, bf16[1,256,4096]{2,1,0:T(8,128)(2,1)}, u32[]{:S(2)}) copy-start(bf16[1,256,4096]{2,1,0:T(8,128)(2,1)} %param.3) | copy-start | bytes 6291460
  6.5 55.0 %all-gather.2.cloned.1.call-start = ((), (), s32[]{:S(2)}) async-start(), calls=%async_computation.2 | async-start | bytes 2359296 | tf_op jit(solution)/shard_map/all_gather | solution.py:23
  7.3 147.4 %reduce-scatter.3.cloned.1.call-start = ((), (), s32[]{:S(2)}) async-start(), calls=%async_computation.3 | async-start | bytes 4718592 | tf_op jit(solution)/shard_map/reduce_scatter | solution.py:31
  67.6 111.2 %reduce-scatter.5.cloned.1.call-start = ((), (), s32[]{:S(2)}) async-start(), calls=%async_computation.4 | async-start | bytes 655360 | tf_op jit(solution)/shard_map/reduce_scatter | solution.py:33
Sparse Core Ops, SparseCore 0:
  9.5 51.9 all-gather.1
  67.7 86.9 reduce-scatter.2
  157.3 21.3 reduce-scatter.4
where the time goes:
time: 187 us
  waiting for transfers between devices  164 us (88%)
  between operations  13.1 us (7%)
  matrix products  6.04 us (3%)
  other arithmetic  3.64 us (2%)
    reduce_scatter x1, waiting for transfers between devices, body(): lax.psum_scatter(product * scale, 'seq', scatter_dimension=0, tiled=True)  87 us
    all_gather x1, waiting for transfers between devices, body(): lax.all_gather(gate_weight, 'seq', axis=0, tiled=True)  54.2 us
    reduce_scatter x1, waiting for transfers between devices, body(): lax.psum_scatter(squared, 'example', scatter_dimension=1, tiled=True)  22 us
    dot_general x1, matrix products, body(): lax.dot_general(columns, local, (((0,), (0,)), ((), ())), preferred_eleme...  6.04 us
  transfers between devices with their start and end apart: 3, of which 3 were waited for; matrix products, arithmetic and copies ran while one was open for 0% of the time, Pallas kernels for 0%

commit v1 on v0

v1 whole, which is shorter than its diff:
```python
import functools

import jax
import jax.numpy as jnp
from jax import lax
from jax.experimental import pallas as pl
from jax.experimental.pallas import tpu as pltpu
from jax.sharding import PartitionSpec as P

F32 = jnp.float32
BF16 = jnp.bfloat16


def local_terms(cotangent, pre):
    sigma = jax.nn.sigmoid(pre)
    return (cotangent.astype(F32) * sigma * (1.0 + pre * (1.0 - sigma))).astype(BF16)


def hop(x, axis, k):
    return lax.ppermute(x, axis, [(i, i ^ k) for i in range(lax.axis_size(axis))])


def columns(block, size):
    return pl.ds(pl.multiple_of(block * size, 128), size)


def call(kernel, outs, flops, *operands):
    vmem = pl.BlockSpec(memory_space=pltpu.VMEM)
    moved = sum(x.size * x.dtype.itemsize for x in (*operands, *outs))
    return pl.pallas_call(
        kernel,
        out_shape=tuple(outs),
        in_specs=[vmem] * len(operands),
        out_specs=(vmem,) * len(outs),
        compiler_params=pltpu.CompilerParams(vmem_limit_bytes=48 * 2**20),
        cost_estimate=pl.CostEstimate(flops=flops, bytes_accessed=moved, transcendentals=0),
    )(*operands)


def local_kernel(rows, *refs):
    a, seeds, own, *pieces = refs[:-2]
    local_ref, first = refs[-2:]
    half = rows // 2
    me = lax.axis_index("seq")
    core = lax.rem(lax.axis_index("example"), 2)
    pre = jnp.dot(a[:, columns(me, rows)], own[...], preferred_element_type=F32)
    count = lax.axis_size("seq")
    for k in range(1, count):
        for flip in range(2):
            block = 2 * (me ^ k) + (core ^ flip)
            pre += jnp.dot(
                a[:, columns(block, half)], pieces[2 * (k - 1) + flip][...], preferred_element_type=F32
            )
    local_t = local_terms(seeds[...], pre).T
    local_ref[...] = local_t
    k = count - 1
    first[...] = jnp.dot(
        local_t, a[:, columns(me ^ k, rows)], preferred_element_type=F32
    ).astype(first.dtype)


def product_kernel(rows, blocks, a, local_t, *outs):
    me = lax.axis_index("seq")
    for k, out in zip(blocks, outs):
        out[...] = jnp.dot(
            local_t[...], a[:, columns(me ^ k, rows)], preferred_element_type=F32
        ).astype(out.dtype)


def add_kernel(mine, other, out):
    out[...] = (mine[...] + other[...].astype(F32)).astype(out.dtype)


def square_kernel(mine, *refs):
    examples = lax.axis_size("example")
    arrived, outs = refs[: len(refs) - examples], refs[len(refs) - examples :]
    me = lax.axis_index("example")
    size = outs[0].shape[0]
    for k, out in enumerate(outs):
        part = pl.ds(pl.multiple_of((me ^ k) * size, size), size)
        grad = mine[part, :]
        for other in arrived:
            grad += other[part, :].astype(F32)
        out[...] = (grad * grad).astype(out.dtype)


def mean_kernel(scale, own, *refs):
    total = own[...]
    for other in refs[:-1]:
        total += other[...].astype(F32)
    refs[-1][...] = total * scale


def direct(activations, gate_weight, seeds):
    inputs, cotangent = activations[0], seeds[0]
    tokens, width = inputs.shape
    rows, hidden = gate_weight.shape
    count, examples = lax.axis_size("seq"), lax.axis_size("example")
    core = lax.rem(lax.axis_index("example"), 2)
    lines = count // 2

    half = lax.dynamic_slice_in_dim(gate_weight, core * (rows // 2), rows // 2)
    held = {0: half}
    for k in range(1, lines):
        held[2 * k] = hop(half, "seq", 2 * k)
    for k in range(lines):
        held[2 * k + 1] = hop(held[2 * k], "seq", 1)
    pieces = []
    for k in range(1, count):
        pieces += [held[k], hop(held[k], "example", 1)]

    dots = 2 * tokens * hidden
    block = lambda dtype: jax.ShapeDtypeStruct((hidden, rows), dtype)
    local_t, first = call(
        functools.partial(local_kernel, rows),
        (jax.ShapeDtypeStruct((hidden, tokens), BF16), block(BF16)),
        dots * (width + rows),
        inputs, cotangent, gate_weight, *pieces,
    )
    order = [2 * k for k in reversed(range(lines))]
    sent = {order[0]: first}
    later = [k + 1 for k in order[1:]] + order
    made = call(
        functools.partial(product_kernel, rows, later),
        [block(BF16)] * (lines - 1) + [block(F32)] * lines,
        dots * rows * len(later),
        inputs, local_t,
    )
    sent.update(zip(order[1:], made))
    mine = dict(zip(order, made[lines - 1 :]))

    arrived = []
    for k in order:
        other = hop(sent[k], "seq", 1)
        if k:
            (pair,) = call(add_kernel, (block(BF16),), mine[k].size, mine[k], other)
            arrived.append(hop(pair, "seq", k))
        else:
            arrived.append(other)

    size = hidden // examples
    part = lambda dtype: jax.ShapeDtypeStruct((size, rows), dtype)
    own, *others = call(
        square_kernel, [part(F32)] + [part(BF16)] * (examples - 1), 8 * hidden * rows, mine[0], *arrived
    )
    others = [hop(x, "example", k + 1) for k, x in enumerate(others)]
    (total,) = call(
        functools.partial(mean_kernel, 1.0 / (tokens * count * examples)),
        (part(F32),), 4 * size * rows, own, *others,
    )
    return total.T


def plain(activations, gate_weight, seeds):
    inputs, cotangent = activations[0], seeds[0]
    count, examples = lax.axis_size("seq"), lax.axis_size("example")
    weights = lax.all_gather(gate_weight, "seq", axis=0, tiled=True)
    pre = jnp.dot(inputs, weights, preferred_element_type=F32)
    local = local_terms(cotangent, pre)
    product = lax.dot_general(inputs, local, (((0,), (0,)), ((), ())), preferred_element_type=F32)
    grad = lax.psum_scatter(product, "seq", scatter_dimension=0, tiled=True)
    total = lax.psum_scatter(grad * grad, "example", scatter_dimension=1, tiled=True)
    return total * (1.0 / (inputs.shape[0] * count * examples))


def body(activations, gate_weight, seeds):
    rows, hidden = gate_weight.shape
    aligned = rows % 256 == 0 and (hidden // lax.axis_size("example")) % 16 == 0
    return (direct if aligned else plain)(activations, gate_weight, seeds)


def solution(mesh):
    return jax.shard_map(
        body,
        mesh=mesh,
        in_specs=(P("example", "seq", None), P("seq", None), P("example", "seq", None)),
        out_specs=P("seq", "example"),
        check_vma=False,
    )
```

time: 187 us -> 71.5 us (0.38)
  waiting for transfers between devices: 164 us -> 38.8 us
  starting transfers between devices: 0.08 us -> 25.3 us
  between operations: 13.1 us -> 0.08 us
  matrix products: 6.04 us -> 0 us
  local copies, waits for them, and re-layouts: 0.01 us -> 4.36 us
  other arithmetic: 3.64 us -> 0 us
  Pallas kernels: 0 us -> 2.75 us
    reduce_scatter x2 -> x0, waiting for transfers between devices: 109 us -> none  [the longest x1 87 us: body(): lax.psum_scatter(product * scale, 'seq', scatter_dimension=0, tiled=True)]
    all_gather x1 -> x0, waiting for transfers between devices: 54.2 us -> none  [body(): lax.all_gather(gate_weight, 'seq', axis=0, tiled=True)]
    ppermute x0 -> x24, waiting for transfers between devices: none -> 38.8 us  [hop(): lax.ppermute(x, axis, [(i, i ^ k) for i in range(lax.axis_size(axis))])]
    ppermute x0 -> x24, starting transfers between devices: none -> 25.3 us  [hop(): lax.ppermute(x, axis, [(i, i ^ k) for i in range(lax.axis_size(axis))])]
    dot_general x1 -> x0, matrix products: 6.04 us -> none  [body(): lax.dot_general(columns, local, (((0,), (0,)), ((), ())), preferred_eleme...]
    unnamed x2 -> x6, local copies, waits for them, and re-layouts: 0.01 us -> 3.44 us
    pallas_call x0 -> x7, Pallas kernels: none -> 2.75 us  [call(): pl.pallas_call(kernel, out_shape=tuple(outs), in_specs=[vmem] * len(opera...]
    mul x1 -> x0, other arithmetic: 2.08 us -> none  [body(): squared = grad * grad]
  transfers between devices with their start and end apart: 3 -> 24, of which waited for: 3 -> 12; matrix products, arithmetic and copies ran while one was open for 0% -> 0% of each run, Pallas kernels for 0% -> 1%
where the time goes in v1:
time: 71.5 us; the launch traced here: 71.2 us
  waiting for transfers between devices  38.8 us (54%)
  starting transfers between devices  25.3 us (35%)
  local copies, waits for them, and re-layouts  4.36 us (6%)
  Pallas kernels  2.75 us (4%)
    ppermute x24, waiting for transfers between devices, hop(): lax.ppermute(x, axis, [(i, i ^ k) for i in range(lax.axis_size(axis))])  38.8 us
    ppermute x24, starting transfers between devices, hop(): lax.ppermute(x, axis, [(i, i ^ k) for i in range(lax.axis_size(axis))])  25.3 us
    unnamed x6, local copies, waits for them, and re-layouts  3.44 us
    pallas_call x7, Pallas kernels, call(): pl.pallas_call(kernel, out_shape=tuple(outs), in_specs=[vmem] * len(opera...  2.75 us
  transfers between devices with their start and end apart: 24, of which 12 were waited for; matrix products, arithmetic and copies ran while one was open for 0% of the time, Pallas kernels for 1%

profile of v1, /device:TPU:0, one launch (start us, length us, event | category | flops | bytes accessed | tf_op | source)
XLA Modules:
  0.0 71.2 jit_solution(2364875015430156743)
XLA Ops:
  0.0 0.9 %constant_dynamic-slice_fusion = bf16[256,256]{1,0:T(8,128)(2,1)S(1)} fusion(bf16[512,256]{1,0:T(8,128)(2,1)} %refs_2_.1, s32[]{:T(128)S(6)} %select_n.3), kind=kLoop, calls=%fused_computation | loop fusion | bytes 262148 | tf_op jit(solution)/shard_map/dynamic_slice | solution.py:102
  0.9 5.1 %collective-permute-start.10 = (bf16[256,256]{1,0:T(8,128)(2,1)S(1)}, bf16[256,256]{1,0:T(8,128)(2,1)S(1)}, u32[]{:S(2)}, u32[]{:S(2)}) collective-permute-start(bf16[256,256]{1,0:T(8,128)(2,1)S(1)} %constant_dynamic-slice_fusion), channel_id=1, source_target_pairs={{0,6},{1,7},{2,4},{3,5},{4,2},{5,3},{6,0},{7,1},{8,14},{9,15},{10,... | collective-permute-start | bytes 393224 | tf_op jit(solution)/shard_map/ppermute | solution.py:20
  6.0 0.0 collective-permute-start.6
  6.0 0.6 collective-permute-start.2
  6.7 1.7 %collective-permute-start = (bf16[256,256]{1,0:T(8,128)(2,1)S(1)}, bf16[256,256]{1,0:T(8,128)(2,1)S(1)}, u32[]{:S(2)}, u32[]{:S(2)}) collective-permute-start(bf16[256,256]{1,0:T(8,128)(2,1)S(1)} %constant_dynamic-slice_fusion), channel_id=1, source_target_pairs={{0,1},{1,0},{2,3},{3,2},{4,5},{5,4},{6,7},{7,6},{8,9},{9,8},{10,11... | collective-permute-start | bytes 393224 | tf_op jit(solution)/shard_map/ppermute | solution.py:20
  8.3 2.1 %collective-permute-done.10.refs_13_ = bf16[256,256]{1,0:T(8,128)(2,1)S(1)} collective-permute-done((bf16[256,256]{1,0:T(8,128)(2,1)S(1)}, bf16[256,256]{1,0:T(8,128)(2,1)S(1)}, u32[]{:S(2)}, u32[]{:S(2)}) %collective-permute-start.10) | collective-permute-done | bytes 131104 | tf_op jit(solution)/shard_map/ppermute | solution.py:20
  10.5 1.7 %collective-permute-start.12 = (bf16[256,256]{1,0:T(8,128)(2,1)S(1)}, bf16[256,256]{1,0:T(8,128)(2,1)S(1)}, u32[]{:S(2)}, u32[]{:S(2)}) collective-permute-start(bf16[256,256]{1,0:T(8,128)(2,1)S(1)} %collective-permute-done.10.refs_13_), channel_id=1, source_target_pairs={{0,1},{1,0},{2,3},{3,2},{4,5},{5,4},{6,7},{7,6},{8,9},{9,8},{10,11... | collective-permute-start | bytes 393224 | tf_op jit(solution)/shard_map/ppermute | solution.py:20
  12.2 0.0 collective-permute-start.11
  12.2 4.9 %collective-permute-done.6.refs_9_ = bf16[256,256]{1,0:T(8,128)(2,1)S(1)} collective-permute-done((bf16[256,256]{1,0:T(8,128)(2,1)S(1)}, bf16[256,256]{1,0:T(8,128)(2,1)S(1)}, u32[]{:S(2)}, u32[]{:S(2)}) %collective-permute-start.6) | collective-permute-done | bytes 131104 | tf_op jit(solution)/shard_map/ppermute | solution.py:20
  17.1 1.5 %collective-permute-start.8 = (bf16[256,256]{1,0:T(8,128)(2,1)S(1)}, bf16[256,256]{1,0:T(8,128)(2,1)S(1)}, u32[]{:S(2)}, u32[]{:S(2)}) collective-permute-start(bf16[256,256]{1,0:T(8,128)(2,1)S(1)} %collective-permute-done.6.refs_9_), channel_id=1, source_target_pairs={{0,1},{1,0},{2,3},{3,2},{4,5},{5,4},{6,7},{7,6},{8,9},{9,8},{10,11... | collective-permute-start | bytes 393224 | tf_op jit(solution)/shard_map/ppermute | solution.py:20
  18.6 0.0 collective-permute-done.2.refs_5_
  18.6 0.0 collective-permute-start.7
  18.6 0.0 collective-permute-done.refs_3_
  18.6 0.6 collective-permute-start.4
  19.2 0.0 collective-permute-done.12.refs_15_
  19.2 0.2 collective-permute-start.3
  19.4 0.0 collective-permute-done.11.refs_14_
  19.4 0.3 collective-permute-start.1
  19.7 2.7 %collective-permute-done.8.refs_11_ = bf16[256,256]{1,0:T(8,128)(2,1)S(1)} collective-permute-done((bf16[256,256]{1,0:T(8,128)(2,1)S(1)}, bf16[256,256]{1,0:T(8,128)(2,1)S(1)}, u32[]{:S(2)}, u32[]{:S(2)}) %collective-permute-start.8) | collective-permute-done | bytes 131104 | tf_op jit(solution)/shard_map/ppermute | solution.py:20
  22.5 0.0 collective-permute-start.13
  22.5 0.0 collective-permute-done.7.refs_10_
  22.5 0.5 collective-permute-start.9
  23.0 1.9 %collective-permute-done.4.refs_7_ = bf16[256,256]{1,0:T(8,128)(2,1)S(1)} collective-permute-done((bf16[256,256]{1,0:T(8,128)(2,1)S(1)}, bf16[256,256]{1,0:T(8,128)(2,1)S(1)}, u32[]{:S(2)}, u32[]{:S(2)}) %collective-permute-start.4) | collective-permute-done | bytes 131104 | tf_op jit(solution)/shard_map/ppermute | solution.py:20
  24.9 0.0 collective-permute-start.5
  24.9 0.0 collective-permute-done.3.refs_6_
  24.9 0.0 collective-permute-done.1.refs_4_
  24.9 0.0 collective-permute-done.13.refs_16_
  24.9 0.0 collective-permute-done.9.refs_12_
  24.9 1.3 %collective-permute-done.5.refs_8_ = bf16[256,256]{1,0:T(8,128)(2,1)S(1)} collective-permute-done((bf16[256,256]{1,0:T(8,128)(2,1)S(1)}, bf16[256,256]{1,0:T(8,128)(2,1)S(1)}, u32[]{:S(2)}, u32[]{:S(2)}) %collective-permute-start.5) | collective-permute-done | bytes 131104 | tf_op jit(solution)/shard_map/ppermute | solution.py:20
  26.2 0.0 copy-start
  26.2 1.6 %copy-done = bf16[1,256,4096]{2,1,0:T(8,128)(2,1)S(1)} copy-done((bf16[1,256,4096]{2,1,0:T(8,128)(2,1)S(1)}, bf16[1,256,4096]{2,1,0:T(8,128)(2,1)}, u32[]{:S(2)}) %copy-start) | copy-done | bytes 2097176
  27.8 0.0 copy-start.1
  27.8 0.9 %copy-done.1 = bf16[512,256]{1,0:T(8,128)(2,1)S(1)} copy-done((bf16[512,256]{1,0:T(8,128)(2,1)S(1)}, bf16[512,256]{1,0:T(8,128)(2,1)}, u32[]{:S(2)}) %copy-start.1) | copy-done | bytes 262168
  28.8 0.0 copy-start.2
  28.8 0.9 %copy-done.2 = bf16[1,256,256]{2,1,0:T(8,128)(2,1)S(1)} copy-done((bf16[1,256,256]{2,1,0:T(8,128)(2,1)S(1)}, bf16[1,256,256]{2,1,0:T(8,128)(2,1)}, u32[]{:S(2)}) %copy-start.2) | copy-done | bytes 131096
  29.7 1.1 %shard_map.37 = (bf16[256,256]{1,0:T(8,128)(2,1)S(1)}, bf16[256,512]{1,0:T(8,128)(2,1)S(1)}) custom-call(bf16[256,4096]{1,0:T(8,128)(2,1)S(1)} %bitcast.3, bf16[256,256]{1,0:T(8,128)(2,1)S(1)} %bitcast.5, bf16[512,256]{1,0:T(8,128)(2,1)S(1)} %copy-done.1, bf16[256,256]{1,0:T(8,128)(2,1)S(1)} %collective-permute-done.refs_3_, ...), custom_call_target="tpu_custom_call" | custom-call | flops 603979776 | bytes 4718592 | tf_op jit(solution)/shard_map/pallas_call | solution.py:30
  30.8 1.6 %collective-permute-start.14 = (bf16[256,512]{1,0:T(8,128)(2,1)S(1)}, bf16[256,512]{1,0:T(8,128)(2,1)S(1)}, u32[]{:S(2)}, u32[]{:S(2)}) collective-permute-start(bf16[256,512]{1,0:T(8,128)(2,1)S(1)} %get-tuple-element.21), channel_id=1, source_target_pairs={{0,1},{1,0},{2,3},{3,2},{4,5},{5,4},{6,7},{7,6},{8,9},{9,8},{10,11... | collective-permute-start | bytes 786440 | tf_op jit(solution)/shard_map/ppermute | solution.py:20
  32.4 0.6 shard_map.38
  33.0 0.6 collective-permute-start.16
  33.6 1.5 %collective-permute-start.18 = (bf16[256,512]{1,0:T(8,128)(2,1)S(1)}, bf16[256,512]{1,0:T(8,128)(2,1)S(1)}, u32[]{:S(2)}, u32[]{:S(2)}) collective-permute-start(bf16[256,512]{1,0:T(8,128)(2,1)S(1)} %get-tuple-element.25), channel_id=1, source_target_pairs={{0,1},{1,0},{2,3},{3,2},{4,5},{5,4},{6,7},{7,6},{8,9},{9,8},{10,11... | collective-permute-start | bytes 786440 | tf_op jit(solution)/shard_map/ppermute | solution.py:20
  35.1 0.5 collective-permute-start.20
  35.6 4.4 %collective-permute-done.14.other = bf16[256,512]{1,0:T(8,128)(2,1)S(1)} collective-permute-done((bf16[256,512]{1,0:T(8,128)(2,1)S(1)}, bf16[256,512]{1,0:T(8,128)(2,1)S(1)}, u32[]{:S(2)}, u32[]{:S(2)}) %collective-permute-start.14) | collective-permute-done | bytes 262176 | tf_op jit(solution)/shard_map/ppermute | solution.py:20
  40.1 2.5 %collective-permute-start.15 = (bf16[256,512]{1,0:T(8,128)(2,1)S(1)}, bf16[256,512]{1,0:T(8,128)(2,1)S(1)}, u32[]{:S(2)}, u32[]{:S(2)}) collective-permute-start(bf16[256,512]{1,0:T(8,128)(2,1)S(1)} %shard_map.39), channel_id=1, source_target_pairs={{0,6},{1,7},{2,4},{3,5},{4,2},{5,3},{6,0},{7,1},{8,14},{9,15},{10,... | collective-permute-start | bytes 786440 | tf_op jit(solution)/shard_map/ppermute | solution.py:20
  42.6 3.0 %collective-permute-done.16.other = bf16[256,512]{1,0:T(8,128)(2,1)S(1)} collective-permute-done((bf16[256,512]{1,0:T(8,128)(2,1)S(1)}, bf16[256,512]{1,0:T(8,128)(2,1)S(1)}, u32[]{:S(2)}, u32[]{:S(2)}) %collective-permute-start.16) | collective-permute-done | bytes 262176 | tf_op jit(solution)/shard_map/ppermute | solution.py:20
  45.7 2.8 %collective-permute-start.17 = (bf16[256,512]{1,0:T(8,128)(2,1)S(1)}, bf16[256,512]{1,0:T(8,128)(2,1)S(1)}, u32[]{:S(2)}, u32[]{:S(2)}) collective-permute-start(bf16[256,512]{1,0:T(8,128)(2,1)S(1)} %shard_map.40), channel_id=1, source_target_pairs={{0,4},{1,5},{2,6},{3,7},{4,0},{5,1},{6,2},{7,3},{8,12},{9,13},{10,... | collective-permute-start | bytes 786440 | tf_op jit(solution)/shard_map/ppermute | solution.py:20
  48.5 2.8 %collective-permute-done.18.other = bf16[256,512]{1,0:T(8,128)(2,1)S(1)} collective-permute-done((bf16[256,512]{1,0:T(8,128)(2,1)S(1)}, bf16[256,512]{1,0:T(8,128)(2,1)S(1)}, u32[]{:S(2)}, u32[]{:S(2)}) %collective-permute-start.18) | collective-permute-done | bytes 262176 | tf_op jit(solution)/shard_map/ppermute | solution.py:20
  51.3 1.6 %collective-permute-start.19 = (bf16[256,512]{1,0:T(8,128)(2,1)S(1)}, bf16[256,512]{1,0:T(8,128)(2,1)S(1)}, u32[]{:S(2)}, u32[]{:S(2)}) collective-permute-start(bf16[256,512]{1,0:T(8,128)(2,1)S(1)} %shard_map.41), channel_id=1, source_target_pairs={{0,2},{1,3},{2,0},{3,1},{4,6},{5,7},{6,4},{7,5},{8,10},{9,11},{10,... | collective-permute-start | bytes 786440 | tf_op jit(solution)/shard_map/ppermute | solution.py:20
  52.9 3.2 %collective-permute-done.20.refs_3_ = bf16[256,512]{1,0:T(8,128)(2,1)S(1)} collective-permute-done((bf16[256,512]{1,0:T(8,128)(2,1)S(1)}, bf16[256,512]{1,0:T(8,128)(2,1)S(1)}, u32[]{:S(2)}, u32[]{:S(2)}) %collective-permute-start.20) | collective-permute-done | bytes 262176 | tf_op jit(solution)/shard_map/ppermute | solution.py:20
  56.1 0.0 collective-permute-done.15.refs_0_
  56.1 8.6 %collective-permute-done.17.refs_1_ = bf16[256,512]{1,0:T(8,128)(2,1)S(1)} collective-permute-done((bf16[256,512]{1,0:T(8,128)(2,1)S(1)}, bf16[256,512]{1,0:T(8,128)(2,1)S(1)}, u32[]{:S(2)}, u32[]{:S(2)}) %collective-permute-start.17) | collective-permute-done | bytes 262176 | tf_op jit(solution)/shard_map/ppermute | solution.py:20
  64.7 0.0 collective-permute-done.19.refs_2_
  64.7 0.2 shard_map.42
  64.9 0.1 collective-permute-start.21
  64.9 1.6 %collective-permute-start.22 = (bf16[64,512]{1,0:T(8,128)(2,1)S(1)}, bf16[64,512]{1,0:T(8,128)(2,1)S(1)}, u32[]{:S(2)}, u32[]{:S(2)}) collective-permute-start(bf16[64,512]{1,0:T(8,128)(2,1)S(1)} %get-tuple-element.29), channel_id=1, source_target_pairs={{0,16},{8,24},{16,0},{24,8},{1,17},{9,25},{17,1},{25,9},{2,18},{10... | collective-permute-start | bytes 196616 | tf_op jit(solution)/shard_map/ppermute | solution.py:20
  66.5 0.3 collective-permute-start.23
  66.8 0.0 collective-permute-done.21.refs_0_
  66.8 2.6 %collective-permute-done.22.refs_1_ = bf16[64,512]{1,0:T(8,128)(2,1)S(1)} collective-permute-done((bf16[64,512]{1,0:T(8,128)(2,1)S(1)}, bf16[64,512]{1,0:T(8,128)(2,1)S(1)}, u32[]{:S(2)}, u32[]{:S(2)}) %collective-permute-start.22) | collective-permute-done | bytes 65568 | tf_op jit(solution)/shard_map/ppermute | solution.py:20
  69.5 1.1 %collective-permute-done.23.refs_2_ = bf16[64,512]{1,0:T(8,128)(2,1)S(1)} collective-permute-done((bf16[64,512]{1,0:T(8,128)(2,1)S(1)}, bf16[64,512]{1,0:T(8,128)(2,1)S(1)}, u32[]{:S(2)}, u32[]{:S(2)}) %collective-permute-start.23) | collective-permute-done | bytes 65568 | tf_op jit(solution)/shard_map/ppermute | solution.py:20
  70.6 0.7 shard_map.43
  (3 shorter events, 0.1 us)
Async XLA Ops:
  0.9 9.5 %collective-permute-start.10 = (bf16[256,256]{1,0:T(8,128)(2,1)S(1)}, bf16[256,256]{1,0:T(8,128)(2,1)S(1)}, u32[]{:S(2)}, u32[]{:S(2)}) collective-permute-start(bf16[256,256]{1,0:T(8,128)(2,1)S(1)} %constant_dynamic-slice_fusion), channel_id=1, source_target_pairs={{0,6},{1,7},{2,4},{3,5},{4,2},{5,3},{6,0},{7,1},{8,14},{9,15},{10,... | collective-permute-start | bytes 393224 | tf_op jit(solution)/shard_map/ppermute | solution.py:20
  6.0 11.1 %collective-permute-start.6 = (bf16[256,256]{1,0:T(8,128)(2,1)S(1)}, bf16[256,256]{1,0:T(8,128)(2,1)S(1)}, u32[]{:S(2)}, u32[]{:S(2)}) collective-permute-start(bf16[256,256]{1,0:T(8,128)(2,1)S(1)} %constant_dynamic-slice_fusion), channel_id=1, source_target_pairs={{0,4},{1,5},{2,6},{3,7},{4,0},{5,1},{6,2},{7,3},{8,12},{9,13},{10,... | collective-permute-start | bytes 393224 | tf_op jit(solution)/shard_map/ppermute | solution.py:20
  6.0 12.6 %collective-permute-start.2 = (bf16[256,256]{1,0:T(8,128)(2,1)S(1)}, bf16[256,256]{1,0:T(8,128)(2,1)S(1)}, u32[]{:S(2)}, u32[]{:S(2)}) collective-permute-start(bf16[256,256]{1,0:T(8,128)(2,1)S(1)} %constant_dynamic-slice_fusion), channel_id=1, source_target_pairs={{0,2},{1,3},{2,0},{3,1},{4,6},{5,7},{6,4},{7,5},{8,10},{9,11},{10,... | collective-permute-start | bytes 393224 | tf_op jit(solution)/shard_map/ppermute | solution.py:20
  6.7 12.0 %collective-permute-start = (bf16[256,256]{1,0:T(8,128)(2,1)S(1)}, bf16[256,256]{1,0:T(8,128)(2,1)S(1)}, u32[]{:S(2)}, u32[]{:S(2)}) collective-permute-start(bf16[256,256]{1,0:T(8,128)(2,1)S(1)} %constant_dynamic-slice_fusion), channel_id=1, source_target_pairs={{0,1},{1,0},{2,3},{3,2},{4,5},{5,4},{6,7},{7,6},{8,9},{9,8},{10,11... | collective-permute-start | bytes 393224 | tf_op jit(solution)/shard_map/ppermute | solution.py:20
  10.5 8.8 %collective-permute-start.12 = (bf16[256,256]{1,0:T(8,128)(2,1)S(1)}, bf16[256,256]{1,0:T(8,128)(2,1)S(1)}, u32[]{:S(2)}, u32[]{:S(2)}) collective-permute-start(bf16[256,256]{1,0:T(8,128)(2,1)S(1)} %collective-permute-done.10.refs_13_), channel_id=1, source_target_pairs={{0,1},{1,0},{2,3},{3,2},{4,5},{5,4},{6,7},{7,6},{8,9},{9,8},{10,11... | collective-permute-start | bytes 393224 | tf_op jit(solution)/shard_map/ppermute | solution.py:20
  12.2 7.2 %collective-permute-start.11 = (bf16[256,256]{1,0:T(8,128)(2,1)S(1)}, bf16[256,256]{1,0:T(8,128)(2,1)S(1)}, u32[]{:S(2)}, u32[]{:S(2)}) collective-permute-start(bf16[256,256]{1,0:T(8,128)(2,1)S(1)} %collective-permute-done.10.refs_13_), channel_id=1, source_target_pairs={{0,8},{8,0},{16,24},{24,16},{1,9},{9,1},{17,25},{25,17},{2,10},{10... | collective-permute-start | bytes 393224 | tf_op jit(solution)/shard_map/ppermute | solution.py:20
  17.1 5.4 %collective-permute-start.8 = (bf16[256,256]{1,0:T(8,128)(2,1)S(1)}, bf16[256,256]{1,0:T(8,128)(2,1)S(1)}, u32[]{:S(2)}, u32[]{:S(2)}) collective-permute-start(bf16[256,256]{1,0:T(8,128)(2,1)S(1)} %collective-permute-done.6.refs_9_), channel_id=1, source_target_pairs={{0,1},{1,0},{2,3},{3,2},{4,5},{5,4},{6,7},{7,6},{8,9},{9,8},{10,11... | collective-permute-start | bytes 393224 | tf_op jit(solution)/shard_map/ppermute | solution.py:20
  18.6 3.8 %collective-permute-start.7 = (bf16[256,256]{1,0:T(8,128)(2,1)S(1)}, bf16[256,256]{1,0:T(8,128)(2,1)S(1)}, u32[]{:S(2)}, u32[]{:S(2)}) collective-permute-start(bf16[256,256]{1,0:T(8,128)(2,1)S(1)} %collective-permute-done.6.refs_9_), channel_id=1, source_target_pairs={{0,8},{8,0},{16,24},{24,16},{1,9},{9,1},{17,25},{25,17},{2,10},{10... | collective-permute-start | bytes 393224 | tf_op jit(solution)/shard_map/ppermute | solution.py:20
  18.6 6.2 %collective-permute-start.4 = (bf16[256,256]{1,0:T(8,128)(2,1)S(1)}, bf16[256,256]{1,0:T(8,128)(2,1)S(1)}, u32[]{:S(2)}, u32[]{:S(2)}) collective-permute-start(bf16[256,256]{1,0:T(8,128)(2,1)S(1)} %collective-permute-done.2.refs_5_), channel_id=1, source_target_pairs={{0,1},{1,0},{2,3},{3,2},{4,5},{5,4},{6,7},{7,6},{8,9},{9,8},{10,11... | collective-permute-start | bytes 393224 | tf_op jit(solution)/shard_map/ppermute | solution.py:20
  19.2 5.7 %collective-permute-start.3 = (bf16[256,256]{1,0:T(8,128)(2,1)S(1)}, bf16[256,256]{1,0:T(8,128)(2,1)S(1)}, u32[]{:S(2)}, u32[]{:S(2)}) collective-permute-start(bf16[256,256]{1,0:T(8,128)(2,1)S(1)} %collective-permute-done.2.refs_5_), channel_id=1, source_target_pairs={{0,8},{8,0},{16,24},{24,16},{1,9},{9,1},{17,25},{25,17},{2,10},{10... | collective-permute-start | bytes 393224 | tf_op jit(solution)/shard_map/ppermute | solution.py:20
  19.4 5.5 %collective-permute-start.1 = (bf16[256,256]{1,0:T(8,128)(2,1)S(1)}, bf16[256,256]{1,0:T(8,128)(2,1)S(1)}, u32[]{:S(2)}, u32[]{:S(2)}) collective-permute-start(bf16[256,256]{1,0:T(8,128)(2,1)S(1)} %collective-permute-done.refs_3_), channel_id=1, source_target_pairs={{0,8},{8,0},{16,24},{24,16},{1,9},{9,1},{17,25},{25,17},{2,10},{10... | collective-permute-start | bytes 393224 | tf_op jit(solution)/shard_map/ppermute | solution.py:20
  22.5 2.4 %collective-permute-start.13 = (bf16[256,256]{1,0:T(8,128)(2,1)S(1)}, bf16[256,256]{1,0:T(8,128)(2,1)S(1)}, u32[]{:S(2)}, u32[]{:S(2)}) collective-permute-start(bf16[256,256]{1,0:T(8,128)(2,1)S(1)} %collective-permute-done.12.refs_15_), channel_id=1, source_target_pairs={{0,8},{8,0},{16,24},{24,16},{1,9},{9,1},{17,25},{25,17},{2,10},{10... | collective-permute-start | bytes 393224 | tf_op jit(solution)/shard_map/ppermute | solution.py:20
  22.5 2.4 %collective-permute-start.9 = (bf16[256,256]{1,0:T(8,128)(2,1)S(1)}, bf16[256,256]{1,0:T(8,128)(2,1)S(1)}, u32[]{:S(2)}, u32[]{:S(2)}) collective-permute-start(bf16[256,256]{1,0:T(8,128)(2,1)S(1)} %collective-permute-done.8.refs_11_), channel_id=1, source_target_pairs={{0,8},{8,0},{16,24},{24,16},{1,9},{9,1},{17,25},{25,17},{2,10},{10... | collective-permute-start | bytes 393224 | tf_op jit(solution)/shard_map/ppermute | solution.py:20
  24.9 1.3 %collective-permute-start.5 = (bf16[256,256]{1,0:T(8,128)(2,1)S(1)}, bf16[256,256]{1,0:T(8,128)(2,1)S(1)}, u32[]{:S(2)}, u32[]{:S(2)}) collective-permute-start(bf16[256,256]{1,0:T(8,128)(2,1)S(1)} %collective-permute-done.4.refs_7_), channel_id=1, source_target_pairs={{0,8},{8,0},{16,24},{24,16},{1,9},{9,1},{17,25},{25,17},{2,10},{10... | collective-permute-start | bytes 393224 | tf_op jit(solution)/shard_map/ppermute | solution.py:20
  26.2 1.6 %copy-start = (bf16[1,256,4096]{2,1,0:T(8,128)(2,1)S(1)}, bf16[1,256,4096]{2,1,0:T(8,128)(2,1)}, u32[]{:S(2)}) copy-start(bf16[1,256,4096]{2,1,0:T(8,128)(2,1)} %param.3) | copy-start | bytes 6291460
  27.8 0.9 %copy-start.1 = (bf16[512,256]{1,0:T(8,128)(2,1)S(1)}, bf16[512,256]{1,0:T(8,128)(2,1)}, u32[]{:S(2)}) copy-start(bf16[512,256]{1,0:T(8,128)(2,1)} %refs_2_.1) | copy-start | bytes 786436
  28.8 0.9 %copy-start.2 = (bf16[1,256,256]{2,1,0:T(8,128)(2,1)S(1)}, bf16[1,256,256]{2,1,0:T(8,128)(2,1)}, u32[]{:S(2)}) copy-start(bf16[1,256,256]{2,1,0:T(8,128)(2,1)} %param.5) | copy-start | bytes 393220
  30.8 9.2 %collective-permute-start.14 = (bf16[256,512]{1,0:T(8,128)(2,1)S(1)}, bf16[256,512]{1,0:T(8,128)(2,1)S(1)}, u32[]{:S(2)}, u32[]{:S(2)}) collective-permute-start(bf16[256,512]{1,0:T(8,128)(2,1)S(1)} %get-tuple-element.21), channel_id=1, source_target_pairs={{0,1},{1,0},{2,3},{3,2},{4,5},{5,4},{6,7},{7,6},{8,9},{9,8},{10,11... | collective-permute-start | bytes 786440 | tf_op jit(solution)/shard_map/ppermute | solution.py:20
  33.0 12.6 %collective-permute-start.16 = (bf16[256,512]{1,0:T(8,128)(2,1)S(1)}, bf16[256,512]{1,0:T(8,128)(2,1)S(1)}, u32[]{:S(2)}, u32[]{:S(2)}) collective-permute-start(bf16[256,512]{1,0:T(8,128)(2,1)S(1)} %get-tuple-element.23), channel_id=1, source_target_pairs={{0,1},{1,0},{2,3},{3,2},{4,5},{5,4},{6,7},{7,6},{8,9},{9,8},{10,11... | collective-permute-start | bytes 786440 | tf_op jit(solution)/shard_map/ppermute | solution.py:20
  33.6 17.6 %collective-permute-start.18 = (bf16[256,512]{1,0:T(8,128)(2,1)S(1)}, bf16[256,512]{1,0:T(8,128)(2,1)S(1)}, u32[]{:S(2)}, u32[]{:S(2)}) collective-permute-start(bf16[256,512]{1,0:T(8,128)(2,1)S(1)} %get-tuple-element.25), channel_id=1, source_target_pairs={{0,1},{1,0},{2,3},{3,2},{4,5},{5,4},{6,7},{7,6},{8,9},{9,8},{10,11... | collective-permute-start | bytes 786440 | tf_op jit(solution)/shard_map/ppermute | solution.py:20
  35.1 21.0 %collective-permute-start.20 = (bf16[256,512]{1,0:T(8,128)(2,1)S(1)}, bf16[256,512]{1,0:T(8,128)(2,1)S(1)}, u32[]{:S(2)}, u32[]{:S(2)}) collective-permute-start(bf16[256,512]{1,0:T(8,128)(2,1)S(1)} %get-tuple-element.26), channel_id=1, source_target_pairs={{0,1},{1,0},{2,3},{3,2},{4,5},{5,4},{6,7},{7,6},{8,9},{9,8},{10,11... | collective-permute-start | bytes 786440 | tf_op jit(solution)/shard_map/ppermute | solution.py:20
  40.1 16.0 %collective-permute-start.15 = (bf16[256,512]{1,0:T(8,128)(2,1)S(1)}, bf16[256,512]{1,0:T(8,128)(2,1)S(1)}, u32[]{:S(2)}, u32[]{:S(2)}) collective-permute-start(bf16[256,512]{1,0:T(8,128)(2,1)S(1)} %shard_map.39), channel_id=1, source_target_pairs={{0,6},{1,7},{2,4},{3,5},{4,2},{5,3},{6,0},{7,1},{8,14},{9,15},{10,... | collective-permute-start | bytes 786440 | tf_op jit(solution)/shard_map/ppermute | solution.py:20
  45.7 19.0 %collective-permute-start.17 = (bf16[256,512]{1,0:T(8,128)(2,1)S(1)}, bf16[256,512]{1,0:T(8,128)(2,1)S(1)}, u32[]{:S(2)}, u32[]{:S(2)}) collective-permute-start(bf16[256,512]{1,0:T(8,128)(2,1)S(1)} %shard_map.40), channel_id=1, source_target_pairs={{0,4},{1,5},{2,6},{3,7},{4,0},{5,1},{6,2},{7,3},{8,12},{9,13},{10,... | collective-permute-start | bytes 786440 | tf_op jit(solution)/shard_map/ppermute | solution.py:20
  51.3 13.4 %collective-permute-start.19 = (bf16[256,512]{1,0:T(8,128)(2,1)S(1)}, bf16[256,512]{1,0:T(8,128)(2,1)S(1)}, u32[]{:S(2)}, u32[]{:S(2)}) collective-permute-start(bf16[256,512]{1,0:T(8,128)(2,1)S(1)} %shard_map.41), channel_id=1, source_target_pairs={{0,2},{1,3},{2,0},{3,1},{4,6},{5,7},{6,4},{7,5},{8,10},{9,11},{10,... | collective-permute-start | bytes 786440 | tf_op jit(solution)/shard_map/ppermute | solution.py:20
  64.9 1.9 %collective-permute-start.21 = (bf16[64,512]{1,0:T(8,128)(2,1)S(1)}, bf16[64,512]{1,0:T(8,128)(2,1)S(1)}, u32[]{:S(2)}, u32[]{:S(2)}) collective-permute-start(bf16[64,512]{1,0:T(8,128)(2,1)S(1)} %get-tuple-element.28), channel_id=1, source_target_pairs={{0,8},{8,0},{16,24},{24,16},{1,9},{9,1},{17,25},{25,17},{2,10},{10... | collective-permute-start | bytes 196616 | tf_op jit(solution)/shard_map/ppermute | solution.py:20
  64.9 4.5 %collective-permute-start.22 = (bf16[64,512]{1,0:T(8,128)(2,1)S(1)}, bf16[64,512]{1,0:T(8,128)(2,1)S(1)}, u32[]{:S(2)}, u32[]{:S(2)}) collective-permute-start(bf16[64,512]{1,0:T(8,128)(2,1)S(1)} %get-tuple-element.29), channel_id=1, source_target_pairs={{0,16},{8,24},{16,0},{24,8},{1,17},{9,25},{17,1},{25,9},{2,18},{10... | collective-permute-start | bytes 196616 | tf_op jit(solution)/shard_map/ppermute | solution.py:20
  66.5 4.0 %collective-permute-start.23 = (bf16[64,512]{1,0:T(8,128)(2,1)S(1)}, bf16[64,512]{1,0:T(8,128)(2,1)S(1)}, u32[]{:S(2)}, u32[]{:S(2)}) collective-permute-start(bf16[64,512]{1,0:T(8,128)(2,1)S(1)} %get-tuple-element.30), channel_id=1, source_target_pairs={{0,24},{8,16},{16,8},{24,0},{1,25},{9,17},{17,9},{25,1},{2,26},{10... | collective-permute-start | bytes 196616 | tf_op jit(solution)/shard_map/ppermute | solution.py:20

commit v2 on v1

v2 whole, which is shorter than its diff:
```python
import functools

import jax
import jax.numpy as jnp
from jax import lax
from jax.experimental import pallas as pl
from jax.experimental.pallas import tpu as pltpu
from jax.sharding import PartitionSpec as P

COST = 20_000_000_000
F32 = jnp.float32
BF16 = jnp.bfloat16


def local_terms(cotangent, pre):
    sigma = jax.nn.sigmoid(pre)
    return (cotangent.astype(F32) * sigma * (1.0 + pre * (1.0 - sigma))).astype(BF16)


def hop(x, axis, k):
    return lax.ppermute(x, axis, [(i, i ^ k) for i in range(lax.axis_size(axis))])


def move(x, axis, hops):
    return lax.ppermute(x, axis, [(i, i ^ k) for i, k in hops.items()])


def columns(block, size):
    return pl.ds(pl.multiple_of(block * size, 128), size)


def call(kernel, outs, *operands, cost=COST):
    vmem = pl.BlockSpec(memory_space=pltpu.VMEM)
    moved = sum(x.size * x.dtype.itemsize for x in (*operands, *outs))
    return pl.pallas_call(
        kernel,
        out_shape=tuple(outs),
        in_specs=[vmem] * len(operands),
        out_specs=(vmem,) * len(outs),
        compiler_params=pltpu.CompilerParams(vmem_limit_bytes=48 * 2**20),
        cost_estimate=pl.CostEstimate(flops=cost, bytes_accessed=moved, transcendentals=0),
    )(*operands)


def encode(x):
    return (x * jnp.abs(x)).astype(BF16)


def decode(y):
    y = y.astype(F32)
    root = jnp.sqrt(jnp.abs(y))
    return jnp.where(y < 0, -root, root)


def put(out, value):
    out[...] = encode(value) if out.dtype == BF16 else value


def add_pieces(pre, a, hops, pieces):
    half = pieces[0].shape[0]
    me = lax.axis_index("seq")
    core = lax.rem(lax.axis_index("example"), 2)
    for i, k in enumerate(hops):
        for flip in range(2):
            block = 2 * (me ^ k) + (core ^ flip)
            pre += jnp.dot(
                a[:, columns(block, half)], pieces[2 * i + flip][...], preferred_element_type=F32
            )
    return pre


def chunk(hops, a, local_t):
    rows = a.shape[1] // lax.axis_size("seq")
    block = lax.axis_index("seq") ^ hops
    return jnp.dot(local_t, a[:, columns(block, rows)], preferred_element_type=F32)


def pass_kernel(piece, out):
    out[...] = piece[...]


def local_kernel(hops, send, a, seeds, own, *refs):
    count = len(refs) - len(send) - 1
    pieces, outs, local_ref = refs[:count], refs[count:-1], refs[-1]
    block = a[:, columns(lax.axis_index("seq"), own.shape[0])]
    pre = jnp.dot(block, own[...], preferred_element_type=F32)
    local_t = local_terms(seeds[...], add_pieces(pre, a, hops, pieces)).T
    local_ref[...] = local_t
    for k, out in zip(send, outs):
        put(out, chunk(k, a, local_t))


def sum_kernel(near, send, a, local_t, *refs):
    outs = refs[len(refs) - len(send) - 1 :]
    total = chunk(near, a, local_t[...])
    for other in refs[: len(refs) - len(outs)]:
        total += decode(other[...])
    put(outs[0], total)
    for k, out in zip(send, outs[1:]):
        put(out, chunk(k, a, local_t[...]))


def add_kernel(mine, *refs):
    total = mine[...]
    for other in refs[:-1]:
        total += decode(other[...])
    put(refs[-1], total)


def square_kernel(grad, last, *outs):
    me = lax.axis_index("example")
    size = outs[0].shape[0]
    for k, out in enumerate(outs):
        part = pl.ds(pl.multiple_of((me ^ k) * size, size), size)
        total = grad[part, :] + decode(last[part, :])
        out[...] = (total * total).astype(out.dtype)


def mean_kernel(scale, own, *refs):
    total = own[...]
    for other in refs[:-1]:
        total += other[...].astype(F32)
    refs[-1][...] = total * scale


def direct(activations, gate_weight, seeds):
    inputs, cotangent = activations[0], seeds[0]
    tokens, width = inputs.shape
    rows, hidden = gate_weight.shape
    count, examples = lax.axis_size("seq"), lax.axis_size("example")

    core = lax.rem(lax.axis_index("example"), 2)
    half = lax.dynamic_slice_in_dim(gate_weight, core * (rows // 2), rows // 2)
    held = {6: hop(half, "seq", 6), 2: hop(half, "seq", 2), 1: hop(half, "seq", 1)}
    held[4] = hop(lax.optimization_barrier((half, held[6]))[0], "seq", 4)
    (copied,) = call(pass_kernel, [jax.ShapeDtypeStruct(half.shape, BF16)], held[2])
    held[3] = hop(copied, "seq", 1)
    held[7] = hop(held[6], "seq", 1)
    held[5] = hop(held[4], "seq", 1)

    block = lambda dtype: jax.ShapeDtypeStruct((hidden, rows), dtype)
    late = (1, 2, 3, 6, 7, 4, 5)
    pieces = []
    for k in late:
        pieces += [held[k], hop(held[k], "example", 1)]
    six, four, local_t = call(
        functools.partial(local_kernel, late, (7, 5)),
        [block(BF16)] * 2 + [jax.ShapeDtypeStruct((hidden, tokens), BF16)],
        inputs, cotangent, gate_weight, *pieces,
    )
    six, four = hop(six, "seq", 1), hop(four, "seq", 1)
    far, two = call(functools.partial(sum_kernel, 6, (3,)), [block(BF16)] * 2, inputs, local_t, six)
    far, passed = (
        move(far, "seq", {i: 6 for i in (2, 3, 4, 5)}),
        move(far, "seq", {i: 2 for i in (0, 1, 6, 7)}),
    )
    two = hop(two, "seq", 1)
    four, none = call(
        functools.partial(sum_kernel, 4, (1,)), [block(F32), block(BF16)], inputs, local_t, four
    )
    none = hop(none, "seq", 1)
    (four,) = call(add_kernel, [block(BF16)], four, passed)
    four, far = lax.optimization_barrier((four, far))
    four = hop(four, "seq", 4)
    two = lax.optimization_barrier((two, far))[0]
    (two,) = call(functools.partial(sum_kernel, 2, ()), [block(BF16)], inputs, local_t, two, cost=1000)
    two = hop(two, "seq", 2)
    (grad,) = call(functools.partial(sum_kernel, 0, ()), [block(F32)], inputs, local_t, none, far, four)

    size = hidden // examples
    part = lambda dtype: jax.ShapeDtypeStruct((size, rows), dtype)
    own, *others = call(square_kernel, [part(F32)] + [part(BF16)] * (examples - 1), grad, two)
    others = [hop(x, "example", k + 1) for k, x in enumerate(others)]
    (total,) = call(
        functools.partial(mean_kernel, 1.0 / (tokens * count * examples)),
        (part(F32),), own, *others,
    )
    return total.T


def plain(activations, gate_weight, seeds):
    inputs, cotangent = activations[0], seeds[0]
    count, examples = lax.axis_size("seq"), lax.axis_size("example")
    weights = lax.all_gather(gate_weight, "seq", axis=0, tiled=True)
    pre = jnp.dot(inputs, weights, preferred_element_type=F32)
    local = local_terms(cotangent, pre)
    product = lax.dot_general(inputs, local, (((0,), (0,)), ((), ())), preferred_element_type=F32)
    grad = lax.psum_scatter(product, "seq", scatter_dimension=0, tiled=True)
    total = lax.psum_scatter(grad * grad, "example", scatter_dimension=1, tiled=True)
    return total * (1.0 / (inputs.shape[0] * count * examples))


def body(activations, gate_weight, seeds):
    rows, hidden = gate_weight.shape
    fits = lax.axis_size("seq") == 8 and rows % 256 == 0 and hidden % (16 * lax.axis_size("example")) == 0
    return (direct if fits else plain)(activations, gate_weight, seeds)


def solution(mesh):
    return jax.shard_map(
        body,
        mesh=mesh,
        in_specs=(P("example", "seq", None), P("seq", None), P("example", "seq", None)),
        out_specs=P("seq", "example"),
        check_vma=False,
    )
```

time: 71.5 us -> 67.1 us (0.938)
  waiting for transfers between devices: 38.8 us -> 31.5 us
  starting transfers between devices: 25.3 us -> 29.9 us
  local copies, waits for them, and re-layouts: 4.36 us -> 0.93 us
  Pallas kernels: 2.75 us -> 4.44 us
    ppermute x24 -> x23, waiting for transfers between devices: 38.8 us -> 29.9 us  [hop(): lax.ppermute(x, axis, [(i, i ^ k) for i in range(lax.axis_size(axis))])]
    ppermute x0 -> x2, starting transfers between devices: none -> 5.82 us  [move(): return lax.ppermute(x, axis, [(i, i ^ k) for i, k in hops.items()])]
    unnamed x6, local copies, waits for them, and re-layouts: 3.44 us -> 0.02 us
    pallas_call x7 -> x9, Pallas kernels: 2.75 us -> 4.44 us  [call(): pl.pallas_call(kernel, out_shape=tuple(outs), in_specs=[vmem] * len(opera...]
    ppermute x0 -> x2, waiting for transfers between devices: none -> 1.67 us  [move(): return lax.ppermute(x, axis, [(i, i ^ k) for i, k in hops.items()])]
    ppermute x24 -> x23, starting transfers between devices: 25.3 us -> 24.1 us  [hop(): lax.ppermute(x, axis, [(i, i ^ k) for i in range(lax.axis_size(axis))])]
  transfers between devices with their start and end apart: 24 -> 25, of which waited for: 12 -> 13; matrix products, arithmetic and copies ran while one was open for 0% -> 0% of each run, Pallas kernels for 1% -> 3%
where the time goes in v2:
time: 67.1 us; the launch traced here: 67 us
  waiting for transfers between devices  31.5 us (47%)
  starting transfers between devices  29.9 us (45%)
  Pallas kernels  4.44 us (7%)
  local copies, waits for them, and re-layouts  0.93 us (1%)
    ppermute x23, waiting for transfers between devices, hop(): lax.ppermute(x, axis, [(i, i ^ k) for i in range(lax.axis_size(axis))])  29.9 us
    ppermute x23, starting transfers between devices, hop(): lax.ppermute(x, axis, [(i, i ^ k) for i in range(lax.axis_size(axis))])  24.1 us
    ppermute x2, starting transfers between devices, move(): return lax.ppermute(x, axis, [(i, i ^ k) for i, k in hops.items()])  5.82 us
    pallas_call x9, Pallas kernels, call(): pl.pallas_call(kernel, out_shape=tuple(outs), in_specs=[vmem] * len(opera...  4.44 us
    ppermute x2, waiting for transfers between devices, move(): return lax.ppermute(x, axis, [(i, i ^ k) for i, k in hops.items()])  1.67 us
  transfers between devices with their start and end apart: 25, of which 13 were waited for; matrix products, arithmetic and copies ran while one was open for 0% of the time, Pallas kernels for 3%

profile of v2, /device:TPU:0, one launch (start us, length us, event | category | flops | bytes accessed | tf_op | source)
XLA Modules:
  0.0 67.0 jit_solution(7159669802777067005)
XLA Ops:
  0.0 0.9 %constant_dynamic-slice_fusion = bf16[256,256]{1,0:T(8,128)(2,1)S(1)} fusion(bf16[512,256]{1,0:T(8,128)(2,1)} %own.1, s32[]{:T(128)S(6)} %select_n.3), kind=kLoop, calls=%fused_computation | loop fusion | bytes 262148 | tf_op jit(solution)/shard_map/dynamic_slice | solution.py:133
  0.9 0.0 copy-start
  0.9 0.0 copy-start.1
  0.9 0.0 copy-start.2
  1.0 5.1 %collective-permute-start.6 = (bf16[256,256]{1,0:T(8,128)(2,1)S(1)}, bf16[256,256]{1,0:T(8,128)(2,1)S(1)}, u32[]{:S(2)}, u32[]{:S(2)}) collective-permute-start(bf16[256,256]{1,0:T(8,128)(2,1)S(1)} %constant_dynamic-slice_fusion), channel_id=1, source_target_pairs={{0,6},{1,7},{2,4},{3,5},{4,2},{5,3},{6,0},{7,1},{8,14},{9,15},{10,... | collective-permute-start | bytes 393224 | tf_op jit(solution)/shard_map/ppermute | solution.py:21
  6.1 0.0 collective-permute-start.2
  6.1 1.5 %collective-permute-start = (bf16[256,256]{1,0:T(8,128)(2,1)S(1)}, bf16[256,256]{1,0:T(8,128)(2,1)S(1)}, u32[]{:S(2)}, u32[]{:S(2)}) collective-permute-start(bf16[256,256]{1,0:T(8,128)(2,1)S(1)} %constant_dynamic-slice_fusion), channel_id=1, source_target_pairs={{0,1},{1,0},{2,3},{3,2},{4,5},{5,4},{6,7},{7,6},{8,9},{9,8},{10,11... | collective-permute-start | bytes 393224 | tf_op jit(solution)/shard_map/ppermute | solution.py:21
  7.6 2.8 %collective-permute-done.6.refs_6_ = bf16[256,256]{1,0:T(8,128)(2,1)S(1)} collective-permute-done((bf16[256,256]{1,0:T(8,128)(2,1)S(1)}, bf16[256,256]{1,0:T(8,128)(2,1)S(1)}, u32[]{:S(2)}, u32[]{:S(2)}) %collective-permute-start.6) | collective-permute-done | bytes 131104 | tf_op jit(solution)/shard_map/ppermute | solution.py:21
  10.4 2.4 %collective-permute-start.10 = (bf16[256,256]{1,0:T(8,128)(2,1)S(1)}, bf16[256,256]{1,0:T(8,128)(2,1)S(1)}, u32[]{:S(2)}, u32[]{:S(2)}) collective-permute-start(bf16[256,256]{1,0:T(8,128)(2,1)S(1)} %constant_dynamic-slice_fusion), channel_id=1, source_target_pairs={{0,4},{1,5},{2,6},{3,7},{4,0},{5,1},{6,2},{7,3},{8,12},{9,13},{10,... | collective-permute-start | bytes 393224 | tf_op jit(solution)/shard_map/ppermute | solution.py:21
  12.8 1.5 %collective-permute-start.8 = (bf16[256,256]{1,0:T(8,128)(2,1)S(1)}, bf16[256,256]{1,0:T(8,128)(2,1)S(1)}, u32[]{:S(2)}, u32[]{:S(2)}) collective-permute-start(bf16[256,256]{1,0:T(8,128)(2,1)S(1)} %collective-permute-done.6.refs_6_), channel_id=1, source_target_pairs={{0,1},{1,0},{2,3},{3,2},{4,5},{5,4},{6,7},{7,6},{8,9},{9,8},{10,11... | collective-permute-start | bytes 393224 | tf_op jit(solution)/shard_map/ppermute | solution.py:21
  14.4 0.0 collective-permute-start.7
  14.4 0.0 collective-permute-done.2.piece.refs_2_
  14.4 1.1 %collective-permute-start.4 = (bf16[256,256]{1,0:T(8,128)(2,1)S(1)}, bf16[256,256]{1,0:T(8,128)(2,1)S(1)}, u32[]{:S(2)}, u32[]{:S(2)}) collective-permute-start(bf16[256,256]{1,0:T(8,128)(2,1)S(1)} %shard_map.37), channel_id=1, source_target_pairs={{0,1},{1,0},{2,3},{3,2},{4,5},{5,4},{6,7},{7,6},{8,9},{9,8},{10,11... | collective-permute-start | bytes 393224 | tf_op jit(solution)/shard_map/ppermute | solution.py:21
  15.5 0.0 collective-permute-done.refs_0_
  15.5 0.0 collective-permute-start.3
  15.5 2.9 %collective-permute-done.10.refs_10_ = bf16[256,256]{1,0:T(8,128)(2,1)S(1)} collective-permute-done((bf16[256,256]{1,0:T(8,128)(2,1)S(1)}, bf16[256,256]{1,0:T(8,128)(2,1)S(1)}, u32[]{:S(2)}, u32[]{:S(2)}) %collective-permute-start.10) | collective-permute-done | bytes 131104 | tf_op jit(solution)/shard_map/ppermute | solution.py:21
  18.4 1.4 %collective-permute-start.12 = (bf16[256,256]{1,0:T(8,128)(2,1)S(1)}, bf16[256,256]{1,0:T(8,128)(2,1)S(1)}, u32[]{:S(2)}, u32[]{:S(2)}) collective-permute-start(bf16[256,256]{1,0:T(8,128)(2,1)S(1)} %collective-permute-done.10.refs_10_), channel_id=1, source_target_pairs={{0,1},{1,0},{2,3},{3,2},{4,5},{5,4},{6,7},{7,6},{8,9},{9,8},{10,11... | collective-permute-start | bytes 393224 | tf_op jit(solution)/shard_map/ppermute | solution.py:21
  19.8 0.0 collective-permute-done.8.refs_8_
  19.8 0.0 collective-permute-start.1
  19.8 0.0 collective-permute-done.7.refs_7_
  19.8 0.5 collective-permute-start.11
  20.3 0.6 collective-permute-done.4.refs_4_
  20.9 0.0 collective-permute-start.9
  20.9 0.0 collective-permute-done.3.refs_3_
  20.9 0.5 collective-permute-start.5
  21.4 2.0 %collective-permute-done.12.refs_12_ = bf16[256,256]{1,0:T(8,128)(2,1)S(1)} collective-permute-done((bf16[256,256]{1,0:T(8,128)(2,1)S(1)}, bf16[256,256]{1,0:T(8,128)(2,1)S(1)}, u32[]{:S(2)}, u32[]{:S(2)}) %collective-permute-start.12) | collective-permute-done | bytes 131104 | tf_op jit(solution)/shard_map/ppermute | solution.py:21
  23.4 0.0 collective-permute-start.13
  23.4 0.0 collective-permute-done.1.refs_1_
  23.4 0.0 collective-permute-done.11.refs_11_
  23.4 0.0 collective-permute-done.9.refs_9_
  23.5 0.0 collective-permute-done.5.refs_5_
  23.5 1.3 %collective-permute-done.13.refs_13_ = bf16[256,256]{1,0:T(8,128)(2,1)S(1)} collective-permute-done((bf16[256,256]{1,0:T(8,128)(2,1)S(1)}, bf16[256,256]{1,0:T(8,128)(2,1)S(1)}, u32[]{:S(2)}, u32[]{:S(2)}) %collective-permute-start.13) | collective-permute-done | bytes 131104 | tf_op jit(solution)/shard_map/ppermute | solution.py:21
  24.8 0.0 copy-done
  24.8 0.0 copy-done.1
  24.8 1.3 %shard_map.38 = (bf16[256,512]{1,0:T(8,128)(2,1)S(1)}, bf16[256,512]{1,0:T(8,128)(2,1)S(1)}, bf16[256,256]{1,0:T(8,128)(2,1)S(1)}) custom-call(bf16[256,4096]{1,0:T(8,128)(2,1)S(1)} %bitcast.3, bf16[256,256]{1,0:T(8,128)(2,1)S(1)} %bitcast.8, bf16[512,256]{1,0:T(8,128)(2,1)S(1)} %copy-done.1, bf16[256,256]{1,0:T(8,128)(2,1)S(1)} %collective-permute-done.refs_0_, ...), custom_call_target="tpu_custom_call" | custom-call | flops 20000000000 | bytes 4980736 | tf_op jit(solution)/shard_map/pallas_call | solution.py:35
  26.1 1.6 %collective-permute-start.16 = (bf16[256,512]{1,0:T(8,128)(2,1)S(1)}, bf16[256,512]{1,0:T(8,128)(2,1)S(1)}, u32[]{:S(2)}, u32[]{:S(2)}) collective-permute-start(bf16[256,512]{1,0:T(8,128)(2,1)S(1)} %get-tuple-element.25), channel_id=1, source_target_pairs={{0,1},{1,0},{2,3},{3,2},{4,5},{5,4},{6,7},{7,6},{8,9},{9,8},{10,11... | collective-permute-start | bytes 786440 | tf_op jit(solution)/shard_map/ppermute | solution.py:21
  27.7 0.5 collective-permute-start.14
  28.2 7.1 %collective-permute-done.16.refs_0_ = bf16[256,512]{1,0:T(8,128)(2,1)S(1)} collective-permute-done((bf16[256,512]{1,0:T(8,128)(2,1)S(1)}, bf16[256,512]{1,0:T(8,128)(2,1)S(1)}, u32[]{:S(2)}, u32[]{:S(2)}) %collective-permute-start.16) | collective-permute-done | bytes 262176 | tf_op jit(solution)/shard_map/ppermute | solution.py:21
  35.3 0.4 shard_map.40
  35.8 0.7 %collective-permute-start.18 = (bf16[256,512]{1,0:T(8,128)(2,1)S(1)}, bf16[256,512]{1,0:T(8,128)(2,1)S(1)}, u32[]{:S(2)}, u32[]{:S(2)}) collective-permute-start(bf16[256,512]{1,0:T(8,128)(2,1)S(1)} %get-tuple-element.26), channel_id=1, source_target_pairs={{2,4},{3,5},{4,2},{5,3},{10,12},{11,13},{12,10},{13,11},{18,20},{1... | collective-permute-start | bytes 786440 | tf_op jit(solution)/shard_map/ppermute | solution.py:25
  36.4 5.1 %collective-permute-start.17 = (bf16[256,512]{1,0:T(8,128)(2,1)S(1)}, bf16[256,512]{1,0:T(8,128)(2,1)S(1)}, u32[]{:S(2)}, u32[]{:S(2)}) collective-permute-start(bf16[256,512]{1,0:T(8,128)(2,1)S(1)} %get-tuple-element.26), channel_id=1, source_target_pairs={{0,2},{1,3},{6,4},{7,5},{8,10},{9,11},{14,12},{15,13},{16,18},{17,... | collective-permute-start | bytes 786440 | tf_op jit(solution)/shard_map/ppermute | solution.py:25
  41.6 1.6 %collective-permute-start.20 = (bf16[256,512]{1,0:T(8,128)(2,1)S(1)}, bf16[256,512]{1,0:T(8,128)(2,1)S(1)}, u32[]{:S(2)}, u32[]{:S(2)}) collective-permute-start(bf16[256,512]{1,0:T(8,128)(2,1)S(1)} %get-tuple-element.29), channel_id=1, source_target_pairs={{0,1},{1,0},{2,3},{3,2},{4,5},{5,4},{6,7},{7,6},{8,9},{9,8},{10,11... | collective-permute-start | bytes 786440 | tf_op jit(solution)/shard_map/ppermute | solution.py:21
  43.2 0.0 collective-permute-done.14.refs_0_
  43.2 0.4 shard_map.39
  43.6 0.6 collective-permute-start.15
  44.1 1.7 %collective-permute-done.17.refs_0_ = bf16[256,512]{1,0:T(8,128)(2,1)S(1)} collective-permute-done((bf16[256,512]{1,0:T(8,128)(2,1)S(1)}, bf16[256,512]{1,0:T(8,128)(2,1)S(1)}, u32[]{:S(2)}, u32[]{:S(2)}) %collective-permute-start.17) | collective-permute-done | bytes 262176 | tf_op jit(solution)/shard_map/ppermute | solution.py:25
  45.8 0.3 shard_map.41
  46.1 0.0 collective-permute-done.18.refs_1_
  46.1 3.7 %collective-permute-start.19 = (bf16[256,512]{1,0:T(8,128)(2,1)S(1)}, bf16[256,512]{1,0:T(8,128)(2,1)S(1)}, u32[]{:S(2)}, u32[]{:S(2)}) collective-permute-start(bf16[256,512]{1,0:T(8,128)(2,1)S(1)} %shard_map.41), channel_id=1, source_target_pairs={{0,4},{1,5},{2,6},{3,7},{4,0},{5,1},{6,2},{7,3},{8,12},{9,13},{10,... | collective-permute-start | bytes 786440 | tf_op jit(solution)/shard_map/ppermute | solution.py:21
  49.8 1.1 %collective-permute-done.20.refs_0_ = bf16[256,512]{1,0:T(8,128)(2,1)S(1)} collective-permute-done((bf16[256,512]{1,0:T(8,128)(2,1)S(1)}, bf16[256,512]{1,0:T(8,128)(2,1)S(1)}, u32[]{:S(2)}, u32[]{:S(2)}) %collective-permute-start.20) | collective-permute-done | bytes 262176 | tf_op jit(solution)/shard_map/ppermute | solution.py:21
  50.9 0.4 shard_map.43
  51.3 0.1 collective-permute-start.21
  51.4 2.4 %collective-permute-done.15.refs_0_ = bf16[256,512]{1,0:T(8,128)(2,1)S(1)} collective-permute-done((bf16[256,512]{1,0:T(8,128)(2,1)S(1)}, bf16[256,512]{1,0:T(8,128)(2,1)S(1)}, u32[]{:S(2)}, u32[]{:S(2)}) %collective-permute-start.15) | collective-permute-done | bytes 262176 | tf_op jit(solution)/shard_map/ppermute | solution.py:21
  53.7 5.6 %collective-permute-done.19.refs_2_ = bf16[256,512]{1,0:T(8,128)(2,1)S(1)} collective-permute-done((bf16[256,512]{1,0:T(8,128)(2,1)S(1)}, bf16[256,512]{1,0:T(8,128)(2,1)S(1)}, u32[]{:S(2)}, u32[]{:S(2)}) %collective-permute-start.19) | collective-permute-done | bytes 262176 | tf_op jit(solution)/shard_map/ppermute | solution.py:21
  59.3 0.8 %shard_map.42.grad = f32[256,512]{1,0:T(8,128)S(1)} custom-call(bf16[256,4096]{1,0:T(8,128)(2,1)S(1)} %bitcast.7, bf16[256,256]{1,0:T(8,128)(2,1)S(1)} %get-tuple-element.21.local_t, bf16[256,512]{1,0:T(8,128)(2,1)S(1)} %collective-permute-done.15.refs_0_, bf16[256,512]{1,0:T(8,128)(2,1)S(1)} %collective-permute-done.18.refs_1_, ...), custom_call_target="tpu_custom_call" | custom-call | flops 20000000000 | bytes 3538944 | tf_op jit(solution)/shard_map/pallas_call | solution.py:35
  60.1 0.3 collective-permute-done.21.last
  60.4 0.2 shard_map.44
  60.6 0.1 collective-permute-start.22
  60.7 1.6 %collective-permute-start.23 = (bf16[64,512]{1,0:T(8,128)(2,1)S(1)}, bf16[64,512]{1,0:T(8,128)(2,1)S(1)}, u32[]{:S(2)}, u32[]{:S(2)}) collective-permute-start(bf16[64,512]{1,0:T(8,128)(2,1)S(1)} %get-tuple-element.33), channel_id=1, source_target_pairs={{0,16},{8,24},{16,0},{24,8},{1,17},{9,25},{17,1},{25,9},{2,18},{10... | collective-permute-start | bytes 196616 | tf_op jit(solution)/shard_map/ppermute | solution.py:21
  62.2 0.3 collective-permute-start.24
  62.6 0.0 collective-permute-done.22.refs_0_
  62.6 2.6 %collective-permute-done.23.refs_1_ = bf16[64,512]{1,0:T(8,128)(2,1)S(1)} collective-permute-done((bf16[64,512]{1,0:T(8,128)(2,1)S(1)}, bf16[64,512]{1,0:T(8,128)(2,1)S(1)}, u32[]{:S(2)}, u32[]{:S(2)}) %collective-permute-start.23) | collective-permute-done | bytes 65568 | tf_op jit(solution)/shard_map/ppermute | solution.py:21
  65.2 1.1 %collective-permute-done.24.refs_2_ = bf16[64,512]{1,0:T(8,128)(2,1)S(1)} collective-permute-done((bf16[64,512]{1,0:T(8,128)(2,1)S(1)}, bf16[64,512]{1,0:T(8,128)(2,1)S(1)}, u32[]{:S(2)}, u32[]{:S(2)}) %collective-permute-start.24) | collective-permute-done | bytes 65568 | tf_op jit(solution)/shard_map/ppermute | solution.py:21
  66.3 0.7 %shard_map.45 = f32[64,512]{1,0:T(8,128)} custom-call(f32[64,512]{1,0:T(8,128)S(1)} %get-tuple-element.31.own, bf16[64,512]{1,0:T(8,128)(2,1)S(1)} %collective-permute-done.22.refs_0_, bf16[64,512]{1,0:T(8,128)(2,1)S(1)} %collective-permute-done.23.refs_1_, bf16[64,512]{1,0:T(8,128)(2,1)S(1)} %collective-permute-done.24.refs_2_), custom_call_target="tpu_custom_call" | custom-call | flops 20000000000 | bytes 458752 | tf_op jit(solution)/shard_map/pallas_call | solution.py:35
  (2 shorter events, 0.0 us)
Async XLA Ops:
  0.9 23.9 %copy-start = (bf16[1,256,4096]{2,1,0:T(8,128)(2,1)S(1)}, bf16[1,256,4096]{2,1,0:T(8,128)(2,1)}, u32[]{:S(2)}) copy-start(bf16[1,256,4096]{2,1,0:T(8,128)(2,1)} %param.3) | copy-start | bytes 6291460
  0.9 23.9 %copy-start.1 = (bf16[512,256]{1,0:T(8,128)(2,1)S(1)}, bf16[512,256]{1,0:T(8,128)(2,1)}, u32[]{:S(2)}) copy-start(bf16[512,256]{1,0:T(8,128)(2,1)} %own.1) | copy-start | bytes 786436
  0.9 23.8 %copy-start.2 = (bf16[1,256,256]{2,1,0:T(8,128)(2,1)S(1)}, bf16[1,256,256]{2,1,0:T(8,128)(2,1)}, u32[]{:S(2)}) copy-start(bf16[1,256,256]{2,1,0:T(8,128)(2,1)} %param.5) | copy-start | bytes 393220
  1.0 9.5 %collective-permute-start.6 = (bf16[256,256]{1,0:T(8,128)(2,1)S(1)}, bf16[256,256]{1,0:T(8,128)(2,1)S(1)}, u32[]{:S(2)}, u32[]{:S(2)}) collective-permute-start(bf16[256,256]{1,0:T(8,128)(2,1)S(1)} %constant_dynamic-slice_fusion), channel_id=1, source_target_pairs={{0,6},{1,7},{2,4},{3,5},{4,2},{5,3},{6,0},{7,1},{8,14},{9,15},{10,... | collective-permute-start | bytes 393224 | tf_op jit(solution)/shard_map/ppermute | solution.py:21
  6.1 8.3 %collective-permute-start.2 = (bf16[256,256]{1,0:T(8,128)(2,1)S(1)}, bf16[256,256]{1,0:T(8,128)(2,1)S(1)}, u32[]{:S(2)}, u32[]{:S(2)}) collective-permute-start(bf16[256,256]{1,0:T(8,128)(2,1)S(1)} %constant_dynamic-slice_fusion), channel_id=1, source_target_pairs={{0,2},{1,3},{2,0},{3,1},{4,6},{5,7},{6,4},{7,5},{8,10},{9,11},{10,... | collective-permute-start | bytes 393224 | tf_op jit(solution)/shard_map/ppermute | solution.py:21
  6.1 9.4 %collective-permute-start = (bf16[256,256]{1,0:T(8,128)(2,1)S(1)}, bf16[256,256]{1,0:T(8,128)(2,1)S(1)}, u32[]{:S(2)}, u32[]{:S(2)}) collective-permute-start(bf16[256,256]{1,0:T(8,128)(2,1)S(1)} %constant_dynamic-slice_fusion), channel_id=1, source_target_pairs={{0,1},{1,0},{2,3},{3,2},{4,5},{5,4},{6,7},{7,6},{8,9},{9,8},{10,11... | collective-permute-start | bytes 393224 | tf_op jit(solution)/shard_map/ppermute | solution.py:21
  10.4 7.9 %collective-permute-start.10 = (bf16[256,256]{1,0:T(8,128)(2,1)S(1)}, bf16[256,256]{1,0:T(8,128)(2,1)S(1)}, u32[]{:S(2)}, u32[]{:S(2)}) collective-permute-start(bf16[256,256]{1,0:T(8,128)(2,1)S(1)} %constant_dynamic-slice_fusion), channel_id=1, source_target_pairs={{0,4},{1,5},{2,6},{3,7},{4,0},{5,1},{6,2},{7,3},{8,12},{9,13},{10,... | collective-permute-start | bytes 393224 | tf_op jit(solution)/shard_map/ppermute | solution.py:21
  12.8 7.0 %collective-permute-start.8 = (bf16[256,256]{1,0:T(8,128)(2,1)S(1)}, bf16[256,256]{1,0:T(8,128)(2,1)S(1)}, u32[]{:S(2)}, u32[]{:S(2)}) collective-permute-start(bf16[256,256]{1,0:T(8,128)(2,1)S(1)} %collective-permute-done.6.refs_6_), channel_id=1, source_target_pairs={{0,1},{1,0},{2,3},{3,2},{4,5},{5,4},{6,7},{7,6},{8,9},{9,8},{10,11... | collective-permute-start | bytes 393224 | tf_op jit(solution)/shard_map/ppermute | solution.py:21
  14.4 5.5 %collective-permute-start.7 = (bf16[256,256]{1,0:T(8,128)(2,1)S(1)}, bf16[256,256]{1,0:T(8,128)(2,1)S(1)}, u32[]{:S(2)}, u32[]{:S(2)}) collective-permute-start(bf16[256,256]{1,0:T(8,128)(2,1)S(1)} %collective-permute-done.6.refs_6_), channel_id=1, source_target_pairs={{0,8},{8,0},{16,24},{24,16},{1,9},{9,1},{17,25},{25,17},{2,10},{10... | collective-permute-start | bytes 393224 | tf_op jit(solution)/shard_map/ppermute | solution.py:21
  14.4 6.5 %collective-permute-start.4 = (bf16[256,256]{1,0:T(8,128)(2,1)S(1)}, bf16[256,256]{1,0:T(8,128)(2,1)S(1)}, u32[]{:S(2)}, u32[]{:S(2)}) collective-permute-start(bf16[256,256]{1,0:T(8,128)(2,1)S(1)} %shard_map.37), channel_id=1, source_target_pairs={{0,1},{1,0},{2,3},{3,2},{4,5},{5,4},{6,7},{7,6},{8,9},{9,8},{10,11... | collective-permute-start | bytes 393224 | tf_op jit(solution)/shard_map/ppermute | solution.py:21
  15.5 5.5 %collective-permute-start.3 = (bf16[256,256]{1,0:T(8,128)(2,1)S(1)}, bf16[256,256]{1,0:T(8,128)(2,1)S(1)}, u32[]{:S(2)}, u32[]{:S(2)}) collective-permute-start(bf16[256,256]{1,0:T(8,128)(2,1)S(1)} %collective-permute-done.2.piece.refs_2_), channel_id=1, source_target_pairs={{0,8},{8,0},{16,24},{24,16},{1,9},{9,1},{17,25},{25,17},{2,10},{10... | collective-permute-start | bytes 393224 | tf_op jit(solution)/shard_map/ppermute | solution.py:21
  18.4 5.0 %collective-permute-start.12 = (bf16[256,256]{1,0:T(8,128)(2,1)S(1)}, bf16[256,256]{1,0:T(8,128)(2,1)S(1)}, u32[]{:S(2)}, u32[]{:S(2)}) collective-permute-start(bf16[256,256]{1,0:T(8,128)(2,1)S(1)} %collective-permute-done.10.refs_10_), channel_id=1, source_target_pairs={{0,1},{1,0},{2,3},{3,2},{4,5},{5,4},{6,7},{7,6},{8,9},{9,8},{10,11... | collective-permute-start | bytes 393224 | tf_op jit(solution)/shard_map/ppermute | solution.py:21
  19.8 3.6 %collective-permute-start.1 = (bf16[256,256]{1,0:T(8,128)(2,1)S(1)}, bf16[256,256]{1,0:T(8,128)(2,1)S(1)}, u32[]{:S(2)}, u32[]{:S(2)}) collective-permute-start(bf16[256,256]{1,0:T(8,128)(2,1)S(1)} %collective-permute-done.refs_0_), channel_id=1, source_target_pairs={{0,8},{8,0},{16,24},{24,16},{1,9},{9,1},{17,25},{25,17},{2,10},{10... | collective-permute-start | bytes 393224 | tf_op jit(solution)/shard_map/ppermute | solution.py:21
  19.8 3.6 %collective-permute-start.11 = (bf16[256,256]{1,0:T(8,128)(2,1)S(1)}, bf16[256,256]{1,0:T(8,128)(2,1)S(1)}, u32[]{:S(2)}, u32[]{:S(2)}) collective-permute-start(bf16[256,256]{1,0:T(8,128)(2,1)S(1)} %collective-permute-done.10.refs_10_), channel_id=1, source_target_pairs={{0,8},{8,0},{16,24},{24,16},{1,9},{9,1},{17,25},{25,17},{2,10},{10... | collective-permute-start | bytes 393224 | tf_op jit(solution)/shard_map/ppermute | solution.py:21
  20.9 2.5 %collective-permute-start.9 = (bf16[256,256]{1,0:T(8,128)(2,1)S(1)}, bf16[256,256]{1,0:T(8,128)(2,1)S(1)}, u32[]{:S(2)}, u32[]{:S(2)}) collective-permute-start(bf16[256,256]{1,0:T(8,128)(2,1)S(1)} %collective-permute-done.8.refs_8_), channel_id=1, source_target_pairs={{0,8},{8,0},{16,24},{24,16},{1,9},{9,1},{17,25},{25,17},{2,10},{10... | collective-permute-start | bytes 393224 | tf_op jit(solution)/shard_map/ppermute | solution.py:21
  20.9 2.5 %collective-permute-start.5 = (bf16[256,256]{1,0:T(8,128)(2,1)S(1)}, bf16[256,256]{1,0:T(8,128)(2,1)S(1)}, u32[]{:S(2)}, u32[]{:S(2)}) collective-permute-start(bf16[256,256]{1,0:T(8,128)(2,1)S(1)} %collective-permute-done.4.refs_4_), channel_id=1, source_target_pairs={{0,8},{8,0},{16,24},{24,16},{1,9},{9,1},{17,25},{25,17},{2,10},{10... | collective-permute-start | bytes 393224 | tf_op jit(solution)/shard_map/ppermute | solution.py:21
  23.4 1.3 %collective-permute-start.13 = (bf16[256,256]{1,0:T(8,128)(2,1)S(1)}, bf16[256,256]{1,0:T(8,128)(2,1)S(1)}, u32[]{:S(2)}, u32[]{:S(2)}) collective-permute-start(bf16[256,256]{1,0:T(8,128)(2,1)S(1)} %collective-permute-done.12.refs_12_), channel_id=1, source_target_pairs={{0,8},{8,0},{16,24},{24,16},{1,9},{9,1},{17,25},{25,17},{2,10},{10... | collective-permute-start | bytes 393224 | tf_op jit(solution)/shard_map/ppermute | solution.py:21
  26.1 9.2 %collective-permute-start.16 = (bf16[256,512]{1,0:T(8,128)(2,1)S(1)}, bf16[256,512]{1,0:T(8,128)(2,1)S(1)}, u32[]{:S(2)}, u32[]{:S(2)}) collective-permute-start(bf16[256,512]{1,0:T(8,128)(2,1)S(1)} %get-tuple-element.25), channel_id=1, source_target_pairs={{0,1},{1,0},{2,3},{3,2},{4,5},{5,4},{6,7},{7,6},{8,9},{9,8},{10,11... | collective-permute-start | bytes 786440 | tf_op jit(solution)/shard_map/ppermute | solution.py:21
  27.7 15.5 %collective-permute-start.14 = (bf16[256,512]{1,0:T(8,128)(2,1)S(1)}, bf16[256,512]{1,0:T(8,128)(2,1)S(1)}, u32[]{:S(2)}, u32[]{:S(2)}) collective-permute-start(bf16[256,512]{1,0:T(8,128)(2,1)S(1)} %get-tuple-element.22), channel_id=1, source_target_pairs={{0,1},{1,0},{2,3},{3,2},{4,5},{5,4},{6,7},{7,6},{8,9},{9,8},{10,11... | collective-permute-start | bytes 786440 | tf_op jit(solution)/shard_map/ppermute | solution.py:21
  35.8 10.3 %collective-permute-start.18 = (bf16[256,512]{1,0:T(8,128)(2,1)S(1)}, bf16[256,512]{1,0:T(8,128)(2,1)S(1)}, u32[]{:S(2)}, u32[]{:S(2)}) collective-permute-start(bf16[256,512]{1,0:T(8,128)(2,1)S(1)} %get-tuple-element.26), channel_id=1, source_target_pairs={{2,4},{3,5},{4,2},{5,3},{10,12},{11,13},{12,10},{13,11},{18,20},{1... | collective-permute-start | bytes 786440 | tf_op jit(solution)/shard_map/ppermute | solution.py:25
  36.4 9.4 %collective-permute-start.17 = (bf16[256,512]{1,0:T(8,128)(2,1)S(1)}, bf16[256,512]{1,0:T(8,128)(2,1)S(1)}, u32[]{:S(2)}, u32[]{:S(2)}) collective-permute-start(bf16[256,512]{1,0:T(8,128)(2,1)S(1)} %get-tuple-element.26), channel_id=1, source_target_pairs={{0,2},{1,3},{6,4},{7,5},{8,10},{9,11},{14,12},{15,13},{16,18},{17,... | collective-permute-start | bytes 786440 | tf_op jit(solution)/shard_map/ppermute | solution.py:25
  41.6 9.3 %collective-permute-start.20 = (bf16[256,512]{1,0:T(8,128)(2,1)S(1)}, bf16[256,512]{1,0:T(8,128)(2,1)S(1)}, u32[]{:S(2)}, u32[]{:S(2)}) collective-permute-start(bf16[256,512]{1,0:T(8,128)(2,1)S(1)} %get-tuple-element.29), channel_id=1, source_target_pairs={{0,1},{1,0},{2,3},{3,2},{4,5},{5,4},{6,7},{7,6},{8,9},{9,8},{10,11... | collective-permute-start | bytes 786440 | tf_op jit(solution)/shard_map/ppermute | solution.py:21
  43.6 10.2 %collective-permute-start.15 = (bf16[256,512]{1,0:T(8,128)(2,1)S(1)}, bf16[256,512]{1,0:T(8,128)(2,1)S(1)}, u32[]{:S(2)}, u32[]{:S(2)}) collective-permute-start(bf16[256,512]{1,0:T(8,128)(2,1)S(1)} %get-tuple-element.23), channel_id=1, source_target_pairs={{0,1},{1,0},{2,3},{3,2},{4,5},{5,4},{6,7},{7,6},{8,9},{9,8},{10,11... | collective-permute-start | bytes 786440 | tf_op jit(solution)/shard_map/ppermute | solution.py:21
  46.1 13.2 %collective-permute-start.19 = (bf16[256,512]{1,0:T(8,128)(2,1)S(1)}, bf16[256,512]{1,0:T(8,128)(2,1)S(1)}, u32[]{:S(2)}, u32[]{:S(2)}) collective-permute-start(bf16[256,512]{1,0:T(8,128)(2,1)S(1)} %shard_map.41), channel_id=1, source_target_pairs={{0,4},{1,5},{2,6},{3,7},{4,0},{5,1},{6,2},{7,3},{8,12},{9,13},{10,... | collective-permute-start | bytes 786440 | tf_op jit(solution)/shard_map/ppermute | solution.py:21
  51.3 9.1 %collective-permute-start.21 = (bf16[256,512]{1,0:T(8,128)(2,1)S(1)}, bf16[256,512]{1,0:T(8,128)(2,1)S(1)}, u32[]{:S(2)}, u32[]{:S(2)}) collective-permute-start(bf16[256,512]{1,0:T(8,128)(2,1)S(1)} %shard_map.43), channel_id=1, source_target_pairs={{0,2},{1,3},{2,0},{3,1},{4,6},{5,7},{6,4},{7,5},{8,10},{9,11},{10,... | collective-permute-start | bytes 786440 | tf_op jit(solution)/shard_map/ppermute | solution.py:21
  60.6 1.9 %collective-permute-start.22 = (bf16[64,512]{1,0:T(8,128)(2,1)S(1)}, bf16[64,512]{1,0:T(8,128)(2,1)S(1)}, u32[]{:S(2)}, u32[]{:S(2)}) collective-permute-start(bf16[64,512]{1,0:T(8,128)(2,1)S(1)} %get-tuple-element.32), channel_id=1, source_target_pairs={{0,8},{8,0},{16,24},{24,16},{1,9},{9,1},{17,25},{25,17},{2,10},{10... | collective-permute-start | bytes 196616 | tf_op jit(solution)/shard_map/ppermute | solution.py:21
  60.7 4.5 %collective-permute-start.23 = (bf16[64,512]{1,0:T(8,128)(2,1)S(1)}, bf16[64,512]{1,0:T(8,128)(2,1)S(1)}, u32[]{:S(2)}, u32[]{:S(2)}) collective-permute-start(bf16[64,512]{1,0:T(8,128)(2,1)S(1)} %get-tuple-element.33), channel_id=1, source_target_pairs={{0,16},{8,24},{16,0},{24,8},{1,17},{9,25},{17,1},{25,9},{2,18},{10... | collective-permute-start | bytes 196616 | tf_op jit(solution)/shard_map/ppermute | solution.py:21
  62.2 4.0 %collective-permute-start.24 = (bf16[64,512]{1,0:T(8,128)(2,1)S(1)}, bf16[64,512]{1,0:T(8,128)(2,1)S(1)}, u32[]{:S(2)}, u32[]{:S(2)}) collective-permute-start(bf16[64,512]{1,0:T(8,128)(2,1)S(1)} %get-tuple-element.34), channel_id=1, source_target_pairs={{0,24},{8,16},{16,8},{24,0},{1,25},{9,17},{17,9},{25,1},{2,26},{10... | collective-permute-start | bytes 196616 | tf_op jit(solution)/shard_map/ppermute | solution.py:21

commit v3 on v2

--- a/solution.py
+++ b/solution.py
@@ -100,6 +100,12 @@
         put(out, chunk(k, a, local_t[...]))
 
 
+def far_kernel(far, send, a, local_t, other_a, other_t, out, next_out):
+    both = jnp.dot(other_t[...], other_a[...], preferred_element_type=F32)
+    put(out, both + chunk(far, a, local_t[...]))
+    put(next_out, chunk(send, a, local_t[...]))
+
+
 def add_kernel(mine, *refs):
     total = mine[...]
     for other in refs[:-1]:
@@ -136,20 +142,24 @@
     (copied,) = call(pass_kernel, [jax.ShapeDtypeStruct(half.shape, BF16)], held[2])
     held[3] = hop(copied, "seq", 1)
     held[7] = hop(held[6], "seq", 1)
-    held[5] = hop(held[4], "seq", 1)
+    block = (lax.axis_index("seq") ^ 7) * rows
+    other_a = hop(lax.dynamic_slice_in_dim(inputs, block, rows, 1), "seq", 1)
+    held[5] = hop(lax.optimization_barrier((held[4], other_a))[0], "seq", 1)
 
     block = lambda dtype: jax.ShapeDtypeStruct((hidden, rows), dtype)
     late = (1, 2, 3, 6, 7, 4, 5)
     pieces = []
     for k in late:
         pieces += [held[k], hop(held[k], "example", 1)]
-    six, four, local_t = call(
-        functools.partial(local_kernel, late, (7, 5)),
-        [block(BF16)] * 2 + [jax.ShapeDtypeStruct((hidden, tokens), BF16)],
+    four, local_t = call(
+        functools.partial(local_kernel, late, (5,)),
+        [block(BF16)] + [jax.ShapeDtypeStruct((hidden, tokens), BF16)],
         inputs, cotangent, gate_weight, *pieces,
     )
-    six, four = hop(six, "seq", 1), hop(four, "seq", 1)
-    far, two = call(functools.partial(sum_kernel, 6, (3,)), [block(BF16)] * 2, inputs, local_t, six)
+    other_t, four = hop(local_t, "seq", 1), hop(four, "seq", 1)
+    far, two = call(
+        functools.partial(far_kernel, 6, 3), [block(BF16)] * 2, inputs, local_t, other_a, other_t
+    )
     far, passed = (
         move(far, "seq", {i: 6 for i in (2, 3, 4, 5)}),
         move(far, "seq", {i: 2 for i in (0, 1, 6, 7)}),
@@ -160,9 +170,7 @@
     )
     none = hop(none, "seq", 1)
     (four,) = call(add_kernel, [block(BF16)], four, passed)
-    four, far = lax.optimization_barrier((four, far))
     four = hop(four, "seq", 4)
-    two = lax.optimization_barrier((two, far))[0]
     (two,) = call(functools.partial(sum_kernel, 2, ()), [block(BF16)], inputs, local_t, two, cost=1000)
     two = hop(two, "seq", 2)
     (grad,) = call(functools.partial(sum_kernel, 0, ()), [block(F32)], inputs, local_t, none, far, four)

time: 67.1 us -> 64.9 us (0.967)
  starting transfers between devices: 29.9 us -> 27.2 us
  local copies, waits for them, and re-layouts: 0.93 us -> 1.9 us
    ppermute x23 -> x24, starting transfers between devices: 24.1 us -> 22.6 us  [hop(): lax.ppermute(x, axis, [(i, i ^ k) for i in range(lax.axis_size(axis))])]
    ppermute x2, starting transfers between devices: 5.82 us -> 4.62 us  [move(): return lax.ppermute(x, axis, [(i, i ^ k) for i, k in hops.items()])]
    dynamic_slice x0 -> x1, local copies, waits for them, and re-layouts: none -> 0.97 us  [direct(): other_a = hop(lax.dynamic_slice_in_dim(inputs, block, rows, 1), 'seq', 1)]
    ppermute x23 -> x24, waiting for transfers between devices: 29.9 us -> 29.6 us  [hop(): lax.ppermute(x, axis, [(i, i ^ k) for i in range(lax.axis_size(axis))])]
  transfers between devices with their start and end apart: 25 -> 26, of which waited for: 13 -> 13; matrix products, arithmetic and copies ran while one was open for 0% -> 1% of each run, Pallas kernels for 3% -> 3%
where the time goes in v3:
time: 64.9 us; the launch traced here: 64.7 us
  waiting for transfers between devices  31.3 us (48%)
  starting transfers between devices  27.2 us (42%)
  Pallas kernels  4.22 us (7%)
  local copies, waits for them, and re-layouts  1.9 us (3%)
    ppermute x24, waiting for transfers between devices, hop(): lax.ppermute(x, axis, [(i, i ^ k) for i in range(lax.axis_size(axis))])  29.6 us
    ppermute x24, starting transfers between devices, hop(): lax.ppermute(x, axis, [(i, i ^ k) for i in range(lax.axis_size(axis))])  22.6 us
    ppermute x2, starting transfers between devices, move(): return lax.ppermute(x, axis, [(i, i ^ k) for i, k in hops.items()])  4.62 us
    pallas_call x9, Pallas kernels, call(): pl.pallas_call(kernel, out_shape=tuple(outs), in_specs=[vmem] * len(opera...  4.22 us
    ppermute x2, waiting for transfers between devices, move(): return lax.ppermute(x, axis, [(i, i ^ k) for i, k in hops.items()])  1.69 us
  transfers between devices with their start and end apart: 26, of which 13 were waited for; matrix products, arithmetic and copies ran while one was open for 1% of the time, Pallas kernels for 3%

profile of v3, /device:TPU:0, one launch (start us, length us, event | category | flops | bytes accessed | tf_op | source)
XLA Modules:
  0.0 64.7 jit_solution(1099679834934972342)
XLA Ops:
  0.0 0.9 %constant_dynamic-slice_fusion = bf16[256,256]{1,0:T(8,128)(2,1)S(1)} fusion(bf16[512,256]{1,0:T(8,128)(2,1)} %own.1, s32[]{:T(128)S(6)} %select_n.6), kind=kLoop, calls=%fused_computation.1 | loop fusion | bytes 262148 | tf_op jit(solution)/shard_map/dynamic_slice | solution.py:139
  0.9 5.1 %collective-permute-start.6 = (bf16[256,256]{1,0:T(8,128)(2,1)S(1)}, bf16[256,256]{1,0:T(8,128)(2,1)S(1)}, u32[]{:S(2)}, u32[]{:S(2)}) collective-permute-start(bf16[256,256]{1,0:T(8,128)(2,1)S(1)} %constant_dynamic-slice_fusion), channel_id=1, source_target_pairs={{0,6},{1,7},{2,4},{3,5},{4,2},{5,3},{6,0},{7,1},{8,14},{9,15},{10,... | collective-permute-start | bytes 393224 | tf_op jit(solution)/shard_map/ppermute | solution.py:21
  6.0 0.0 collective-permute-start.2
  6.0 1.5 %collective-permute-start = (bf16[256,256]{1,0:T(8,128)(2,1)S(1)}, bf16[256,256]{1,0:T(8,128)(2,1)S(1)}, u32[]{:S(2)}, u32[]{:S(2)}) collective-permute-start(bf16[256,256]{1,0:T(8,128)(2,1)S(1)} %constant_dynamic-slice_fusion), channel_id=1, source_target_pairs={{0,1},{1,0},{2,3},{3,2},{4,5},{5,4},{6,7},{7,6},{8,9},{9,8},{10,11... | collective-permute-start | bytes 393224 | tf_op jit(solution)/shard_map/ppermute | solution.py:21
  7.6 1.0 %dynamic-slice_bitcast_fusion = bf16[256,512]{1,0:T(8,128)(2,1)S(1)} fusion(bf16[1,256,4096]{2,1,0:T(8,128)(2,1)} %param.3, s32[]{:T(128)S(6)} %select_n.7), kind=kLoop, calls=%fused_computation | loop fusion | bytes 524292 | tf_op jit(solution)/shard_map/dynamic_slice | solution.py:146
  8.5 0.0 copy-start
  8.5 0.0 copy-start.1
  8.5 0.0 copy-start.2
  8.6 0.6 collective-permute-start.12
  9.1 1.3 %collective-permute-done.6.refs_6_ = bf16[256,256]{1,0:T(8,128)(2,1)S(1)} collective-permute-done((bf16[256,256]{1,0:T(8,128)(2,1)S(1)}, bf16[256,256]{1,0:T(8,128)(2,1)S(1)}, u32[]{:S(2)}, u32[]{:S(2)}) %collective-permute-start.6) | collective-permute-done | bytes 131104 | tf_op jit(solution)/shard_map/ppermute | solution.py:21
  10.4 2.4 %collective-permute-start.10 = (bf16[256,256]{1,0:T(8,128)(2,1)S(1)}, bf16[256,256]{1,0:T(8,128)(2,1)S(1)}, u32[]{:S(2)}, u32[]{:S(2)}) collective-permute-start(bf16[256,256]{1,0:T(8,128)(2,1)S(1)} %constant_dynamic-slice_fusion), channel_id=1, source_target_pairs={{0,4},{1,5},{2,6},{3,7},{4,0},{5,1},{6,2},{7,3},{8,12},{9,13},{10,... | collective-permute-start | bytes 393224 | tf_op jit(solution)/shard_map/ppermute | solution.py:21
  12.8 0.0 collective-permute-done.2.piece.refs_2_
  12.8 2.6 %collective-permute-start.4 = (bf16[256,256]{1,0:T(8,128)(2,1)S(1)}, bf16[256,256]{1,0:T(8,128)(2,1)S(1)}, u32[]{:S(2)}, u32[]{:S(2)}) collective-permute-start(bf16[256,256]{1,0:T(8,128)(2,1)S(1)} %shard_map.37), channel_id=1, source_target_pairs={{0,1},{1,0},{2,3},{3,2},{4,5},{5,4},{6,7},{7,6},{8,9},{9,8},{10,11... | collective-permute-start | bytes 393224 | tf_op jit(solution)/shard_map/ppermute | solution.py:21
  15.4 0.1 collective-permute-start.8
  15.5 2.8 %collective-permute-done.10.refs_10_ = bf16[256,256]{1,0:T(8,128)(2,1)S(1)} collective-permute-done((bf16[256,256]{1,0:T(8,128)(2,1)S(1)}, bf16[256,256]{1,0:T(8,128)(2,1)S(1)}, u32[]{:S(2)}, u32[]{:S(2)}) %collective-permute-start.10) | collective-permute-done | bytes 131104 | tf_op jit(solution)/shard_map/ppermute | solution.py:21
  18.3 0.0 collective-permute-start.7
  18.3 0.0 collective-permute-done.12.other_a
  18.4 0.5 collective-permute-start.3
  18.9 0.0 collective-permute-done.refs_0_
  18.9 1.4 %collective-permute-start.13 = (bf16[256,256]{1,0:T(8,128)(2,1)S(1)}, bf16[256,256]{1,0:T(8,128)(2,1)S(1)}, u32[]{:S(2)}, u32[]{:S(2)}) collective-permute-start(bf16[256,256]{1,0:T(8,128)(2,1)S(1)} %collective-permute-done.10.refs_10_), channel_id=1, source_target_pairs={{0,1},{1,0},{2,3},{3,2},{4,5},{5,4},{6,7},{7,6},{8,9},{9,8},{10,11... | collective-permute-start | bytes 393224 | tf_op jit(solution)/shard_map/ppermute | solution.py:21
  20.3 2.6 %collective-permute-done.8.refs_8_ = bf16[256,256]{1,0:T(8,128)(2,1)S(1)} collective-permute-done((bf16[256,256]{1,0:T(8,128)(2,1)S(1)}, bf16[256,256]{1,0:T(8,128)(2,1)S(1)}, u32[]{:S(2)}, u32[]{:S(2)}) %collective-permute-start.8) | collective-permute-done | bytes 131104 | tf_op jit(solution)/shard_map/ppermute | solution.py:21
  22.9 0.0 collective-permute-start.1
  22.9 0.0 collective-permute-done.7.refs_7_
  22.9 0.5 collective-permute-start.11
  23.4 0.0 collective-permute-done.4.refs_4_
  23.4 0.1 collective-permute-start.9
  23.5 0.0 collective-permute-done.3.refs_3_
  23.5 0.4 collective-permute-start.5
  23.9 1.1 %collective-permute-done.13.refs_12_ = bf16[256,256]{1,0:T(8,128)(2,1)S(1)} collective-permute-done((bf16[256,256]{1,0:T(8,128)(2,1)S(1)}, bf16[256,256]{1,0:T(8,128)(2,1)S(1)}, u32[]{:S(2)}, u32[]{:S(2)}) %collective-permute-start.13) | collective-permute-done | bytes 131104 | tf_op jit(solution)/shard_map/ppermute | solution.py:21
  25.0 0.0 collective-permute-start.14
  25.1 0.0 collective-permute-done.1.refs_1_
  25.1 0.0 collective-permute-done.11.refs_11_
  25.1 0.0 collective-permute-done.9.refs_9_
  25.1 0.0 collective-permute-done.5.refs_5_
  25.1 1.3 %collective-permute-done.14.refs_13_ = bf16[256,256]{1,0:T(8,128)(2,1)S(1)} collective-permute-done((bf16[256,256]{1,0:T(8,128)(2,1)S(1)}, bf16[256,256]{1,0:T(8,128)(2,1)S(1)}, u32[]{:S(2)}, u32[]{:S(2)}) %collective-permute-start.14) | collective-permute-done | bytes 131104 | tf_op jit(solution)/shard_map/ppermute | solution.py:21
  26.4 1.1 %shard_map.38 = (bf16[256,512]{1,0:T(8,128)(2,1)S(1)}, bf16[256,256]{1,0:T(8,128)(2,1)S(1)}) custom-call(bf16[256,4096]{1,0:T(8,128)(2,1)S(1)} %bitcast.5, bf16[256,256]{1,0:T(8,128)(2,1)S(1)} %bitcast.10, bf16[512,256]{1,0:T(8,128)(2,1)S(1)} %copy-done.1, bf16[256,256]{1,0:T(8,128)(2,1)S(1)} %collective-permute-done.refs_0_, ...), custom_call_target="tpu_custom_call" | custom-call | flops 20000000000 | bytes 4718592 | tf_op jit(solution)/shard_map/pallas_call | solution.py:35
  27.5 1.6 %collective-permute-start.17 = (bf16[256,256]{1,0:T(8,128)(2,1)S(1)}, bf16[256,256]{1,0:T(8,128)(2,1)S(1)}, u32[]{:S(2)}, u32[]{:S(2)}) collective-permute-start(bf16[256,256]{1,0:T(8,128)(2,1)S(1)} %get-tuple-element.19.local_t), channel_id=1, source_target_pairs={{0,1},{1,0},{2,3},{3,2},{4,5},{5,4},{6,7},{7,6},{8,9},{9,8},{10,11... | collective-permute-start | bytes 393224 | tf_op jit(solution)/shard_map/ppermute | solution.py:21
  29.1 0.5 collective-permute-start.15
  29.6 4.3 %collective-permute-done.17.other_t = bf16[256,256]{1,0:T(8,128)(2,1)S(1)} collective-permute-done((bf16[256,256]{1,0:T(8,128)(2,1)S(1)}, bf16[256,256]{1,0:T(8,128)(2,1)S(1)}, u32[]{:S(2)}, u32[]{:S(2)}) %collective-permute-start.17) | collective-permute-done | bytes 131104 | tf_op jit(solution)/shard_map/ppermute | solution.py:21
  33.9 0.4 shard_map.40
  34.3 3.9 %collective-permute-start.19 = (bf16[256,512]{1,0:T(8,128)(2,1)S(1)}, bf16[256,512]{1,0:T(8,128)(2,1)S(1)}, u32[]{:S(2)}, u32[]{:S(2)}) collective-permute-start(bf16[256,512]{1,0:T(8,128)(2,1)S(1)} %get-tuple-element.22), channel_id=1, source_target_pairs={{0,2},{1,3},{6,4},{7,5},{8,10},{9,11},{14,12},{15,13},{16,18},{17,... | collective-permute-start | bytes 786440 | tf_op jit(solution)/shard_map/ppermute | solution.py:25
  38.3 0.7 %collective-permute-start.18 = (bf16[256,512]{1,0:T(8,128)(2,1)S(1)}, bf16[256,512]{1,0:T(8,128)(2,1)S(1)}, u32[]{:S(2)}, u32[]{:S(2)}) collective-permute-start(bf16[256,512]{1,0:T(8,128)(2,1)S(1)} %get-tuple-element.22), channel_id=1, source_target_pairs={{2,4},{3,5},{4,2},{5,3},{10,12},{11,13},{12,10},{13,11},{18,20},{1... | collective-permute-start | bytes 786440 | tf_op jit(solution)/shard_map/ppermute | solution.py:25
  39.0 1.3 %collective-permute-start.21 = (bf16[256,512]{1,0:T(8,128)(2,1)S(1)}, bf16[256,512]{1,0:T(8,128)(2,1)S(1)}, u32[]{:S(2)}, u32[]{:S(2)}) collective-permute-start(bf16[256,512]{1,0:T(8,128)(2,1)S(1)} %get-tuple-element.24), channel_id=1, source_target_pairs={{0,1},{1,0},{2,3},{3,2},{4,5},{5,4},{6,7},{7,6},{8,9},{9,8},{10,11... | collective-permute-start | bytes 786440 | tf_op jit(solution)/shard_map/ppermute | solution.py:21
  40.3 0.0 collective-permute-done.15.refs_0_
  40.3 0.4 shard_map.39
  40.6 0.9 %collective-permute-start.16 = (bf16[256,512]{1,0:T(8,128)(2,1)S(1)}, bf16[256,512]{1,0:T(8,128)(2,1)S(1)}, u32[]{:S(2)}, u32[]{:S(2)}) collective-permute-start(bf16[256,512]{1,0:T(8,128)(2,1)S(1)} %get-tuple-element.21), channel_id=1, source_target_pairs={{0,1},{1,0},{2,3},{3,2},{4,5},{5,4},{6,7},{7,6},{8,9},{9,8},{10,11... | collective-permute-start | bytes 786440 | tf_op jit(solution)/shard_map/ppermute | solution.py:21
  41.5 1.7 %collective-permute-done.19.refs_0_ = bf16[256,512]{1,0:T(8,128)(2,1)S(1)} collective-permute-done((bf16[256,512]{1,0:T(8,128)(2,1)S(1)}, bf16[256,512]{1,0:T(8,128)(2,1)S(1)}, u32[]{:S(2)}, u32[]{:S(2)}) %collective-permute-start.19) | collective-permute-done | bytes 262176 | tf_op jit(solution)/shard_map/ppermute | solution.py:25
  43.2 0.3 shard_map.41
  43.5 0.4 collective-permute-start.20
  43.9 4.4 %collective-permute-done.21.refs_0_ = bf16[256,512]{1,0:T(8,128)(2,1)S(1)} collective-permute-done((bf16[256,512]{1,0:T(8,128)(2,1)S(1)}, bf16[256,512]{1,0:T(8,128)(2,1)S(1)}, u32[]{:S(2)}, u32[]{:S(2)}) %collective-permute-start.21) | collective-permute-done | bytes 262176 | tf_op jit(solution)/shard_map/ppermute | solution.py:21
  48.3 0.4 shard_map.43
  48.6 0.7 %collective-permute-start.22 = (bf16[256,512]{1,0:T(8,128)(2,1)S(1)}, bf16[256,512]{1,0:T(8,128)(2,1)S(1)}, u32[]{:S(2)}, u32[]{:S(2)}) collective-permute-start(bf16[256,512]{1,0:T(8,128)(2,1)S(1)} %shard_map.43), channel_id=1, source_target_pairs={{0,2},{1,3},{2,0},{3,1},{4,6},{5,7},{6,4},{7,5},{8,10},{9,11},{10,... | collective-permute-start | bytes 786440 | tf_op jit(solution)/shard_map/ppermute | solution.py:21
  49.3 0.0 collective-permute-done.18.refs_1_
  49.3 1.8 %collective-permute-done.16.refs_0_ = bf16[256,512]{1,0:T(8,128)(2,1)S(1)} collective-permute-done((bf16[256,512]{1,0:T(8,128)(2,1)S(1)}, bf16[256,512]{1,0:T(8,128)(2,1)S(1)}, u32[]{:S(2)}, u32[]{:S(2)}) %collective-permute-start.16) | collective-permute-done | bytes 262176 | tf_op jit(solution)/shard_map/ppermute | solution.py:21
  51.1 6.0 %collective-permute-done.20.refs_2_ = bf16[256,512]{1,0:T(8,128)(2,1)S(1)} collective-permute-done((bf16[256,512]{1,0:T(8,128)(2,1)S(1)}, bf16[256,512]{1,0:T(8,128)(2,1)S(1)}, u32[]{:S(2)}, u32[]{:S(2)}) %collective-permute-start.20) | collective-permute-done | bytes 262176 | tf_op jit(solution)/shard_map/ppermute | solution.py:21
  57.0 0.8 %shard_map.42.grad = f32[256,512]{1,0:T(8,128)S(1)} custom-call(bf16[256,4096]{1,0:T(8,128)(2,1)S(1)} %bitcast.9, bf16[256,256]{1,0:T(8,128)(2,1)S(1)} %get-tuple-element.19.local_t, bf16[256,512]{1,0:T(8,128)(2,1)S(1)} %collective-permute-done.16.refs_0_, bf16[256,512]{1,0:T(8,128)(2,1)S(1)} %collective-permute-done.18.refs_1_, ...), custom_call_target="tpu_custom_call" | custom-call | flops 20000000000 | bytes 3538944 | tf_op jit(solution)/shard_map/pallas_call | solution.py:35
  57.8 0.3 collective-permute-done.22.last
  58.1 0.2 shard_map.44
  58.3 0.1 collective-permute-start.23
  58.4 1.6 %collective-permute-start.24 = (bf16[64,512]{1,0:T(8,128)(2,1)S(1)}, bf16[64,512]{1,0:T(8,128)(2,1)S(1)}, u32[]{:S(2)}, u32[]{:S(2)}) collective-permute-start(bf16[64,512]{1,0:T(8,128)(2,1)S(1)} %get-tuple-element.27), channel_id=1, source_target_pairs={{0,16},{8,24},{16,0},{24,8},{1,17},{9,25},{17,1},{25,9},{2,18},{10... | collective-permute-start | bytes 196616 | tf_op jit(solution)/shard_map/ppermute | solution.py:21
  60.0 0.3 collective-permute-start.25
  60.3 2.6 %collective-permute-done.24.refs_1_ = bf16[64,512]{1,0:T(8,128)(2,1)S(1)} collective-permute-done((bf16[64,512]{1,0:T(8,128)(2,1)S(1)}, bf16[64,512]{1,0:T(8,128)(2,1)S(1)}, u32[]{:S(2)}, u32[]{:S(2)}) %collective-permute-start.24) | collective-permute-done | bytes 65568 | tf_op jit(solution)/shard_map/ppermute | solution.py:21
  62.9 1.1 %collective-permute-done.25.refs_2_ = bf16[64,512]{1,0:T(8,128)(2,1)S(1)} collective-permute-done((bf16[64,512]{1,0:T(8,128)(2,1)S(1)}, bf16[64,512]{1,0:T(8,128)(2,1)S(1)}, u32[]{:S(2)}, u32[]{:S(2)}) %collective-permute-start.25) | collective-permute-done | bytes 65568 | tf_op jit(solution)/shard_map/ppermute | solution.py:21
  64.1 0.7 %shard_map.45 = f32[64,512]{1,0:T(8,128)} custom-call(f32[64,512]{1,0:T(8,128)S(1)} %get-tuple-element.25.own, bf16[64,512]{1,0:T(8,128)(2,1)S(1)} %collective-permute-done.23.refs_0_, bf16[64,512]{1,0:T(8,128)(2,1)S(1)} %collective-permute-done.24.refs_1_, bf16[64,512]{1,0:T(8,128)(2,1)S(1)} %collective-permute-done.25.refs_2_), custom_call_target="tpu_custom_call" | custom-call | flops 20000000000 | bytes 458752 | tf_op jit(solution)/shard_map/pallas_call | solution.py:35
  (5 shorter events, 0.0 us)
Async XLA Ops:
  0.9 9.5 %collective-permute-start.6 = (bf16[256,256]{1,0:T(8,128)(2,1)S(1)}, bf16[256,256]{1,0:T(8,128)(2,1)S(1)}, u32[]{:S(2)}, u32[]{:S(2)}) collective-permute-start(bf16[256,256]{1,0:T(8,128)(2,1)S(1)} %constant_dynamic-slice_fusion), channel_id=1, source_target_pairs={{0,6},{1,7},{2,4},{3,5},{4,2},{5,3},{6,0},{7,1},{8,14},{9,15},{10,... | collective-permute-start | bytes 393224 | tf_op jit(solution)/shard_map/ppermute | solution.py:21
  6.0 6.8 %collective-permute-start.2 = (bf16[256,256]{1,0:T(8,128)(2,1)S(1)}, bf16[256,256]{1,0:T(8,128)(2,1)S(1)}, u32[]{:S(2)}, u32[]{:S(2)}) collective-permute-start(bf16[256,256]{1,0:T(8,128)(2,1)S(1)} %constant_dynamic-slice_fusion), channel_id=1, source_target_pairs={{0,2},{1,3},{2,0},{3,1},{4,6},{5,7},{6,4},{7,5},{8,10},{9,11},{10,... | collective-permute-start | bytes 393224 | tf_op jit(solution)/shard_map/ppermute | solution.py:21
  6.0 12.8 %collective-permute-start = (bf16[256,256]{1,0:T(8,128)(2,1)S(1)}, bf16[256,256]{1,0:T(8,128)(2,1)S(1)}, u32[]{:S(2)}, u32[]{:S(2)}) collective-permute-start(bf16[256,256]{1,0:T(8,128)(2,1)S(1)} %constant_dynamic-slice_fusion), channel_id=1, source_target_pairs={{0,1},{1,0},{2,3},{3,2},{4,5},{5,4},{6,7},{7,6},{8,9},{9,8},{10,11... | collective-permute-start | bytes 393224 | tf_op jit(solution)/shard_map/ppermute | solution.py:21
  8.5 17.9 %copy-start = (bf16[1,256,4096]{2,1,0:T(8,128)(2,1)S(1)}, bf16[1,256,4096]{2,1,0:T(8,128)(2,1)}, u32[]{:S(2)}) copy-start(bf16[1,256,4096]{2,1,0:T(8,128)(2,1)} %param.3) | copy-start | bytes 6291460
  8.5 17.9 %copy-start.1 = (bf16[512,256]{1,0:T(8,128)(2,1)S(1)}, bf16[512,256]{1,0:T(8,128)(2,1)}, u32[]{:S(2)}) copy-start(bf16[512,256]{1,0:T(8,128)(2,1)} %own.1) | copy-start | bytes 786436
  8.5 17.9 %copy-start.2 = (bf16[1,256,256]{2,1,0:T(8,128)(2,1)S(1)}, bf16[1,256,256]{2,1,0:T(8,128)(2,1)}, u32[]{:S(2)}) copy-start(bf16[1,256,256]{2,1,0:T(8,128)(2,1)} %param.5) | copy-start | bytes 393220
  8.6 9.8 %collective-permute-start.12 = (bf16[256,512]{1,0:T(8,128)(2,1)S(1)}, bf16[256,512]{1,0:T(8,128)(2,1)S(1)}, u32[]{:S(2)}, u32[]{:S(2)}) collective-permute-start(bf16[256,512]{1,0:T(8,128)(2,1)S(1)} %dynamic-slice_bitcast_fusion), channel_id=1, source_target_pairs={{0,1},{1,0},{2,3},{3,2},{4,5},{5,4},{6,7},{7,6},{8,9},{9,8},{10,11... | collective-permute-start | bytes 786440 | tf_op jit(solution)/shard_map/ppermute | solution.py:21
  10.4 7.9 %collective-permute-start.10 = (bf16[256,256]{1,0:T(8,128)(2,1)S(1)}, bf16[256,256]{1,0:T(8,128)(2,1)S(1)}, u32[]{:S(2)}, u32[]{:S(2)}) collective-permute-start(bf16[256,256]{1,0:T(8,128)(2,1)S(1)} %constant_dynamic-slice_fusion), channel_id=1, source_target_pairs={{0,4},{1,5},{2,6},{3,7},{4,0},{5,1},{6,2},{7,3},{8,12},{9,13},{10,... | collective-permute-start | bytes 393224 | tf_op jit(solution)/shard_map/ppermute | solution.py:21
  12.8 10.6 %collective-permute-start.4 = (bf16[256,256]{1,0:T(8,128)(2,1)S(1)}, bf16[256,256]{1,0:T(8,128)(2,1)S(1)}, u32[]{:S(2)}, u32[]{:S(2)}) collective-permute-start(bf16[256,256]{1,0:T(8,128)(2,1)S(1)} %shard_map.37), channel_id=1, source_target_pairs={{0,1},{1,0},{2,3},{3,2},{4,5},{5,4},{6,7},{7,6},{8,9},{9,8},{10,11... | collective-permute-start | bytes 393224 | tf_op jit(solution)/shard_map/ppermute | solution.py:21
  15.4 7.4 %collective-permute-start.8 = (bf16[256,256]{1,0:T(8,128)(2,1)S(1)}, bf16[256,256]{1,0:T(8,128)(2,1)S(1)}, u32[]{:S(2)}, u32[]{:S(2)}) collective-permute-start(bf16[256,256]{1,0:T(8,128)(2,1)S(1)} %collective-permute-done.6.refs_6_), channel_id=1, source_target_pairs={{0,1},{1,0},{2,3},{3,2},{4,5},{5,4},{6,7},{7,6},{8,9},{9,8},{10,11... | collective-permute-start | bytes 393224 | tf_op jit(solution)/shard_map/ppermute | solution.py:21
  18.3 4.5 %collective-permute-start.7 = (bf16[256,256]{1,0:T(8,128)(2,1)S(1)}, bf16[256,256]{1,0:T(8,128)(2,1)S(1)}, u32[]{:S(2)}, u32[]{:S(2)}) collective-permute-start(bf16[256,256]{1,0:T(8,128)(2,1)S(1)} %collective-permute-done.6.refs_6_), channel_id=1, source_target_pairs={{0,8},{8,0},{16,24},{24,16},{1,9},{9,1},{17,25},{25,17},{2,10},{10... | collective-permute-start | bytes 393224 | tf_op jit(solution)/shard_map/ppermute | solution.py:21
  18.4 5.1 %collective-permute-start.3 = (bf16[256,256]{1,0:T(8,128)(2,1)S(1)}, bf16[256,256]{1,0:T(8,128)(2,1)S(1)}, u32[]{:S(2)}, u32[]{:S(2)}) collective-permute-start(bf16[256,256]{1,0:T(8,128)(2,1)S(1)} %collective-permute-done.2.piece.refs_2_), channel_id=1, source_target_pairs={{0,8},{8,0},{16,24},{24,16},{1,9},{9,1},{17,25},{25,17},{2,10},{10... | collective-permute-start | bytes 393224 | tf_op jit(solution)/shard_map/ppermute | solution.py:21
  18.9 6.2 %collective-permute-start.13 = (bf16[256,256]{1,0:T(8,128)(2,1)S(1)}, bf16[256,256]{1,0:T(8,128)(2,1)S(1)}, u32[]{:S(2)}, u32[]{:S(2)}) collective-permute-start(bf16[256,256]{1,0:T(8,128)(2,1)S(1)} %collective-permute-done.10.refs_10_), channel_id=1, source_target_pairs={{0,1},{1,0},{2,3},{3,2},{4,5},{5,4},{6,7},{7,6},{8,9},{9,8},{10,11... | collective-permute-start | bytes 393224 | tf_op jit(solution)/shard_map/ppermute | solution.py:21
  22.9 2.2 %collective-permute-start.1 = (bf16[256,256]{1,0:T(8,128)(2,1)S(1)}, bf16[256,256]{1,0:T(8,128)(2,1)S(1)}, u32[]{:S(2)}, u32[]{:S(2)}) collective-permute-start(bf16[256,256]{1,0:T(8,128)(2,1)S(1)} %collective-permute-done.refs_0_), channel_id=1, source_target_pairs={{0,8},{8,0},{16,24},{24,16},{1,9},{9,1},{17,25},{25,17},{2,10},{10... | collective-permute-start | bytes 393224 | tf_op jit(solution)/shard_map/ppermute | solution.py:21
  22.9 2.2 %collective-permute-start.11 = (bf16[256,256]{1,0:T(8,128)(2,1)S(1)}, bf16[256,256]{1,0:T(8,128)(2,1)S(1)}, u32[]{:S(2)}, u32[]{:S(2)}) collective-permute-start(bf16[256,256]{1,0:T(8,128)(2,1)S(1)} %collective-permute-done.10.refs_10_), channel_id=1, source_target_pairs={{0,8},{8,0},{16,24},{24,16},{1,9},{9,1},{17,25},{25,17},{2,10},{10... | collective-permute-start | bytes 393224 | tf_op jit(solution)/shard_map/ppermute | solution.py:21
  23.4 1.7 %collective-permute-start.9 = (bf16[256,256]{1,0:T(8,128)(2,1)S(1)}, bf16[256,256]{1,0:T(8,128)(2,1)S(1)}, u32[]{:S(2)}, u32[]{:S(2)}) collective-permute-start(bf16[256,256]{1,0:T(8,128)(2,1)S(1)} %collective-permute-done.8.refs_8_), channel_id=1, source_target_pairs={{0,8},{8,0},{16,24},{24,16},{1,9},{9,1},{17,25},{25,17},{2,10},{10... | collective-permute-start | bytes 393224 | tf_op jit(solution)/shard_map/ppermute | solution.py:21
  23.5 1.6 %collective-permute-start.5 = (bf16[256,256]{1,0:T(8,128)(2,1)S(1)}, bf16[256,256]{1,0:T(8,128)(2,1)S(1)}, u32[]{:S(2)}, u32[]{:S(2)}) collective-permute-start(bf16[256,256]{1,0:T(8,128)(2,1)S(1)} %collective-permute-done.4.refs_4_), channel_id=1, source_target_pairs={{0,8},{8,0},{16,24},{24,16},{1,9},{9,1},{17,25},{25,17},{2,10},{10... | collective-permute-start | bytes 393224 | tf_op jit(solution)/shard_map/ppermute | solution.py:21
  25.0 1.3 %collective-permute-start.14 = (bf16[256,256]{1,0:T(8,128)(2,1)S(1)}, bf16[256,256]{1,0:T(8,128)(2,1)S(1)}, u32[]{:S(2)}, u32[]{:S(2)}) collective-permute-start(bf16[256,256]{1,0:T(8,128)(2,1)S(1)} %collective-permute-done.13.refs_12_), channel_id=1, source_target_pairs={{0,8},{8,0},{16,24},{24,16},{1,9},{9,1},{17,25},{25,17},{2,10},{10... | collective-permute-start | bytes 393224 | tf_op jit(solution)/shard_map/ppermute | solution.py:21
  27.5 6.4 %collective-permute-start.17 = (bf16[256,256]{1,0:T(8,128)(2,1)S(1)}, bf16[256,256]{1,0:T(8,128)(2,1)S(1)}, u32[]{:S(2)}, u32[]{:S(2)}) collective-permute-start(bf16[256,256]{1,0:T(8,128)(2,1)S(1)} %get-tuple-element.19.local_t), channel_id=1, source_target_pairs={{0,1},{1,0},{2,3},{3,2},{4,5},{5,4},{6,7},{7,6},{8,9},{9,8},{10,11... | collective-permute-start | bytes 393224 | tf_op jit(solution)/shard_map/ppermute | solution.py:21
  29.1 11.1 %collective-permute-start.15 = (bf16[256,512]{1,0:T(8,128)(2,1)S(1)}, bf16[256,512]{1,0:T(8,128)(2,1)S(1)}, u32[]{:S(2)}, u32[]{:S(2)}) collective-permute-start(bf16[256,512]{1,0:T(8,128)(2,1)S(1)} %get-tuple-element.20), channel_id=1, source_target_pairs={{0,1},{1,0},{2,3},{3,2},{4,5},{5,4},{6,7},{7,6},{8,9},{9,8},{10,11... | collective-permute-start | bytes 786440 | tf_op jit(solution)/shard_map/ppermute | solution.py:21
  34.3 8.9 %collective-permute-start.19 = (bf16[256,512]{1,0:T(8,128)(2,1)S(1)}, bf16[256,512]{1,0:T(8,128)(2,1)S(1)}, u32[]{:S(2)}, u32[]{:S(2)}) collective-permute-start(bf16[256,512]{1,0:T(8,128)(2,1)S(1)} %get-tuple-element.22), channel_id=1, source_target_pairs={{0,2},{1,3},{6,4},{7,5},{8,10},{9,11},{14,12},{15,13},{16,18},{17,... | collective-permute-start | bytes 786440 | tf_op jit(solution)/shard_map/ppermute | solution.py:25
  38.3 11.0 %collective-permute-start.18 = (bf16[256,512]{1,0:T(8,128)(2,1)S(1)}, bf16[256,512]{1,0:T(8,128)(2,1)S(1)}, u32[]{:S(2)}, u32[]{:S(2)}) collective-permute-start(bf16[256,512]{1,0:T(8,128)(2,1)S(1)} %get-tuple-element.22), channel_id=1, source_target_pairs={{2,4},{3,5},{4,2},{5,3},{10,12},{11,13},{12,10},{13,11},{18,20},{1... | collective-permute-start | bytes 786440 | tf_op jit(solution)/shard_map/ppermute | solution.py:25
  39.0 9.3 %collective-permute-start.21 = (bf16[256,512]{1,0:T(8,128)(2,1)S(1)}, bf16[256,512]{1,0:T(8,128)(2,1)S(1)}, u32[]{:S(2)}, u32[]{:S(2)}) collective-permute-start(bf16[256,512]{1,0:T(8,128)(2,1)S(1)} %get-tuple-element.24), channel_id=1, source_target_pairs={{0,1},{1,0},{2,3},{3,2},{4,5},{5,4},{6,7},{7,6},{8,9},{9,8},{10,11... | collective-permute-start | bytes 786440 | tf_op jit(solution)/shard_map/ppermute | solution.py:21
  40.6 10.5 %collective-permute-start.16 = (bf16[256,512]{1,0:T(8,128)(2,1)S(1)}, bf16[256,512]{1,0:T(8,128)(2,1)S(1)}, u32[]{:S(2)}, u32[]{:S(2)}) collective-permute-start(bf16[256,512]{1,0:T(8,128)(2,1)S(1)} %get-tuple-element.21), channel_id=1, source_target_pairs={{0,1},{1,0},{2,3},{3,2},{4,5},{5,4},{6,7},{7,6},{8,9},{9,8},{10,11... | collective-permute-start | bytes 786440 | tf_op jit(solution)/shard_map/ppermute | solution.py:21
  43.5 13.6 %collective-permute-start.20 = (bf16[256,512]{1,0:T(8,128)(2,1)S(1)}, bf16[256,512]{1,0:T(8,128)(2,1)S(1)}, u32[]{:S(2)}, u32[]{:S(2)}) collective-permute-start(bf16[256,512]{1,0:T(8,128)(2,1)S(1)} %shard_map.41), channel_id=1, source_target_pairs={{0,4},{1,5},{2,6},{3,7},{4,0},{5,1},{6,2},{7,3},{8,12},{9,13},{10,... | collective-permute-start | bytes 786440 | tf_op jit(solution)/shard_map/ppermute | solution.py:21
  48.6 9.4 %collective-permute-start.22 = (bf16[256,512]{1,0:T(8,128)(2,1)S(1)}, bf16[256,512]{1,0:T(8,128)(2,1)S(1)}, u32[]{:S(2)}, u32[]{:S(2)}) collective-permute-start(bf16[256,512]{1,0:T(8,128)(2,1)S(1)} %shard_map.43), channel_id=1, source_target_pairs={{0,2},{1,3},{2,0},{3,1},{4,6},{5,7},{6,4},{7,5},{8,10},{9,11},{10,... | collective-permute-start | bytes 786440 | tf_op jit(solution)/shard_map/ppermute | solution.py:21
  58.3 1.9 %collective-permute-start.23 = (bf16[64,512]{1,0:T(8,128)(2,1)S(1)}, bf16[64,512]{1,0:T(8,128)(2,1)S(1)}, u32[]{:S(2)}, u32[]{:S(2)}) collective-permute-start(bf16[64,512]{1,0:T(8,128)(2,1)S(1)} %get-tuple-element.26), channel_id=1, source_target_pairs={{0,8},{8,0},{16,24},{24,16},{1,9},{9,1},{17,25},{25,17},{2,10},{10... | collective-permute-start | bytes 196616 | tf_op jit(solution)/shard_map/ppermute | solution.py:21
  58.4 4.5 %collective-permute-start.24 = (bf16[64,512]{1,0:T(8,128)(2,1)S(1)}, bf16[64,512]{1,0:T(8,128)(2,1)S(1)}, u32[]{:S(2)}, u32[]{:S(2)}) collective-permute-start(bf16[64,512]{1,0:T(8,128)(2,1)S(1)} %get-tuple-element.27), channel_id=1, source_target_pairs={{0,16},{8,24},{16,0},{24,8},{1,17},{9,25},{17,1},{25,9},{2,18},{10... | collective-permute-start | bytes 196616 | tf_op jit(solution)/shard_map/ppermute | solution.py:21
  60.0 4.0 %collective-permute-start.25 = (bf16[64,512]{1,0:T(8,128)(2,1)S(1)}, bf16[64,512]{1,0:T(8,128)(2,1)S(1)}, u32[]{:S(2)}, u32[]{:S(2)}) collective-permute-start(bf16[64,512]{1,0:T(8,128)(2,1)S(1)} %get-tuple-element.28), channel_id=1, source_target_pairs={{0,24},{8,16},{16,8},{24,0},{1,25},{9,17},{17,9},{25,1},{2,26},{10... | collective-permute-start | bytes 196616 | tf_op jit(solution)/shard_map/ppermute | solution.py:21

commit v4 on v3

--- a/solution.py
+++ b/solution.py
@@ -139,8 +139,8 @@
     half = lax.dynamic_slice_in_dim(gate_weight, core * (rows // 2), rows // 2)
     held = {6: hop(half, "seq", 6), 2: hop(half, "seq", 2), 1: hop(half, "seq", 1)}
     held[4] = hop(lax.optimization_barrier((half, held[6]))[0], "seq", 4)
-    (copied,) = call(pass_kernel, [jax.ShapeDtypeStruct(half.shape, BF16)], held[2])
-    held[3] = hop(copied, "seq", 1)
+    (copied,) = call(pass_kernel, [jax.ShapeDtypeStruct(half.shape, BF16)], held[1])
+    held[3] = hop(copied, "seq", 2)
     held[7] = hop(held[6], "seq", 1)
     block = (lax.axis_index("seq") ^ 7) * rows
     other_a = hop(lax.dynamic_slice_in_dim(inputs, block, rows, 1), "seq", 1)

time: 64.9 us -> 63.1 us (0.972)
  waiting for transfers between devices: 31.3 us -> 26.1 us
  starting transfers between devices: 27.2 us -> 30.6 us
    ppermute x24, waiting for transfers between devices: 29.6 us -> 25.1 us  [hop(): lax.ppermute(x, axis, [(i, i ^ k) for i in range(lax.axis_size(axis))])]
    ppermute x24, starting transfers between devices: 22.6 us -> 26.9 us  [hop(): lax.ppermute(x, axis, [(i, i ^ k) for i in range(lax.axis_size(axis))])]
    ppermute x2, starting transfers between devices: 4.62 us -> 3.64 us  [move(): return lax.ppermute(x, axis, [(i, i ^ k) for i, k in hops.items()])]
    ppermute x2, waiting for transfers between devices: 1.69 us -> 0.95 us  [move(): return lax.ppermute(x, axis, [(i, i ^ k) for i, k in hops.items()])]
  transfers between devices with their start and end apart: 26 -> 26, of which waited for: 13 -> 13; matrix products, arithmetic and copies ran while one was open for 1% -> 2% of each run, Pallas kernels for 3% -> 3%
where the time goes in v4:
time: 63.1 us; the launch traced here: 62.9 us
  starting transfers between devices  30.6 us (48%)
  waiting for transfers between devices  26.1 us (41%)
  Pallas kernels  4.21 us (7%)
  local copies, waits for them, and re-layouts  1.9 us (3%)
    ppermute x24, starting transfers between devices, hop(): lax.ppermute(x, axis, [(i, i ^ k) for i in range(lax.axis_size(axis))])  26.9 us
    ppermute x24, waiting for transfers between devices, hop(): lax.ppermute(x, axis, [(i, i ^ k) for i in range(lax.axis_size(axis))])  25.1 us
    pallas_call x9, Pallas kernels, call(): pl.pallas_call(kernel, out_shape=tuple(outs), in_specs=[vmem] * len(opera...  4.21 us
    ppermute x2, starting transfers between devices, move(): return lax.ppermute(x, axis, [(i, i ^ k) for i, k in hops.items()])  3.64 us
  transfers between devices with their start and end apart: 26, of which 13 were waited for; matrix products, arithmetic and copies ran while one was open for 2% of the time, Pallas kernels for 3%

profile of v4, /device:TPU:0, one launch (start us, length us, event | category | flops | bytes accessed | tf_op | source)
XLA Modules:
  0.0 62.9 jit_solution(12348280305833474838)
XLA Ops:
  0.0 0.9 %constant_dynamic-slice_fusion = bf16[256,256]{1,0:T(8,128)(2,1)S(1)} fusion(bf16[512,256]{1,0:T(8,128)(2,1)} %own.1, s32[]{:T(128)S(6)} %select_n.6), kind=kLoop, calls=%fused_computation.1 | loop fusion | bytes 262148 | tf_op jit(solution)/shard_map/dynamic_slice | solution.py:139
  0.9 5.1 %collective-permute-start.6 = (bf16[256,256]{1,0:T(8,128)(2,1)S(1)}, bf16[256,256]{1,0:T(8,128)(2,1)S(1)}, u32[]{:S(2)}, u32[]{:S(2)}) collective-permute-start(bf16[256,256]{1,0:T(8,128)(2,1)S(1)} %constant_dynamic-slice_fusion), channel_id=1, source_target_pairs={{0,6},{1,7},{2,4},{3,5},{4,2},{5,3},{6,0},{7,1},{8,14},{9,15},{10,... | collective-permute-start | bytes 393224 | tf_op jit(solution)/shard_map/ppermute | solution.py:21
  6.0 1.5 %collective-permute-start = (bf16[256,256]{1,0:T(8,128)(2,1)S(1)}, bf16[256,256]{1,0:T(8,128)(2,1)S(1)}, u32[]{:S(2)}, u32[]{:S(2)}) collective-permute-start(bf16[256,256]{1,0:T(8,128)(2,1)S(1)} %constant_dynamic-slice_fusion), channel_id=1, source_target_pairs={{0,1},{1,0},{2,3},{3,2},{4,5},{5,4},{6,7},{7,6},{8,9},{9,8},{10,11... | collective-permute-start | bytes 393224 | tf_op jit(solution)/shard_map/ppermute | solution.py:21
  7.6 0.0 collective-permute-start.2
  7.6 1.0 %dynamic-slice_bitcast_fusion = bf16[256,512]{1,0:T(8,128)(2,1)S(1)} fusion(bf16[1,256,4096]{2,1,0:T(8,128)(2,1)} %param.3, s32[]{:T(128)S(6)} %select_n.7), kind=kLoop, calls=%fused_computation | loop fusion | bytes 524292 | tf_op jit(solution)/shard_map/dynamic_slice | solution.py:146
  8.5 0.0 copy-start
  8.5 0.0 copy-start.1
  8.5 0.0 copy-start.2
  8.6 0.6 collective-permute-start.12
  9.1 1.3 %collective-permute-done.6.refs_6_ = bf16[256,256]{1,0:T(8,128)(2,1)S(1)} collective-permute-done((bf16[256,256]{1,0:T(8,128)(2,1)S(1)}, bf16[256,256]{1,0:T(8,128)(2,1)S(1)}, u32[]{:S(2)}, u32[]{:S(2)}) %collective-permute-start.6) | collective-permute-done | bytes 131104 | tf_op jit(solution)/shard_map/ppermute | solution.py:21
  10.4 2.4 %collective-permute-start.10 = (bf16[256,256]{1,0:T(8,128)(2,1)S(1)}, bf16[256,256]{1,0:T(8,128)(2,1)S(1)}, u32[]{:S(2)}, u32[]{:S(2)}) collective-permute-start(bf16[256,256]{1,0:T(8,128)(2,1)S(1)} %constant_dynamic-slice_fusion), channel_id=1, source_target_pairs={{0,4},{1,5},{2,6},{3,7},{4,0},{5,1},{6,2},{7,3},{8,12},{9,13},{10,... | collective-permute-start | bytes 393224 | tf_op jit(solution)/shard_map/ppermute | solution.py:21
  12.8 0.0 collective-permute-done.piece.refs_0_
  12.8 2.0 %collective-permute-start.4 = (bf16[256,256]{1,0:T(8,128)(2,1)S(1)}, bf16[256,256]{1,0:T(8,128)(2,1)S(1)}, u32[]{:S(2)}, u32[]{:S(2)}) collective-permute-start(bf16[256,256]{1,0:T(8,128)(2,1)S(1)} %shard_map.37), channel_id=1, source_target_pairs={{0,2},{1,3},{2,0},{3,1},{4,6},{5,7},{6,4},{7,5},{8,10},{9,11},{10,... | collective-permute-start | bytes 393224 | tf_op jit(solution)/shard_map/ppermute | solution.py:21
  14.9 1.5 %collective-permute-start.8 = (bf16[256,256]{1,0:T(8,128)(2,1)S(1)}, bf16[256,256]{1,0:T(8,128)(2,1)S(1)}, u32[]{:S(2)}, u32[]{:S(2)}) collective-permute-start(bf16[256,256]{1,0:T(8,128)(2,1)S(1)} %collective-permute-done.6.refs_6_), channel_id=1, source_target_pairs={{0,1},{1,0},{2,3},{3,2},{4,5},{5,4},{6,7},{7,6},{8,9},{9,8},{10,11... | collective-permute-start | bytes 393224 | tf_op jit(solution)/shard_map/ppermute | solution.py:21
  16.4 0.0 collective-permute-done.2.refs_2_
  16.4 0.0 collective-permute-start.7
  16.4 1.5 %collective-permute-done.10.refs_10_ = bf16[256,256]{1,0:T(8,128)(2,1)S(1)} collective-permute-done((bf16[256,256]{1,0:T(8,128)(2,1)S(1)}, bf16[256,256]{1,0:T(8,128)(2,1)S(1)}, u32[]{:S(2)}, u32[]{:S(2)}) %collective-permute-start.10) | collective-permute-done | bytes 131104 | tf_op jit(solution)/shard_map/ppermute | solution.py:21
  17.9 0.0 collective-permute-start.3
  17.9 0.0 collective-permute-done.12.other_a
  17.9 1.7 %collective-permute-start.13 = (bf16[256,256]{1,0:T(8,128)(2,1)S(1)}, bf16[256,256]{1,0:T(8,128)(2,1)S(1)}, u32[]{:S(2)}, u32[]{:S(2)}) collective-permute-start(bf16[256,256]{1,0:T(8,128)(2,1)S(1)} %collective-permute-done.10.refs_10_), channel_id=1, source_target_pairs={{0,1},{1,0},{2,3},{3,2},{4,5},{5,4},{6,7},{7,6},{8,9},{9,8},{10,11... | collective-permute-start | bytes 393224 | tf_op jit(solution)/shard_map/ppermute | solution.py:21
  19.5 0.3 collective-permute-done.8.refs_8_
  19.8 0.0 collective-permute-start.1
  19.8 0.0 collective-permute-done.7.refs_7_
  19.8 0.5 collective-permute-start.11
  20.3 0.0 collective-permute-done.3.refs_3_
  20.3 0.1 collective-permute-start.9
  20.4 0.0 collective-permute-done.4.refs_4_
  20.4 0.4 collective-permute-start.5
  20.9 2.9 %collective-permute-done.13.refs_12_ = bf16[256,256]{1,0:T(8,128)(2,1)S(1)} collective-permute-done((bf16[256,256]{1,0:T(8,128)(2,1)S(1)}, bf16[256,256]{1,0:T(8,128)(2,1)S(1)}, u32[]{:S(2)}, u32[]{:S(2)}) %collective-permute-start.13) | collective-permute-done | bytes 131104 | tf_op jit(solution)/shard_map/ppermute | solution.py:21
  23.8 0.0 collective-permute-start.14
  23.8 0.0 collective-permute-done.1.refs_1_
  23.8 0.0 collective-permute-done.11.refs_11_
  23.8 0.0 collective-permute-done.9.refs_9_
  23.8 0.0 collective-permute-done.5.refs_5_
  23.8 1.3 %collective-permute-done.14.refs_13_ = bf16[256,256]{1,0:T(8,128)(2,1)S(1)} collective-permute-done((bf16[256,256]{1,0:T(8,128)(2,1)S(1)}, bf16[256,256]{1,0:T(8,128)(2,1)S(1)}, u32[]{:S(2)}, u32[]{:S(2)}) %collective-permute-start.14) | collective-permute-done | bytes 131104 | tf_op jit(solution)/shard_map/ppermute | solution.py:21
  25.1 1.1 %shard_map.38 = (bf16[256,512]{1,0:T(8,128)(2,1)S(1)}, bf16[256,256]{1,0:T(8,128)(2,1)S(1)}) custom-call(bf16[256,4096]{1,0:T(8,128)(2,1)S(1)} %bitcast.5, bf16[256,256]{1,0:T(8,128)(2,1)S(1)} %bitcast.10, bf16[512,256]{1,0:T(8,128)(2,1)S(1)} %copy-done.1, bf16[256,256]{1,0:T(8,128)(2,1)S(1)} %collective-permute-done.piece.refs_0_, ...), custom_call_target="tpu_custom_call" | custom-call | flops 20000000000 | bytes 4718592 | tf_op jit(solution)/shard_map/pallas_call | solution.py:35
  26.3 1.4 %collective-permute-start.17 = (bf16[256,256]{1,0:T(8,128)(2,1)S(1)}, bf16[256,256]{1,0:T(8,128)(2,1)S(1)}, u32[]{:S(2)}, u32[]{:S(2)}) collective-permute-start(bf16[256,256]{1,0:T(8,128)(2,1)S(1)} %get-tuple-element.19.local_t), channel_id=1, source_target_pairs={{0,1},{1,0},{2,3},{3,2},{4,5},{5,4},{6,7},{7,6},{8,9},{9,8},{10,11... | collective-permute-start | bytes 393224 | tf_op jit(solution)/shard_map/ppermute | solution.py:21
  27.7 0.7 %collective-permute-start.15 = (bf16[256,512]{1,0:T(8,128)(2,1)S(1)}, bf16[256,512]{1,0:T(8,128)(2,1)S(1)}, u32[]{:S(2)}, u32[]{:S(2)}) collective-permute-start(bf16[256,512]{1,0:T(8,128)(2,1)S(1)} %get-tuple-element.20), channel_id=1, source_target_pairs={{0,1},{1,0},{2,3},{3,2},{4,5},{5,4},{6,7},{7,6},{8,9},{9,8},{10,11... | collective-permute-start | bytes 786440 | tf_op jit(solution)/shard_map/ppermute | solution.py:21
  28.4 4.3 %collective-permute-done.17.other_t = bf16[256,256]{1,0:T(8,128)(2,1)S(1)} collective-permute-done((bf16[256,256]{1,0:T(8,128)(2,1)S(1)}, bf16[256,256]{1,0:T(8,128)(2,1)S(1)}, u32[]{:S(2)}, u32[]{:S(2)}) %collective-permute-start.17) | collective-permute-done | bytes 131104 | tf_op jit(solution)/shard_map/ppermute | solution.py:21
  32.7 0.4 shard_map.40
  33.1 3.0 %collective-permute-start.19 = (bf16[256,512]{1,0:T(8,128)(2,1)S(1)}, bf16[256,512]{1,0:T(8,128)(2,1)S(1)}, u32[]{:S(2)}, u32[]{:S(2)}) collective-permute-start(bf16[256,512]{1,0:T(8,128)(2,1)S(1)} %get-tuple-element.22), channel_id=1, source_target_pairs={{0,2},{1,3},{6,4},{7,5},{8,10},{9,11},{14,12},{15,13},{16,18},{17,... | collective-permute-start | bytes 786440 | tf_op jit(solution)/shard_map/ppermute | solution.py:25
  36.0 0.7 %collective-permute-start.18 = (bf16[256,512]{1,0:T(8,128)(2,1)S(1)}, bf16[256,512]{1,0:T(8,128)(2,1)S(1)}, u32[]{:S(2)}, u32[]{:S(2)}) collective-permute-start(bf16[256,512]{1,0:T(8,128)(2,1)S(1)} %get-tuple-element.22), channel_id=1, source_target_pairs={{2,4},{3,5},{4,2},{5,3},{10,12},{11,13},{12,10},{13,11},{18,20},{1... | collective-permute-start | bytes 786440 | tf_op jit(solution)/shard_map/ppermute | solution.py:25
  36.7 1.5 %collective-permute-start.21 = (bf16[256,512]{1,0:T(8,128)(2,1)S(1)}, bf16[256,512]{1,0:T(8,128)(2,1)S(1)}, u32[]{:S(2)}, u32[]{:S(2)}) collective-permute-start(bf16[256,512]{1,0:T(8,128)(2,1)S(1)} %get-tuple-element.24), channel_id=1, source_target_pairs={{0,1},{1,0},{2,3},{3,2},{4,5},{5,4},{6,7},{7,6},{8,9},{9,8},{10,11... | collective-permute-start | bytes 786440 | tf_op jit(solution)/shard_map/ppermute | solution.py:21
  38.2 0.0 collective-permute-done.15.refs_0_
  38.2 0.4 shard_map.39
  38.6 0.7 %collective-permute-start.16 = (bf16[256,512]{1,0:T(8,128)(2,1)S(1)}, bf16[256,512]{1,0:T(8,128)(2,1)S(1)}, u32[]{:S(2)}, u32[]{:S(2)}) collective-permute-start(bf16[256,512]{1,0:T(8,128)(2,1)S(1)} %get-tuple-element.21), channel_id=1, source_target_pairs={{0,1},{1,0},{2,3},{3,2},{4,5},{5,4},{6,7},{7,6},{8,9},{9,8},{10,11... | collective-permute-start | bytes 786440 | tf_op jit(solution)/shard_map/ppermute | solution.py:21
  39.3 1.0 %collective-permute-done.19.refs_0_ = bf16[256,512]{1,0:T(8,128)(2,1)S(1)} collective-permute-done((bf16[256,512]{1,0:T(8,128)(2,1)S(1)}, bf16[256,512]{1,0:T(8,128)(2,1)S(1)}, u32[]{:S(2)}, u32[]{:S(2)}) %collective-permute-start.19) | collective-permute-done | bytes 262176 | tf_op jit(solution)/shard_map/ppermute | solution.py:25
  40.2 0.3 shard_map.41
  40.5 3.2 %collective-permute-start.20 = (bf16[256,512]{1,0:T(8,128)(2,1)S(1)}, bf16[256,512]{1,0:T(8,128)(2,1)S(1)}, u32[]{:S(2)}, u32[]{:S(2)}) collective-permute-start(bf16[256,512]{1,0:T(8,128)(2,1)S(1)} %shard_map.41), channel_id=1, source_target_pairs={{0,4},{1,5},{2,6},{3,7},{4,0},{5,1},{6,2},{7,3},{8,12},{9,13},{10,... | collective-permute-start | bytes 786440 | tf_op jit(solution)/shard_map/ppermute | solution.py:21
  43.7 2.3 %collective-permute-done.21.refs_0_ = bf16[256,512]{1,0:T(8,128)(2,1)S(1)} collective-permute-done((bf16[256,512]{1,0:T(8,128)(2,1)S(1)}, bf16[256,512]{1,0:T(8,128)(2,1)S(1)}, u32[]{:S(2)}, u32[]{:S(2)}) %collective-permute-start.21) | collective-permute-done | bytes 262176 | tf_op jit(solution)/shard_map/ppermute | solution.py:21
  46.0 0.4 shard_map.43
  46.4 1.7 %collective-permute-start.22 = (bf16[256,512]{1,0:T(8,128)(2,1)S(1)}, bf16[256,512]{1,0:T(8,128)(2,1)S(1)}, u32[]{:S(2)}, u32[]{:S(2)}) collective-permute-start(bf16[256,512]{1,0:T(8,128)(2,1)S(1)} %shard_map.43), channel_id=1, source_target_pairs={{0,2},{1,3},{2,0},{3,1},{4,6},{5,7},{6,4},{7,5},{8,10},{9,11},{10,... | collective-permute-start | bytes 786440 | tf_op jit(solution)/shard_map/ppermute | solution.py:21
  48.1 0.0 collective-permute-done.18.refs_1_
  48.1 0.8 %collective-permute-done.16.refs_0_ = bf16[256,512]{1,0:T(8,128)(2,1)S(1)} collective-permute-done((bf16[256,512]{1,0:T(8,128)(2,1)S(1)}, bf16[256,512]{1,0:T(8,128)(2,1)S(1)}, u32[]{:S(2)}, u32[]{:S(2)}) %collective-permute-start.16) | collective-permute-done | bytes 262176 | tf_op jit(solution)/shard_map/ppermute | solution.py:21
  48.8 5.9 %collective-permute-done.20.refs_2_ = bf16[256,512]{1,0:T(8,128)(2,1)S(1)} collective-permute-done((bf16[256,512]{1,0:T(8,128)(2,1)S(1)}, bf16[256,512]{1,0:T(8,128)(2,1)S(1)}, u32[]{:S(2)}, u32[]{:S(2)}) %collective-permute-start.20) | collective-permute-done | bytes 262176 | tf_op jit(solution)/shard_map/ppermute | solution.py:21
  54.8 0.8 %shard_map.42.grad = f32[256,512]{1,0:T(8,128)S(1)} custom-call(bf16[256,4096]{1,0:T(8,128)(2,1)S(1)} %bitcast.9, bf16[256,256]{1,0:T(8,128)(2,1)S(1)} %get-tuple-element.19.local_t, bf16[256,512]{1,0:T(8,128)(2,1)S(1)} %collective-permute-done.16.refs_0_, bf16[256,512]{1,0:T(8,128)(2,1)S(1)} %collective-permute-done.18.refs_1_, ...), custom_call_target="tpu_custom_call" | custom-call | flops 20000000000 | bytes 3538944 | tf_op jit(solution)/shard_map/pallas_call | solution.py:35
  55.5 0.7 %collective-permute-done.22.last = bf16[256,512]{1,0:T(8,128)(2,1)S(1)} collective-permute-done((bf16[256,512]{1,0:T(8,128)(2,1)S(1)}, bf16[256,512]{1,0:T(8,128)(2,1)S(1)}, u32[]{:S(2)}, u32[]{:S(2)}) %collective-permute-start.22) | collective-permute-done | bytes 262176 | tf_op jit(solution)/shard_map/ppermute | solution.py:21
  56.2 0.2 shard_map.44
  56.5 0.1 collective-permute-start.23
  56.6 1.4 %collective-permute-start.24 = (bf16[64,512]{1,0:T(8,128)(2,1)S(1)}, bf16[64,512]{1,0:T(8,128)(2,1)S(1)}, u32[]{:S(2)}, u32[]{:S(2)}) collective-permute-start(bf16[64,512]{1,0:T(8,128)(2,1)S(1)} %get-tuple-element.27), channel_id=1, source_target_pairs={{0,16},{8,24},{16,0},{24,8},{1,17},{9,25},{17,1},{25,9},{2,18},{10... | collective-permute-start | bytes 196616 | tf_op jit(solution)/shard_map/ppermute | solution.py:21
  58.0 0.4 collective-permute-start.25
  58.4 2.7 %collective-permute-done.24.refs_1_ = bf16[64,512]{1,0:T(8,128)(2,1)S(1)} collective-permute-done((bf16[64,512]{1,0:T(8,128)(2,1)S(1)}, bf16[64,512]{1,0:T(8,128)(2,1)S(1)}, u32[]{:S(2)}, u32[]{:S(2)}) %collective-permute-start.24) | collective-permute-done | bytes 65568 | tf_op jit(solution)/shard_map/ppermute | solution.py:21
  61.2 1.0 %collective-permute-done.25.refs_2_ = bf16[64,512]{1,0:T(8,128)(2,1)S(1)} collective-permute-done((bf16[64,512]{1,0:T(8,128)(2,1)S(1)}, bf16[64,512]{1,0:T(8,128)(2,1)S(1)}, u32[]{:S(2)}, u32[]{:S(2)}) %collective-permute-start.25) | collective-permute-done | bytes 65568 | tf_op jit(solution)/shard_map/ppermute | solution.py:21
  62.2 0.7 %shard_map.45 = f32[64,512]{1,0:T(8,128)} custom-call(f32[64,512]{1,0:T(8,128)S(1)} %get-tuple-element.25.own, bf16[64,512]{1,0:T(8,128)(2,1)S(1)} %collective-permute-done.23.refs_0_, bf16[64,512]{1,0:T(8,128)(2,1)S(1)} %collective-permute-done.24.refs_1_, bf16[64,512]{1,0:T(8,128)(2,1)S(1)} %collective-permute-done.25.refs_2_), custom_call_target="tpu_custom_call" | custom-call | flops 20000000000 | bytes 458752 | tf_op jit(solution)/shard_map/pallas_call | solution.py:35
  (5 shorter events, 0.0 us)
Async XLA Ops:
  0.9 9.5 %collective-permute-start.6 = (bf16[256,256]{1,0:T(8,128)(2,1)S(1)}, bf16[256,256]{1,0:T(8,128)(2,1)S(1)}, u32[]{:S(2)}, u32[]{:S(2)}) collective-permute-start(bf16[256,256]{1,0:T(8,128)(2,1)S(1)} %constant_dynamic-slice_fusion), channel_id=1, source_target_pairs={{0,6},{1,7},{2,4},{3,5},{4,2},{5,3},{6,0},{7,1},{8,14},{9,15},{10,... | collective-permute-start | bytes 393224 | tf_op jit(solution)/shard_map/ppermute | solution.py:21
  6.0 6.8 %collective-permute-start = (bf16[256,256]{1,0:T(8,128)(2,1)S(1)}, bf16[256,256]{1,0:T(8,128)(2,1)S(1)}, u32[]{:S(2)}, u32[]{:S(2)}) collective-permute-start(bf16[256,256]{1,0:T(8,128)(2,1)S(1)} %constant_dynamic-slice_fusion), channel_id=1, source_target_pairs={{0,1},{1,0},{2,3},{3,2},{4,5},{5,4},{6,7},{7,6},{8,9},{9,8},{10,11... | collective-permute-start | bytes 393224 | tf_op jit(solution)/shard_map/ppermute | solution.py:21
  7.6 8.8 %collective-permute-start.2 = (bf16[256,256]{1,0:T(8,128)(2,1)S(1)}, bf16[256,256]{1,0:T(8,128)(2,1)S(1)}, u32[]{:S(2)}, u32[]{:S(2)}) collective-permute-start(bf16[256,256]{1,0:T(8,128)(2,1)S(1)} %constant_dynamic-slice_fusion), channel_id=1, source_target_pairs={{0,2},{1,3},{2,0},{3,1},{4,6},{5,7},{6,4},{7,5},{8,10},{9,11},{10,... | collective-permute-start | bytes 393224 | tf_op jit(solution)/shard_map/ppermute | solution.py:21
  8.5 16.6 %copy-start = (bf16[1,256,4096]{2,1,0:T(8,128)(2,1)S(1)}, bf16[1,256,4096]{2,1,0:T(8,128)(2,1)}, u32[]{:S(2)}) copy-start(bf16[1,256,4096]{2,1,0:T(8,128)(2,1)} %param.3) | copy-start | bytes 6291460
  8.5 16.6 %copy-start.1 = (bf16[512,256]{1,0:T(8,128)(2,1)S(1)}, bf16[512,256]{1,0:T(8,128)(2,1)}, u32[]{:S(2)}) copy-start(bf16[512,256]{1,0:T(8,128)(2,1)} %own.1) | copy-start | bytes 786436
  8.5 16.6 %copy-start.2 = (bf16[1,256,256]{2,1,0:T(8,128)(2,1)S(1)}, bf16[1,256,256]{2,1,0:T(8,128)(2,1)}, u32[]{:S(2)}) copy-start(bf16[1,256,256]{2,1,0:T(8,128)(2,1)} %param.5) | copy-start | bytes 393220
  8.6 9.3 %collective-permute-start.12 = (bf16[256,512]{1,0:T(8,128)(2,1)S(1)}, bf16[256,512]{1,0:T(8,128)(2,1)S(1)}, u32[]{:S(2)}, u32[]{:S(2)}) collective-permute-start(bf16[256,512]{1,0:T(8,128)(2,1)S(1)} %dynamic-slice_bitcast_fusion), channel_id=1, source_target_pairs={{0,1},{1,0},{2,3},{3,2},{4,5},{5,4},{6,7},{7,6},{8,9},{9,8},{10,11... | collective-permute-start | bytes 786440 | tf_op jit(solution)/shard_map/ppermute | solution.py:21
  10.4 7.5 %collective-permute-start.10 = (bf16[256,256]{1,0:T(8,128)(2,1)S(1)}, bf16[256,256]{1,0:T(8,128)(2,1)S(1)}, u32[]{:S(2)}, u32[]{:S(2)}) collective-permute-start(bf16[256,256]{1,0:T(8,128)(2,1)S(1)} %constant_dynamic-slice_fusion), channel_id=1, source_target_pairs={{0,4},{1,5},{2,6},{3,7},{4,0},{5,1},{6,2},{7,3},{8,12},{9,13},{10,... | collective-permute-start | bytes 393224 | tf_op jit(solution)/shard_map/ppermute | solution.py:21
  12.8 7.6 %collective-permute-start.4 = (bf16[256,256]{1,0:T(8,128)(2,1)S(1)}, bf16[256,256]{1,0:T(8,128)(2,1)S(1)}, u32[]{:S(2)}, u32[]{:S(2)}) collective-permute-start(bf16[256,256]{1,0:T(8,128)(2,1)S(1)} %shard_map.37), channel_id=1, source_target_pairs={{0,2},{1,3},{2,0},{3,1},{4,6},{5,7},{6,4},{7,5},{8,10},{9,11},{10,... | collective-permute-start | bytes 393224 | tf_op jit(solution)/shard_map/ppermute | solution.py:21
  14.9 5.0 %collective-permute-start.8 = (bf16[256,256]{1,0:T(8,128)(2,1)S(1)}, bf16[256,256]{1,0:T(8,128)(2,1)S(1)}, u32[]{:S(2)}, u32[]{:S(2)}) collective-permute-start(bf16[256,256]{1,0:T(8,128)(2,1)S(1)} %collective-permute-done.6.refs_6_), channel_id=1, source_target_pairs={{0,1},{1,0},{2,3},{3,2},{4,5},{5,4},{6,7},{7,6},{8,9},{9,8},{10,11... | collective-permute-start | bytes 393224 | tf_op jit(solution)/shard_map/ppermute | solution.py:21
  16.4 3.4 %collective-permute-start.7 = (bf16[256,256]{1,0:T(8,128)(2,1)S(1)}, bf16[256,256]{1,0:T(8,128)(2,1)S(1)}, u32[]{:S(2)}, u32[]{:S(2)}) collective-permute-start(bf16[256,256]{1,0:T(8,128)(2,1)S(1)} %collective-permute-done.6.refs_6_), channel_id=1, source_target_pairs={{0,8},{8,0},{16,24},{24,16},{1,9},{9,1},{17,25},{25,17},{2,10},{10... | collective-permute-start | bytes 393224 | tf_op jit(solution)/shard_map/ppermute | solution.py:21
  17.9 2.5 %collective-permute-start.3 = (bf16[256,256]{1,0:T(8,128)(2,1)S(1)}, bf16[256,256]{1,0:T(8,128)(2,1)S(1)}, u32[]{:S(2)}, u32[]{:S(2)}) collective-permute-start(bf16[256,256]{1,0:T(8,128)(2,1)S(1)} %collective-permute-done.2.refs_2_), channel_id=1, source_target_pairs={{0,8},{8,0},{16,24},{24,16},{1,9},{9,1},{17,25},{25,17},{2,10},{10... | collective-permute-start | bytes 393224 | tf_op jit(solution)/shard_map/ppermute | solution.py:21
  17.9 5.9 %collective-permute-start.13 = (bf16[256,256]{1,0:T(8,128)(2,1)S(1)}, bf16[256,256]{1,0:T(8,128)(2,1)S(1)}, u32[]{:S(2)}, u32[]{:S(2)}) collective-permute-start(bf16[256,256]{1,0:T(8,128)(2,1)S(1)} %collective-permute-done.10.refs_10_), channel_id=1, source_target_pairs={{0,1},{1,0},{2,3},{3,2},{4,5},{5,4},{6,7},{7,6},{8,9},{9,8},{10,11... | collective-permute-start | bytes 393224 | tf_op jit(solution)/shard_map/ppermute | solution.py:21
  19.8 4.0 %collective-permute-start.1 = (bf16[256,256]{1,0:T(8,128)(2,1)S(1)}, bf16[256,256]{1,0:T(8,128)(2,1)S(1)}, u32[]{:S(2)}, u32[]{:S(2)}) collective-permute-start(bf16[256,256]{1,0:T(8,128)(2,1)S(1)} %collective-permute-done.piece.refs_0_), channel_id=1, source_target_pairs={{0,8},{8,0},{16,24},{24,16},{1,9},{9,1},{17,25},{25,17},{2,10},{10... | collective-permute-start | bytes 393224 | tf_op jit(solution)/shard_map/ppermute | solution.py:21
  19.8 3.9 %collective-permute-start.11 = (bf16[256,256]{1,0:T(8,128)(2,1)S(1)}, bf16[256,256]{1,0:T(8,128)(2,1)S(1)}, u32[]{:S(2)}, u32[]{:S(2)}) collective-permute-start(bf16[256,256]{1,0:T(8,128)(2,1)S(1)} %collective-permute-done.10.refs_10_), channel_id=1, source_target_pairs={{0,8},{8,0},{16,24},{24,16},{1,9},{9,1},{17,25},{25,17},{2,10},{10... | collective-permute-start | bytes 393224 | tf_op jit(solution)/shard_map/ppermute | solution.py:21
  20.3 3.4 %collective-permute-start.9 = (bf16[256,256]{1,0:T(8,128)(2,1)S(1)}, bf16[256,256]{1,0:T(8,128)(2,1)S(1)}, u32[]{:S(2)}, u32[]{:S(2)}) collective-permute-start(bf16[256,256]{1,0:T(8,128)(2,1)S(1)} %collective-permute-done.8.refs_8_), channel_id=1, source_target_pairs={{0,8},{8,0},{16,24},{24,16},{1,9},{9,1},{17,25},{25,17},{2,10},{10... | collective-permute-start | bytes 393224 | tf_op jit(solution)/shard_map/ppermute | solution.py:21
  20.4 3.4 %collective-permute-start.5 = (bf16[256,256]{1,0:T(8,128)(2,1)S(1)}, bf16[256,256]{1,0:T(8,128)(2,1)S(1)}, u32[]{:S(2)}, u32[]{:S(2)}) collective-permute-start(bf16[256,256]{1,0:T(8,128)(2,1)S(1)} %collective-permute-done.4.refs_4_), channel_id=1, source_target_pairs={{0,8},{8,0},{16,24},{24,16},{1,9},{9,1},{17,25},{25,17},{2,10},{10... | collective-permute-start | bytes 393224 | tf_op jit(solution)/shard_map/ppermute | solution.py:21
  23.8 1.3 %collective-permute-start.14 = (bf16[256,256]{1,0:T(8,128)(2,1)S(1)}, bf16[256,256]{1,0:T(8,128)(2,1)S(1)}, u32[]{:S(2)}, u32[]{:S(2)}) collective-permute-start(bf16[256,256]{1,0:T(8,128)(2,1)S(1)} %collective-permute-done.13.refs_12_), channel_id=1, source_target_pairs={{0,8},{8,0},{16,24},{24,16},{1,9},{9,1},{17,25},{25,17},{2,10},{10... | collective-permute-start | bytes 393224 | tf_op jit(solution)/shard_map/ppermute | solution.py:21
  26.3 6.4 %collective-permute-start.17 = (bf16[256,256]{1,0:T(8,128)(2,1)S(1)}, bf16[256,256]{1,0:T(8,128)(2,1)S(1)}, u32[]{:S(2)}, u32[]{:S(2)}) collective-permute-start(bf16[256,256]{1,0:T(8,128)(2,1)S(1)} %get-tuple-element.19.local_t), channel_id=1, source_target_pairs={{0,1},{1,0},{2,3},{3,2},{4,5},{5,4},{6,7},{7,6},{8,9},{9,8},{10,11... | collective-permute-start | bytes 393224 | tf_op jit(solution)/shard_map/ppermute | solution.py:21
  27.7 10.6 %collective-permute-start.15 = (bf16[256,512]{1,0:T(8,128)(2,1)S(1)}, bf16[256,512]{1,0:T(8,128)(2,1)S(1)}, u32[]{:S(2)}, u32[]{:S(2)}) collective-permute-start(bf16[256,512]{1,0:T(8,128)(2,1)S(1)} %get-tuple-element.20), channel_id=1, source_target_pairs={{0,1},{1,0},{2,3},{3,2},{4,5},{5,4},{6,7},{7,6},{8,9},{9,8},{10,11... | collective-permute-start | bytes 786440 | tf_op jit(solution)/shard_map/ppermute | solution.py:21
  33.1 7.2 %collective-permute-start.19 = (bf16[256,512]{1,0:T(8,128)(2,1)S(1)}, bf16[256,512]{1,0:T(8,128)(2,1)S(1)}, u32[]{:S(2)}, u32[]{:S(2)}) collective-permute-start(bf16[256,512]{1,0:T(8,128)(2,1)S(1)} %get-tuple-element.22), channel_id=1, source_target_pairs={{0,2},{1,3},{6,4},{7,5},{8,10},{9,11},{14,12},{15,13},{16,18},{17,... | collective-permute-start | bytes 786440 | tf_op jit(solution)/shard_map/ppermute | solution.py:25
  36.0 12.0 %collective-permute-start.18 = (bf16[256,512]{1,0:T(8,128)(2,1)S(1)}, bf16[256,512]{1,0:T(8,128)(2,1)S(1)}, u32[]{:S(2)}, u32[]{:S(2)}) collective-permute-start(bf16[256,512]{1,0:T(8,128)(2,1)S(1)} %get-tuple-element.22), channel_id=1, source_target_pairs={{2,4},{3,5},{4,2},{5,3},{10,12},{11,13},{12,10},{13,11},{18,20},{1... | collective-permute-start | bytes 786440 | tf_op jit(solution)/shard_map/ppermute | solution.py:25
  36.7 9.3 %collective-permute-start.21 = (bf16[256,512]{1,0:T(8,128)(2,1)S(1)}, bf16[256,512]{1,0:T(8,128)(2,1)S(1)}, u32[]{:S(2)}, u32[]{:S(2)}) collective-permute-start(bf16[256,512]{1,0:T(8,128)(2,1)S(1)} %get-tuple-element.24), channel_id=1, source_target_pairs={{0,1},{1,0},{2,3},{3,2},{4,5},{5,4},{6,7},{7,6},{8,9},{9,8},{10,11... | collective-permute-start | bytes 786440 | tf_op jit(solution)/shard_map/ppermute | solution.py:21
  38.6 10.2 %collective-permute-start.16 = (bf16[256,512]{1,0:T(8,128)(2,1)S(1)}, bf16[256,512]{1,0:T(8,128)(2,1)S(1)}, u32[]{:S(2)}, u32[]{:S(2)}) collective-permute-start(bf16[256,512]{1,0:T(8,128)(2,1)S(1)} %get-tuple-element.21), channel_id=1, source_target_pairs={{0,1},{1,0},{2,3},{3,2},{4,5},{5,4},{6,7},{7,6},{8,9},{9,8},{10,11... | collective-permute-start | bytes 786440 | tf_op jit(solution)/shard_map/ppermute | solution.py:21
  40.5 14.2 %collective-permute-start.20 = (bf16[256,512]{1,0:T(8,128)(2,1)S(1)}, bf16[256,512]{1,0:T(8,128)(2,1)S(1)}, u32[]{:S(2)}, u32[]{:S(2)}) collective-permute-start(bf16[256,512]{1,0:T(8,128)(2,1)S(1)} %shard_map.41), channel_id=1, source_target_pairs={{0,4},{1,5},{2,6},{3,7},{4,0},{5,1},{6,2},{7,3},{8,12},{9,13},{10,... | collective-permute-start | bytes 786440 | tf_op jit(solution)/shard_map/ppermute | solution.py:21
  46.4 9.8 %collective-permute-start.22 = (bf16[256,512]{1,0:T(8,128)(2,1)S(1)}, bf16[256,512]{1,0:T(8,128)(2,1)S(1)}, u32[]{:S(2)}, u32[]{:S(2)}) collective-permute-start(bf16[256,512]{1,0:T(8,128)(2,1)S(1)} %shard_map.43), channel_id=1, source_target_pairs={{0,2},{1,3},{2,0},{3,1},{4,6},{5,7},{6,4},{7,5},{8,10},{9,11},{10,... | collective-permute-start | bytes 786440 | tf_op jit(solution)/shard_map/ppermute | solution.py:21
  56.5 1.9 %collective-permute-start.23 = (bf16[64,512]{1,0:T(8,128)(2,1)S(1)}, bf16[64,512]{1,0:T(8,128)(2,1)S(1)}, u32[]{:S(2)}, u32[]{:S(2)}) collective-permute-start(bf16[64,512]{1,0:T(8,128)(2,1)S(1)} %get-tuple-element.26), channel_id=1, source_target_pairs={{0,8},{8,0},{16,24},{24,16},{1,9},{9,1},{17,25},{25,17},{2,10},{10... | collective-permute-start | bytes 196616 | tf_op jit(solution)/shard_map/ppermute | solution.py:21
  56.6 4.6 %collective-permute-start.24 = (bf16[64,512]{1,0:T(8,128)(2,1)S(1)}, bf16[64,512]{1,0:T(8,128)(2,1)S(1)}, u32[]{:S(2)}, u32[]{:S(2)}) collective-permute-start(bf16[64,512]{1,0:T(8,128)(2,1)S(1)} %get-tuple-element.27), channel_id=1, source_target_pairs={{0,16},{8,24},{16,0},{24,8},{1,17},{9,25},{17,1},{25,9},{2,18},{10... | collective-permute-start | bytes 196616 | tf_op jit(solution)/shard_map/ppermute | solution.py:21
  58.0 4.2 %collective-permute-start.25 = (bf16[64,512]{1,0:T(8,128)(2,1)S(1)}, bf16[64,512]{1,0:T(8,128)(2,1)S(1)}, u32[]{:S(2)}, u32[]{:S(2)}) collective-permute-start(bf16[64,512]{1,0:T(8,128)(2,1)S(1)} %get-tuple-element.28), channel_id=1, source_target_pairs={{0,24},{8,16},{16,8},{24,0},{1,25},{9,17},{17,9},{25,1},{2,26},{10... | collective-permute-start | bytes 196616 | tf_op jit(solution)/shard_map/ppermute | solution.py:21

commit v5 on v4

--- a/solution.py
+++ b/solution.py
@@ -60,7 +60,10 @@
     half = pieces[0].shape[0]
     me = lax.axis_index("seq")
     core = lax.rem(lax.axis_index("example"), 2)
+    x = lax.div(lax.axis_index("example"), 2)
     for i, k in enumerate(hops):
+        if isinstance(k, tuple):
+            k = jnp.where(x == 0, *k)
         for flip in range(2):
             block = 2 * (me ^ k) + (core ^ flip)
             pre += jnp.dot(
@@ -137,19 +140,23 @@
 
     core = lax.rem(lax.axis_index("example"), 2)
     half = lax.dynamic_slice_in_dim(gate_weight, core * (rows // 2), rows // 2)
-    held = {6: hop(half, "seq", 6), 2: hop(half, "seq", 2), 1: hop(half, "seq", 1)}
-    held[4] = hop(lax.optimization_barrier((half, held[6]))[0], "seq", 4)
+    everyone = ("example", "seq")
+    size = examples * count
+    across = [(i, i ^ (4 if i // count < 2 else 6)) for i in range(size)]
+    held = {"own": lax.ppermute(half, everyone, across), 2: hop(half, "seq", 2), 1: hop(half, "seq", 1)}
     (copied,) = call(pass_kernel, [jax.ShapeDtypeStruct(half.shape, BF16)], held[1])
     held[3] = hop(copied, "seq", 2)
-    held[7] = hop(held[6], "seq", 1)
     block = (lax.axis_index("seq") ^ 7) * rows
     other_a = hop(lax.dynamic_slice_in_dim(inputs, block, rows, 1), "seq", 1)
-    held[5] = hop(lax.optimization_barrier((held[4], other_a))[0], "seq", 1)
+    held["x"] = hop(held["own"], "example", 2)
+    held["x"] = lax.optimization_barrier((held["x"], other_a))[0]
+    held["y"] = hop(held["own"], "seq", 1)
+    held["xy"] = hop(held["x"], "seq", 1)
 
     block = lambda dtype: jax.ShapeDtypeStruct((hidden, rows), dtype)
-    late = (1, 2, 3, 6, 7, 4, 5)
+    late = (1, 2, 3, (4, 6), (6, 4), (5, 7), (7, 5))
     pieces = []
-    for k in late:
+    for k in (1, 2, 3, "own", "x", "y", "xy"):
         pieces += [held[k], hop(held[k], "example", 1)]
     four, local_t = call(
         functools.partial(local_kernel, late, (5,)),
@@ -175,8 +182,8 @@
     two = hop(two, "seq", 2)
     (grad,) = call(functools.partial(sum_kernel, 0, ()), [block(F32)], inputs, local_t, none, far, four)
 
-    size = hidden // examples
-    part = lambda dtype: jax.ShapeDtypeStruct((size, rows), dtype)
+    share = hidden // examples
+    part = lambda dtype: jax.ShapeDtypeStruct((share, rows), dtype)
     own, *others = call(square_kernel, [part(F32)] + [part(BF16)] * (examples - 1), grad, two)
     others = [hop(x, "example", k + 1) for k, x in enumerate(others)]
     (total,) = call(
@@ -200,7 +207,8 @@
 
 def body(activations, gate_weight, seeds):
     rows, hidden = gate_weight.shape
-    fits = lax.axis_size("seq") == 8 and rows % 256 == 0 and hidden % (16 * lax.axis_size("example")) == 0
+    fits = lax.axis_size("seq") == 8 and lax.axis_size("example") == 4
+    fits = fits and rows % 256 == 0 and hidden % 64 == 0
     return (direct if fits else plain)(activations, gate_weight, seeds)
 
 

time: 63.1 us -> 62.4 us (0.989)
  starting transfers between devices: 30.6 us -> 28 us
  waiting for transfers between devices: 26.1 us -> 28 us
    ppermute x24 -> x23, starting transfers between devices: 26.9 us -> 20.5 us  [hop(): lax.ppermute(x, axis, [(i, i ^ k) for i in range(lax.axis_size(axis))])]
    ppermute x0 -> x1, starting transfers between devices: none -> 4.1 us  [direct(): lax.ppermute(half, everyone, across)]
    ppermute x0 -> x1, waiting for transfers between devices: none -> 1.74 us  [direct(): lax.ppermute(half, everyone, across)]
    ppermute x24 -> x23, waiting for transfers between devices: 25.1 us -> 25.4 us  [hop(): lax.ppermute(x, axis, [(i, i ^ k) for i in range(lax.axis_size(axis))])]
  transfers between devices with their start and end apart: 26 -> 26, of which waited for: 13 -> 14; matrix products, arithmetic and copies ran while one was open for 2% -> 2% of each run, Pallas kernels for 3% -> 3%
where the time goes in v5:
time: 62.4 us; the launch traced here: 62.2 us
  starting transfers between devices  28 us (45%)
  waiting for transfers between devices  28 us (45%)
  Pallas kernels  4.21 us (7%)
  local copies, waits for them, and re-layouts  1.9 us (3%)
    ppermute x23, waiting for transfers between devices, hop(): lax.ppermute(x, axis, [(i, i ^ k) for i in range(lax.axis_size(axis))])  25.4 us
    ppermute x23, starting transfers between devices, hop(): lax.ppermute(x, axis, [(i, i ^ k) for i in range(lax.axis_size(axis))])  20.5 us
    pallas_call x9, Pallas kernels, call(): pl.pallas_call(kernel, out_shape=tuple(outs), in_specs=[vmem] * len(opera...  4.21 us
    ppermute x1, starting transfers between devices, direct(): lax.ppermute(half, everyone, across)  4.1 us
    ppermute x2, starting transfers between devices, move(): return lax.ppermute(x, axis, [(i, i ^ k) for i, k in hops.items()])  3.38 us
    ppermute x1, waiting for transfers between devices, direct(): lax.ppermute(half, everyone, across)  1.74 us
  transfers between devices with their start and end apart: 26, of which 14 were waited for; matrix products, arithmetic and copies ran while one was open for 2% of the time, Pallas kernels for 3%

profile of v5, /device:TPU:0, one launch (start us, length us, event | category | flops | bytes accessed | tf_op | source)
XLA Modules:
  0.0 62.2 jit_solution(790472371457146615)
XLA Ops:
  0.0 0.9 %constant_dynamic-slice_fusion = bf16[256,256]{1,0:T(8,128)(2,1)S(1)} fusion(bf16[512,256]{1,0:T(8,128)(2,1)} %own.1, s32[]{:T(128)S(6)} %select_n.6), kind=kLoop, calls=%fused_computation.1 | loop fusion | bytes 262148 | tf_op jit(solution)/shard_map/dynamic_slice | solution.py:142
  0.9 4.1 %collective-permute-start.6 = (bf16[256,256]{1,0:T(8,128)(2,1)S(1)}, bf16[256,256]{1,0:T(8,128)(2,1)S(1)}, u32[]{:S(2)}, u32[]{:S(2)}) collective-permute-start(bf16[256,256]{1,0:T(8,128)(2,1)S(1)} %constant_dynamic-slice_fusion), channel_id=1, source_target_pairs={{0,4},{1,5},{2,6},{3,7},{4,0},{5,1},{6,2},{7,3},{8,12},{9,13},{10,... | collective-permute-start | bytes 393224 | tf_op jit(solution)/shard_map/ppermute | solution.py:146
  5.0 1.5 %collective-permute-start = (bf16[256,256]{1,0:T(8,128)(2,1)S(1)}, bf16[256,256]{1,0:T(8,128)(2,1)S(1)}, u32[]{:S(2)}, u32[]{:S(2)}) collective-permute-start(bf16[256,256]{1,0:T(8,128)(2,1)S(1)} %constant_dynamic-slice_fusion), channel_id=1, source_target_pairs={{0,1},{1,0},{2,3},{3,2},{4,5},{5,4},{6,7},{7,6},{8,9},{9,8},{10,11... | collective-permute-start | bytes 393224 | tf_op jit(solution)/shard_map/ppermute | solution.py:21
  6.5 1.6 %collective-permute-start.2 = (bf16[256,256]{1,0:T(8,128)(2,1)S(1)}, bf16[256,256]{1,0:T(8,128)(2,1)S(1)}, u32[]{:S(2)}, u32[]{:S(2)}) collective-permute-start(bf16[256,256]{1,0:T(8,128)(2,1)S(1)} %constant_dynamic-slice_fusion), channel_id=1, source_target_pairs={{0,2},{1,3},{2,0},{3,1},{4,6},{5,7},{6,4},{7,5},{8,10},{9,11},{10,... | collective-permute-start | bytes 393224 | tf_op jit(solution)/shard_map/ppermute | solution.py:21
  8.1 1.0 %dynamic-slice_bitcast_fusion = bf16[256,512]{1,0:T(8,128)(2,1)S(1)} fusion(bf16[1,256,4096]{2,1,0:T(8,128)(2,1)} %param.3, s32[]{:T(128)S(6)} %select_n.7), kind=kLoop, calls=%fused_computation | loop fusion | bytes 524292 | tf_op jit(solution)/shard_map/dynamic_slice | solution.py:150
  9.1 0.0 copy-start
  9.1 0.0 copy-start.1
  9.1 0.0 copy-start.2
  9.1 0.6 collective-permute-start.9
  9.7 1.7 %collective-permute-done.6.refs_6_ = bf16[256,256]{1,0:T(8,128)(2,1)S(1)} collective-permute-done((bf16[256,256]{1,0:T(8,128)(2,1)S(1)}, bf16[256,256]{1,0:T(8,128)(2,1)S(1)}, u32[]{:S(2)}, u32[]{:S(2)}) %collective-permute-start.6) | collective-permute-done | bytes 131104 | tf_op jit(solution)/shard_map/ppermute | solution.py:146
  11.4 0.7 %collective-permute-start.8 = (bf16[256,256]{1,0:T(8,128)(2,1)S(1)}, bf16[256,256]{1,0:T(8,128)(2,1)S(1)}, u32[]{:S(2)}, u32[]{:S(2)}) collective-permute-start(bf16[256,256]{1,0:T(8,128)(2,1)S(1)} %collective-permute-done.6.refs_6_), channel_id=1, source_target_pairs={{0,16},{8,24},{16,0},{24,8},{1,17},{9,25},{17,1},{25,9},{2,18},{10... | collective-permute-start | bytes 393224 | tf_op jit(solution)/shard_map/ppermute | solution.py:21
  12.1 0.0 collective-permute-done.piece.refs_0_
  12.1 1.5 %collective-permute-start.4 = (bf16[256,256]{1,0:T(8,128)(2,1)S(1)}, bf16[256,256]{1,0:T(8,128)(2,1)S(1)}, u32[]{:S(2)}, u32[]{:S(2)}) collective-permute-start(bf16[256,256]{1,0:T(8,128)(2,1)S(1)} %shard_map.37), channel_id=1, source_target_pairs={{0,2},{1,3},{2,0},{3,1},{4,6},{5,7},{6,4},{7,5},{8,10},{9,11},{10,... | collective-permute-start | bytes 393224 | tf_op jit(solution)/shard_map/ppermute | solution.py:21
  13.6 1.5 %collective-permute-start.11 = (bf16[256,256]{1,0:T(8,128)(2,1)S(1)}, bf16[256,256]{1,0:T(8,128)(2,1)S(1)}, u32[]{:S(2)}, u32[]{:S(2)}) collective-permute-start(bf16[256,256]{1,0:T(8,128)(2,1)S(1)} %collective-permute-done.6.refs_6_), channel_id=1, source_target_pairs={{0,1},{1,0},{2,3},{3,2},{4,5},{5,4},{6,7},{7,6},{8,9},{9,8},{10,11... | collective-permute-start | bytes 393224 | tf_op jit(solution)/shard_map/ppermute | solution.py:21
  15.1 0.0 collective-permute-done.2.refs_2_
  15.1 0.0 collective-permute-start.7
  15.2 1.2 %collective-permute-done.8.refs_8_ = bf16[256,256]{1,0:T(8,128)(2,1)S(1)} collective-permute-done((bf16[256,256]{1,0:T(8,128)(2,1)S(1)}, bf16[256,256]{1,0:T(8,128)(2,1)S(1)}, u32[]{:S(2)}, u32[]{:S(2)}) %collective-permute-start.8) | collective-permute-done | bytes 131104 | tf_op jit(solution)/shard_map/ppermute | solution.py:21
  16.4 0.0 collective-permute-start.3
  16.4 1.4 %collective-permute-done.9.other_a = bf16[256,512]{1,0:T(8,128)(2,1)S(1)} collective-permute-done((bf16[256,512]{1,0:T(8,128)(2,1)S(1)}, bf16[256,512]{1,0:T(8,128)(2,1)S(1)}, u32[]{:S(2)}, u32[]{:S(2)}) %collective-permute-start.9) | collective-permute-done | bytes 262176 | tf_op jit(solution)/shard_map/ppermute | solution.py:21
  17.8 0.2 collective-permute-start.13
  18.0 1.2 %collective-permute-done.11.refs_10_ = bf16[256,256]{1,0:T(8,128)(2,1)S(1)} collective-permute-done((bf16[256,256]{1,0:T(8,128)(2,1)S(1)}, bf16[256,256]{1,0:T(8,128)(2,1)S(1)}, u32[]{:S(2)}, u32[]{:S(2)}) %collective-permute-start.11) | collective-permute-done | bytes 131104 | tf_op jit(solution)/shard_map/ppermute | solution.py:21
  19.2 0.0 collective-permute-start.1
  19.2 0.0 collective-permute-done.7.refs_7_
  19.2 0.5 collective-permute-start.10
  19.7 0.0 collective-permute-done.3.refs_3_
  19.7 0.1 collective-permute-start.12
  19.8 0.0 collective-permute-done.4.refs_4_
  19.8 0.4 collective-permute-start.5
  20.2 2.5 %collective-permute-done.13.refs_12_ = bf16[256,256]{1,0:T(8,128)(2,1)S(1)} collective-permute-done((bf16[256,256]{1,0:T(8,128)(2,1)S(1)}, bf16[256,256]{1,0:T(8,128)(2,1)S(1)}, u32[]{:S(2)}, u32[]{:S(2)}) %collective-permute-start.13) | collective-permute-done | bytes 131104 | tf_op jit(solution)/shard_map/ppermute | solution.py:21
  22.8 0.0 collective-permute-start.14
  22.8 0.0 collective-permute-done.1.refs_1_
  22.8 0.0 collective-permute-done.12.refs_11_
  22.8 0.0 collective-permute-done.5.refs_5_
  22.8 0.0 collective-permute-done.10.refs_9_
  22.8 1.3 %collective-permute-done.14.refs_13_ = bf16[256,256]{1,0:T(8,128)(2,1)S(1)} collective-permute-done((bf16[256,256]{1,0:T(8,128)(2,1)S(1)}, bf16[256,256]{1,0:T(8,128)(2,1)S(1)}, u32[]{:S(2)}, u32[]{:S(2)}) %collective-permute-start.14) | collective-permute-done | bytes 131104 | tf_op jit(solution)/shard_map/ppermute | solution.py:21
  24.1 1.1 %shard_map.38 = (bf16[256,512]{1,0:T(8,128)(2,1)S(1)}, bf16[256,256]{1,0:T(8,128)(2,1)S(1)}) custom-call(bf16[256,4096]{1,0:T(8,128)(2,1)S(1)} %bitcast.5, bf16[256,256]{1,0:T(8,128)(2,1)S(1)} %bitcast.10, bf16[512,256]{1,0:T(8,128)(2,1)S(1)} %copy-done.1, bf16[256,256]{1,0:T(8,128)(2,1)S(1)} %collective-permute-done.piece.refs_0_, ...), custom_call_target="tpu_custom_call" | custom-call | flops 20000000000 | bytes 4718592 | tf_op jit(solution)/shard_map/pallas_call | solution.py:35
  25.3 1.2 %collective-permute-start.17 = (bf16[256,256]{1,0:T(8,128)(2,1)S(1)}, bf16[256,256]{1,0:T(8,128)(2,1)S(1)}, u32[]{:S(2)}, u32[]{:S(2)}) collective-permute-start(bf16[256,256]{1,0:T(8,128)(2,1)S(1)} %get-tuple-element.17.local_t), channel_id=1, source_target_pairs={{0,1},{1,0},{2,3},{3,2},{4,5},{5,4},{6,7},{7,6},{8,9},{9,8},{10,11... | collective-permute-start | bytes 393224 | tf_op jit(solution)/shard_map/ppermute | solution.py:21
  26.4 0.9 %collective-permute-start.15 = (bf16[256,512]{1,0:T(8,128)(2,1)S(1)}, bf16[256,512]{1,0:T(8,128)(2,1)S(1)}, u32[]{:S(2)}, u32[]{:S(2)}) collective-permute-start(bf16[256,512]{1,0:T(8,128)(2,1)S(1)} %get-tuple-element.18), channel_id=1, source_target_pairs={{0,1},{1,0},{2,3},{3,2},{4,5},{5,4},{6,7},{7,6},{8,9},{9,8},{10,11... | collective-permute-start | bytes 786440 | tf_op jit(solution)/shard_map/ppermute | solution.py:21
  27.3 4.3 %collective-permute-done.17.other_t = bf16[256,256]{1,0:T(8,128)(2,1)S(1)} collective-permute-done((bf16[256,256]{1,0:T(8,128)(2,1)S(1)}, bf16[256,256]{1,0:T(8,128)(2,1)S(1)}, u32[]{:S(2)}, u32[]{:S(2)}) %collective-permute-start.17) | collective-permute-done | bytes 131104 | tf_op jit(solution)/shard_map/ppermute | solution.py:21
  31.7 0.4 shard_map.40
  32.1 2.7 %collective-permute-start.19 = (bf16[256,512]{1,0:T(8,128)(2,1)S(1)}, bf16[256,512]{1,0:T(8,128)(2,1)S(1)}, u32[]{:S(2)}, u32[]{:S(2)}) collective-permute-start(bf16[256,512]{1,0:T(8,128)(2,1)S(1)} %get-tuple-element.20), channel_id=1, source_target_pairs={{0,2},{1,3},{6,4},{7,5},{8,10},{9,11},{14,12},{15,13},{16,18},{17,... | collective-permute-start | bytes 786440 | tf_op jit(solution)/shard_map/ppermute | solution.py:25
  34.8 0.7 %collective-permute-start.18 = (bf16[256,512]{1,0:T(8,128)(2,1)S(1)}, bf16[256,512]{1,0:T(8,128)(2,1)S(1)}, u32[]{:S(2)}, u32[]{:S(2)}) collective-permute-start(bf16[256,512]{1,0:T(8,128)(2,1)S(1)} %get-tuple-element.20), channel_id=1, source_target_pairs={{2,4},{3,5},{4,2},{5,3},{10,12},{11,13},{12,10},{13,11},{18,20},{1... | collective-permute-start | bytes 786440 | tf_op jit(solution)/shard_map/ppermute | solution.py:25
  35.5 1.5 %collective-permute-start.21 = (bf16[256,512]{1,0:T(8,128)(2,1)S(1)}, bf16[256,512]{1,0:T(8,128)(2,1)S(1)}, u32[]{:S(2)}, u32[]{:S(2)}) collective-permute-start(bf16[256,512]{1,0:T(8,128)(2,1)S(1)} %get-tuple-element.22), channel_id=1, source_target_pairs={{0,1},{1,0},{2,3},{3,2},{4,5},{5,4},{6,7},{7,6},{8,9},{9,8},{10,11... | collective-permute-start | bytes 786440 | tf_op jit(solution)/shard_map/ppermute | solution.py:21
  37.0 0.0 collective-permute-done.15.refs_0_
  37.0 0.4 shard_map.39
  37.4 0.7 %collective-permute-start.16 = (bf16[256,512]{1,0:T(8,128)(2,1)S(1)}, bf16[256,512]{1,0:T(8,128)(2,1)S(1)}, u32[]{:S(2)}, u32[]{:S(2)}) collective-permute-start(bf16[256,512]{1,0:T(8,128)(2,1)S(1)} %get-tuple-element.19), channel_id=1, source_target_pairs={{0,1},{1,0},{2,3},{3,2},{4,5},{5,4},{6,7},{7,6},{8,9},{9,8},{10,11... | collective-permute-start | bytes 786440 | tf_op jit(solution)/shard_map/ppermute | solution.py:21
  38.1 0.9 %collective-permute-done.19.refs_0_ = bf16[256,512]{1,0:T(8,128)(2,1)S(1)} collective-permute-done((bf16[256,512]{1,0:T(8,128)(2,1)S(1)}, bf16[256,512]{1,0:T(8,128)(2,1)S(1)}, u32[]{:S(2)}, u32[]{:S(2)}) %collective-permute-start.19) | collective-permute-done | bytes 262176 | tf_op jit(solution)/shard_map/ppermute | solution.py:25
  39.0 0.3 shard_map.41
  39.2 3.5 %collective-permute-start.20 = (bf16[256,512]{1,0:T(8,128)(2,1)S(1)}, bf16[256,512]{1,0:T(8,128)(2,1)S(1)}, u32[]{:S(2)}, u32[]{:S(2)}) collective-permute-start(bf16[256,512]{1,0:T(8,128)(2,1)S(1)} %shard_map.41), channel_id=1, source_target_pairs={{0,4},{1,5},{2,6},{3,7},{4,0},{5,1},{6,2},{7,3},{8,12},{9,13},{10,... | collective-permute-start | bytes 786440 | tf_op jit(solution)/shard_map/ppermute | solution.py:21
  42.7 2.1 %collective-permute-done.21.refs_0_ = bf16[256,512]{1,0:T(8,128)(2,1)S(1)} collective-permute-done((bf16[256,512]{1,0:T(8,128)(2,1)S(1)}, bf16[256,512]{1,0:T(8,128)(2,1)S(1)}, u32[]{:S(2)}, u32[]{:S(2)}) %collective-permute-start.21) | collective-permute-done | bytes 262176 | tf_op jit(solution)/shard_map/ppermute | solution.py:21
  44.8 0.4 shard_map.43
  45.1 1.8 %collective-permute-start.22 = (bf16[256,512]{1,0:T(8,128)(2,1)S(1)}, bf16[256,512]{1,0:T(8,128)(2,1)S(1)}, u32[]{:S(2)}, u32[]{:S(2)}) collective-permute-start(bf16[256,512]{1,0:T(8,128)(2,1)S(1)} %shard_map.43), channel_id=1, source_target_pairs={{0,2},{1,3},{2,0},{3,1},{4,6},{5,7},{6,4},{7,5},{8,10},{9,11},{10,... | collective-permute-start | bytes 786440 | tf_op jit(solution)/shard_map/ppermute | solution.py:21
  46.9 0.0 collective-permute-done.18.refs_1_
  46.9 0.8 %collective-permute-done.16.refs_0_ = bf16[256,512]{1,0:T(8,128)(2,1)S(1)} collective-permute-done((bf16[256,512]{1,0:T(8,128)(2,1)S(1)}, bf16[256,512]{1,0:T(8,128)(2,1)S(1)}, u32[]{:S(2)}, u32[]{:S(2)}) %collective-permute-start.16) | collective-permute-done | bytes 262176 | tf_op jit(solution)/shard_map/ppermute | solution.py:21
  47.7 5.8 %collective-permute-done.20.refs_2_ = bf16[256,512]{1,0:T(8,128)(2,1)S(1)} collective-permute-done((bf16[256,512]{1,0:T(8,128)(2,1)S(1)}, bf16[256,512]{1,0:T(8,128)(2,1)S(1)}, u32[]{:S(2)}, u32[]{:S(2)}) %collective-permute-start.20) | collective-permute-done | bytes 262176 | tf_op jit(solution)/shard_map/ppermute | solution.py:21
  53.5 0.8 %shard_map.42.grad = f32[256,512]{1,0:T(8,128)S(1)} custom-call(bf16[256,4096]{1,0:T(8,128)(2,1)S(1)} %bitcast.9, bf16[256,256]{1,0:T(8,128)(2,1)S(1)} %get-tuple-element.17.local_t, bf16[256,512]{1,0:T(8,128)(2,1)S(1)} %collective-permute-done.16.refs_0_, bf16[256,512]{1,0:T(8,128)(2,1)S(1)} %collective-permute-done.18.refs_1_, ...), custom_call_target="tpu_custom_call" | custom-call | flops 20000000000 | bytes 3538944 | tf_op jit(solution)/shard_map/pallas_call | solution.py:35
  54.2 0.7 %collective-permute-done.22.last = bf16[256,512]{1,0:T(8,128)(2,1)S(1)} collective-permute-done((bf16[256,512]{1,0:T(8,128)(2,1)S(1)}, bf16[256,512]{1,0:T(8,128)(2,1)S(1)}, u32[]{:S(2)}, u32[]{:S(2)}) %collective-permute-start.22) | collective-permute-done | bytes 262176 | tf_op jit(solution)/shard_map/ppermute | solution.py:21
  55.0 0.2 shard_map.44
  55.2 0.1 collective-permute-start.23
  55.3 2.2 %collective-permute-start.24 = (bf16[64,512]{1,0:T(8,128)(2,1)S(1)}, bf16[64,512]{1,0:T(8,128)(2,1)S(1)}, u32[]{:S(2)}, u32[]{:S(2)}) collective-permute-start(bf16[64,512]{1,0:T(8,128)(2,1)S(1)} %get-tuple-element.25), channel_id=1, source_target_pairs={{0,16},{8,24},{16,0},{24,8},{1,17},{9,25},{17,1},{25,9},{2,18},{10... | collective-permute-start | bytes 196616 | tf_op jit(solution)/shard_map/ppermute | solution.py:21
  57.5 0.1 collective-permute-start.25
  57.5 2.6 %collective-permute-done.24.refs_1_ = bf16[64,512]{1,0:T(8,128)(2,1)S(1)} collective-permute-done((bf16[64,512]{1,0:T(8,128)(2,1)S(1)}, bf16[64,512]{1,0:T(8,128)(2,1)S(1)}, u32[]{:S(2)}, u32[]{:S(2)}) %collective-permute-start.24) | collective-permute-done | bytes 65568 | tf_op jit(solution)/shard_map/ppermute | solution.py:21
  60.2 1.4 %collective-permute-done.25.refs_2_ = bf16[64,512]{1,0:T(8,128)(2,1)S(1)} collective-permute-done((bf16[64,512]{1,0:T(8,128)(2,1)S(1)}, bf16[64,512]{1,0:T(8,128)(2,1)S(1)}, u32[]{:S(2)}, u32[]{:S(2)}) %collective-permute-start.25) | collective-permute-done | bytes 65568 | tf_op jit(solution)/shard_map/ppermute | solution.py:21
  61.5 0.7 %shard_map.45 = f32[64,512]{1,0:T(8,128)} custom-call(f32[64,512]{1,0:T(8,128)S(1)} %get-tuple-element.23.own, bf16[64,512]{1,0:T(8,128)(2,1)S(1)} %collective-permute-done.23.refs_0_, bf16[64,512]{1,0:T(8,128)(2,1)S(1)} %collective-permute-done.24.refs_1_, bf16[64,512]{1,0:T(8,128)(2,1)S(1)} %collective-permute-done.25.refs_2_), custom_call_target="tpu_custom_call" | custom-call | flops 20000000000 | bytes 458752 | tf_op jit(solution)/shard_map/pallas_call | solution.py:35
  (5 shorter events, 0.0 us)
Async XLA Ops:
  0.9 10.5 %collective-permute-start.6 = (bf16[256,256]{1,0:T(8,128)(2,1)S(1)}, bf16[256,256]{1,0:T(8,128)(2,1)S(1)}, u32[]{:S(2)}, u32[]{:S(2)}) collective-permute-start(bf16[256,256]{1,0:T(8,128)(2,1)S(1)} %constant_dynamic-slice_fusion), channel_id=1, source_target_pairs={{0,4},{1,5},{2,6},{3,7},{4,0},{5,1},{6,2},{7,3},{8,12},{9,13},{10,... | collective-permute-start | bytes 393224 | tf_op jit(solution)/shard_map/ppermute | solution.py:146
  5.0 7.1 %collective-permute-start = (bf16[256,256]{1,0:T(8,128)(2,1)S(1)}, bf16[256,256]{1,0:T(8,128)(2,1)S(1)}, u32[]{:S(2)}, u32[]{:S(2)}) collective-permute-start(bf16[256,256]{1,0:T(8,128)(2,1)S(1)} %constant_dynamic-slice_fusion), channel_id=1, source_target_pairs={{0,1},{1,0},{2,3},{3,2},{4,5},{5,4},{6,7},{7,6},{8,9},{9,8},{10,11... | collective-permute-start | bytes 393224 | tf_op jit(solution)/shard_map/ppermute | solution.py:21
  6.5 8.6 %collective-permute-start.2 = (bf16[256,256]{1,0:T(8,128)(2,1)S(1)}, bf16[256,256]{1,0:T(8,128)(2,1)S(1)}, u32[]{:S(2)}, u32[]{:S(2)}) collective-permute-start(bf16[256,256]{1,0:T(8,128)(2,1)S(1)} %constant_dynamic-slice_fusion), channel_id=1, source_target_pairs={{0,2},{1,3},{2,0},{3,1},{4,6},{5,7},{6,4},{7,5},{8,10},{9,11},{10,... | collective-permute-start | bytes 393224 | tf_op jit(solution)/shard_map/ppermute | solution.py:21
  9.1 15.0 %copy-start = (bf16[1,256,4096]{2,1,0:T(8,128)(2,1)S(1)}, bf16[1,256,4096]{2,1,0:T(8,128)(2,1)}, u32[]{:S(2)}) copy-start(bf16[1,256,4096]{2,1,0:T(8,128)(2,1)} %param.3) | copy-start | bytes 6291460
  9.1 15.0 %copy-start.1 = (bf16[512,256]{1,0:T(8,128)(2,1)S(1)}, bf16[512,256]{1,0:T(8,128)(2,1)}, u32[]{:S(2)}) copy-start(bf16[512,256]{1,0:T(8,128)(2,1)} %own.1) | copy-start | bytes 786436
  9.1 15.0 %copy-start.2 = (bf16[1,256,256]{2,1,0:T(8,128)(2,1)S(1)}, bf16[1,256,256]{2,1,0:T(8,128)(2,1)}, u32[]{:S(2)}) copy-start(bf16[1,256,256]{2,1,0:T(8,128)(2,1)} %param.5) | copy-start | bytes 393220
  9.1 8.7 %collective-permute-start.9 = (bf16[256,512]{1,0:T(8,128)(2,1)S(1)}, bf16[256,512]{1,0:T(8,128)(2,1)S(1)}, u32[]{:S(2)}, u32[]{:S(2)}) collective-permute-start(bf16[256,512]{1,0:T(8,128)(2,1)S(1)} %dynamic-slice_bitcast_fusion), channel_id=1, source_target_pairs={{0,1},{1,0},{2,3},{3,2},{4,5},{5,4},{6,7},{7,6},{8,9},{9,8},{10,11... | collective-permute-start | bytes 786440 | tf_op jit(solution)/shard_map/ppermute | solution.py:21
  11.4 5.0 %collective-permute-start.8 = (bf16[256,256]{1,0:T(8,128)(2,1)S(1)}, bf16[256,256]{1,0:T(8,128)(2,1)S(1)}, u32[]{:S(2)}, u32[]{:S(2)}) collective-permute-start(bf16[256,256]{1,0:T(8,128)(2,1)S(1)} %collective-permute-done.6.refs_6_), channel_id=1, source_target_pairs={{0,16},{8,24},{16,0},{24,8},{1,17},{9,25},{17,1},{25,9},{2,18},{10... | collective-permute-start | bytes 393224 | tf_op jit(solution)/shard_map/ppermute | solution.py:21
  12.1 7.7 %collective-permute-start.4 = (bf16[256,256]{1,0:T(8,128)(2,1)S(1)}, bf16[256,256]{1,0:T(8,128)(2,1)S(1)}, u32[]{:S(2)}, u32[]{:S(2)}) collective-permute-start(bf16[256,256]{1,0:T(8,128)(2,1)S(1)} %shard_map.37), channel_id=1, source_target_pairs={{0,2},{1,3},{2,0},{3,1},{4,6},{5,7},{6,4},{7,5},{8,10},{9,11},{10,... | collective-permute-start | bytes 393224 | tf_op jit(solution)/shard_map/ppermute | solution.py:21
  13.6 5.6 %collective-permute-start.11 = (bf16[256,256]{1,0:T(8,128)(2,1)S(1)}, bf16[256,256]{1,0:T(8,128)(2,1)S(1)}, u32[]{:S(2)}, u32[]{:S(2)}) collective-permute-start(bf16[256,256]{1,0:T(8,128)(2,1)S(1)} %collective-permute-done.6.refs_6_), channel_id=1, source_target_pairs={{0,1},{1,0},{2,3},{3,2},{4,5},{5,4},{6,7},{7,6},{8,9},{9,8},{10,11... | collective-permute-start | bytes 393224 | tf_op jit(solution)/shard_map/ppermute | solution.py:21
  15.1 4.1 %collective-permute-start.7 = (bf16[256,256]{1,0:T(8,128)(2,1)S(1)}, bf16[256,256]{1,0:T(8,128)(2,1)S(1)}, u32[]{:S(2)}, u32[]{:S(2)}) collective-permute-start(bf16[256,256]{1,0:T(8,128)(2,1)S(1)} %collective-permute-done.6.refs_6_), channel_id=1, source_target_pairs={{0,8},{8,0},{16,24},{24,16},{1,9},{9,1},{17,25},{25,17},{2,10},{10... | collective-permute-start | bytes 393224 | tf_op jit(solution)/shard_map/ppermute | solution.py:21
  16.4 3.3 %collective-permute-start.3 = (bf16[256,256]{1,0:T(8,128)(2,1)S(1)}, bf16[256,256]{1,0:T(8,128)(2,1)S(1)}, u32[]{:S(2)}, u32[]{:S(2)}) collective-permute-start(bf16[256,256]{1,0:T(8,128)(2,1)S(1)} %collective-permute-done.2.refs_2_), channel_id=1, source_target_pairs={{0,8},{8,0},{16,24},{24,16},{1,9},{9,1},{17,25},{25,17},{2,10},{10... | collective-permute-start | bytes 393224 | tf_op jit(solution)/shard_map/ppermute | solution.py:21
  17.8 5.0 %collective-permute-start.13 = (bf16[256,256]{1,0:T(8,128)(2,1)S(1)}, bf16[256,256]{1,0:T(8,128)(2,1)S(1)}, u32[]{:S(2)}, u32[]{:S(2)}) collective-permute-start(bf16[256,256]{1,0:T(8,128)(2,1)S(1)} %collective-permute-done.8.refs_8_), channel_id=1, source_target_pairs={{0,1},{1,0},{2,3},{3,2},{4,5},{5,4},{6,7},{7,6},{8,9},{9,8},{10,11... | collective-permute-start | bytes 393224 | tf_op jit(solution)/shard_map/ppermute | solution.py:21
  19.2 3.6 %collective-permute-start.1 = (bf16[256,256]{1,0:T(8,128)(2,1)S(1)}, bf16[256,256]{1,0:T(8,128)(2,1)S(1)}, u32[]{:S(2)}, u32[]{:S(2)}) collective-permute-start(bf16[256,256]{1,0:T(8,128)(2,1)S(1)} %collective-permute-done.piece.refs_0_), channel_id=1, source_target_pairs={{0,8},{8,0},{16,24},{24,16},{1,9},{9,1},{17,25},{25,17},{2,10},{10... | collective-permute-start | bytes 393224 | tf_op jit(solution)/shard_map/ppermute | solution.py:21
  19.2 3.6 %collective-permute-start.10 = (bf16[256,256]{1,0:T(8,128)(2,1)S(1)}, bf16[256,256]{1,0:T(8,128)(2,1)S(1)}, u32[]{:S(2)}, u32[]{:S(2)}) collective-permute-start(bf16[256,256]{1,0:T(8,128)(2,1)S(1)} %collective-permute-done.8.refs_8_), channel_id=1, source_target_pairs={{0,8},{8,0},{16,24},{24,16},{1,9},{9,1},{17,25},{25,17},{2,10},{10... | collective-permute-start | bytes 393224 | tf_op jit(solution)/shard_map/ppermute | solution.py:21
  19.7 3.1 %collective-permute-start.12 = (bf16[256,256]{1,0:T(8,128)(2,1)S(1)}, bf16[256,256]{1,0:T(8,128)(2,1)S(1)}, u32[]{:S(2)}, u32[]{:S(2)}) collective-permute-start(bf16[256,256]{1,0:T(8,128)(2,1)S(1)} %collective-permute-done.11.refs_10_), channel_id=1, source_target_pairs={{0,8},{8,0},{16,24},{24,16},{1,9},{9,1},{17,25},{25,17},{2,10},{10... | collective-permute-start | bytes 393224 | tf_op jit(solution)/shard_map/ppermute | solution.py:21
  19.8 3.0 %collective-permute-start.5 = (bf16[256,256]{1,0:T(8,128)(2,1)S(1)}, bf16[256,256]{1,0:T(8,128)(2,1)S(1)}, u32[]{:S(2)}, u32[]{:S(2)}) collective-permute-start(bf16[256,256]{1,0:T(8,128)(2,1)S(1)} %collective-permute-done.4.refs_4_), channel_id=1, source_target_pairs={{0,8},{8,0},{16,24},{24,16},{1,9},{9,1},{17,25},{25,17},{2,10},{10... | collective-permute-start | bytes 393224 | tf_op jit(solution)/shard_map/ppermute | solution.py:21
  22.8 1.3 %collective-permute-start.14 = (bf16[256,256]{1,0:T(8,128)(2,1)S(1)}, bf16[256,256]{1,0:T(8,128)(2,1)S(1)}, u32[]{:S(2)}, u32[]{:S(2)}) collective-permute-start(bf16[256,256]{1,0:T(8,128)(2,1)S(1)} %collective-permute-done.13.refs_12_), channel_id=1, source_target_pairs={{0,8},{8,0},{16,24},{24,16},{1,9},{9,1},{17,25},{25,17},{2,10},{10... | collective-permute-start | bytes 393224 | tf_op jit(solution)/shard_map/ppermute | solution.py:21
  25.3 6.4 %collective-permute-start.17 = (bf16[256,256]{1,0:T(8,128)(2,1)S(1)}, bf16[256,256]{1,0:T(8,128)(2,1)S(1)}, u32[]{:S(2)}, u32[]{:S(2)}) collective-permute-start(bf16[256,256]{1,0:T(8,128)(2,1)S(1)} %get-tuple-element.17.local_t), channel_id=1, source_target_pairs={{0,1},{1,0},{2,3},{3,2},{4,5},{5,4},{6,7},{7,6},{8,9},{9,8},{10,11... | collective-permute-start | bytes 393224 | tf_op jit(solution)/shard_map/ppermute | solution.py:21
  26.4 10.6 %collective-permute-start.15 = (bf16[256,512]{1,0:T(8,128)(2,1)S(1)}, bf16[256,512]{1,0:T(8,128)(2,1)S(1)}, u32[]{:S(2)}, u32[]{:S(2)}) collective-permute-start(bf16[256,512]{1,0:T(8,128)(2,1)S(1)} %get-tuple-element.18), channel_id=1, source_target_pairs={{0,1},{1,0},{2,3},{3,2},{4,5},{5,4},{6,7},{7,6},{8,9},{9,8},{10,11... | collective-permute-start | bytes 786440 | tf_op jit(solution)/shard_map/ppermute | solution.py:21
  32.1 6.9 %collective-permute-start.19 = (bf16[256,512]{1,0:T(8,128)(2,1)S(1)}, bf16[256,512]{1,0:T(8,128)(2,1)S(1)}, u32[]{:S(2)}, u32[]{:S(2)}) collective-permute-start(bf16[256,512]{1,0:T(8,128)(2,1)S(1)} %get-tuple-element.20), channel_id=1, source_target_pairs={{0,2},{1,3},{6,4},{7,5},{8,10},{9,11},{14,12},{15,13},{16,18},{17,... | collective-permute-start | bytes 786440 | tf_op jit(solution)/shard_map/ppermute | solution.py:25
  34.8 12.2 %collective-permute-start.18 = (bf16[256,512]{1,0:T(8,128)(2,1)S(1)}, bf16[256,512]{1,0:T(8,128)(2,1)S(1)}, u32[]{:S(2)}, u32[]{:S(2)}) collective-permute-start(bf16[256,512]{1,0:T(8,128)(2,1)S(1)} %get-tuple-element.20), channel_id=1, source_target_pairs={{2,4},{3,5},{4,2},{5,3},{10,12},{11,13},{12,10},{13,11},{18,20},{1... | collective-permute-start | bytes 786440 | tf_op jit(solution)/shard_map/ppermute | solution.py:25
  35.5 9.3 %collective-permute-start.21 = (bf16[256,512]{1,0:T(8,128)(2,1)S(1)}, bf16[256,512]{1,0:T(8,128)(2,1)S(1)}, u32[]{:S(2)}, u32[]{:S(2)}) collective-permute-start(bf16[256,512]{1,0:T(8,128)(2,1)S(1)} %get-tuple-element.22), channel_id=1, source_target_pairs={{0,1},{1,0},{2,3},{3,2},{4,5},{5,4},{6,7},{7,6},{8,9},{9,8},{10,11... | collective-permute-start | bytes 786440 | tf_op jit(solution)/shard_map/ppermute | solution.py:21
  37.4 10.3 %collective-permute-start.16 = (bf16[256,512]{1,0:T(8,128)(2,1)S(1)}, bf16[256,512]{1,0:T(8,128)(2,1)S(1)}, u32[]{:S(2)}, u32[]{:S(2)}) collective-permute-start(bf16[256,512]{1,0:T(8,128)(2,1)S(1)} %get-tuple-element.19), channel_id=1, source_target_pairs={{0,1},{1,0},{2,3},{3,2},{4,5},{5,4},{6,7},{7,6},{8,9},{9,8},{10,11... | collective-permute-start | bytes 786440 | tf_op jit(solution)/shard_map/ppermute | solution.py:21
  39.2 14.2 %collective-permute-start.20 = (bf16[256,512]{1,0:T(8,128)(2,1)S(1)}, bf16[256,512]{1,0:T(8,128)(2,1)S(1)}, u32[]{:S(2)}, u32[]{:S(2)}) collective-permute-start(bf16[256,512]{1,0:T(8,128)(2,1)S(1)} %shard_map.41), channel_id=1, source_target_pairs={{0,4},{1,5},{2,6},{3,7},{4,0},{5,1},{6,2},{7,3},{8,12},{9,13},{10,... | collective-permute-start | bytes 786440 | tf_op jit(solution)/shard_map/ppermute | solution.py:21
  45.1 9.8 %collective-permute-start.22 = (bf16[256,512]{1,0:T(8,128)(2,1)S(1)}, bf16[256,512]{1,0:T(8,128)(2,1)S(1)}, u32[]{:S(2)}, u32[]{:S(2)}) collective-permute-start(bf16[256,512]{1,0:T(8,128)(2,1)S(1)} %shard_map.43), channel_id=1, source_target_pairs={{0,2},{1,3},{2,0},{3,1},{4,6},{5,7},{6,4},{7,5},{8,10},{9,11},{10,... | collective-permute-start | bytes 786440 | tf_op jit(solution)/shard_map/ppermute | solution.py:21
  55.2 2.3 %collective-permute-start.23 = (bf16[64,512]{1,0:T(8,128)(2,1)S(1)}, bf16[64,512]{1,0:T(8,128)(2,1)S(1)}, u32[]{:S(2)}, u32[]{:S(2)}) collective-permute-start(bf16[64,512]{1,0:T(8,128)(2,1)S(1)} %get-tuple-element.24), channel_id=1, source_target_pairs={{0,8},{8,0},{16,24},{24,16},{1,9},{9,1},{17,25},{25,17},{2,10},{10... | collective-permute-start | bytes 196616 | tf_op jit(solution)/shard_map/ppermute | solution.py:21
  55.3 4.9 %collective-permute-start.24 = (bf16[64,512]{1,0:T(8,128)(2,1)S(1)}, bf16[64,512]{1,0:T(8,128)(2,1)S(1)}, u32[]{:S(2)}, u32[]{:S(2)}) collective-permute-start(bf16[64,512]{1,0:T(8,128)(2,1)S(1)} %get-tuple-element.25), channel_id=1, source_target_pairs={{0,16},{8,24},{16,0},{24,8},{1,17},{9,25},{17,1},{25,9},{2,18},{10... | collective-permute-start | bytes 196616 | tf_op jit(solution)/shard_map/ppermute | solution.py:21
  57.5 4.0 %collective-permute-start.25 = (bf16[64,512]{1,0:T(8,128)(2,1)S(1)}, bf16[64,512]{1,0:T(8,128)(2,1)S(1)}, u32[]{:S(2)}, u32[]{:S(2)}) collective-permute-start(bf16[64,512]{1,0:T(8,128)(2,1)S(1)} %get-tuple-element.26), channel_id=1, source_target_pairs={{0,24},{8,16},{16,8},{24,0},{1,25},{9,17},{17,9},{25,1},{2,26},{10... | collective-permute-start | bytes 196616 | tf_op jit(solution)/shard_map/ppermute | solution.py:21

commit v6 on v5

--- a/solution.py
+++ b/solution.py
@@ -185,7 +185,7 @@
     share = hidden // examples
     part = lambda dtype: jax.ShapeDtypeStruct((share, rows), dtype)
     own, *others = call(square_kernel, [part(F32)] + [part(BF16)] * (examples - 1), grad, two)
-    others = [hop(x, "example", k + 1) for k, x in enumerate(others)]
+    others = [hop(others[k - 1], "example", k) for k in (3, 2, 1)]
     (total,) = call(
         functools.partial(mean_kernel, 1.0 / (tokens * count * examples)),
         (part(F32),), own, *others,

time: 62.4 us -> 61.5 us (0.986)
  waiting for transfers between devices: 28 us -> 27.2 us
    ppermute x23, waiting for transfers between devices: 25.4 us -> 24.5 us  [hop(): lax.ppermute(x, axis, [(i, i ^ k) for i in range(lax.axis_size(axis))])]
where the time goes in v6:
time: 61.5 us; the launch traced here: 61.3 us
  starting transfers between devices  27.9 us (45%)
  waiting for transfers between devices  27.2 us (44%)
  Pallas kernels  4.21 us (7%)
  local copies, waits for them, and re-layouts  1.9 us (3%)
    ppermute x23, waiting for transfers between devices, hop(): lax.ppermute(x, axis, [(i, i ^ k) for i in range(lax.axis_size(axis))])  24.5 us
    ppermute x23, starting transfers between devices, hop(): lax.ppermute(x, axis, [(i, i ^ k) for i in range(lax.axis_size(axis))])  20.4 us
    pallas_call x9, Pallas kernels, call(): pl.pallas_call(kernel, out_shape=tuple(outs), in_specs=[vmem] * len(opera...  4.21 us
    ppermute x1, starting transfers between devices, direct(): lax.ppermute(half, everyone, across)  4.1 us
    ppermute x2, starting transfers between devices, move(): return lax.ppermute(x, axis, [(i, i ^ k) for i, k in hops.items()])  3.38 us
    ppermute x1, waiting for transfers between devices, direct(): lax.ppermute(half, everyone, across)  1.74 us
  transfers between devices with their start and end apart: 26, of which 14 were waited for; matrix products, arithmetic and copies ran while one was open for 2% of the time, Pallas kernels for 3%

profile of v6, /device:TPU:0, one launch (start us, length us, event | category | flops | bytes accessed | tf_op | source)
XLA Modules:
  0.0 61.3 jit_solution(12443270465965257898)
XLA Ops:
  0.0 0.9 %constant_dynamic-slice_fusion = bf16[256,256]{1,0:T(8,128)(2,1)S(1)} fusion(bf16[512,256]{1,0:T(8,128)(2,1)} %own.1, s32[]{:T(128)S(6)} %select_n.6), kind=kLoop, calls=%fused_computation.1 | loop fusion | bytes 262148 | tf_op jit(solution)/shard_map/dynamic_slice | solution.py:142
  0.9 4.1 %collective-permute-start.6 = (bf16[256,256]{1,0:T(8,128)(2,1)S(1)}, bf16[256,256]{1,0:T(8,128)(2,1)S(1)}, u32[]{:S(2)}, u32[]{:S(2)}) collective-permute-start(bf16[256,256]{1,0:T(8,128)(2,1)S(1)} %constant_dynamic-slice_fusion), channel_id=1, source_target_pairs={{0,4},{1,5},{2,6},{3,7},{4,0},{5,1},{6,2},{7,3},{8,12},{9,13},{10,... | collective-permute-start | bytes 393224 | tf_op jit(solution)/shard_map/ppermute | solution.py:146
  5.0 1.5 %collective-permute-start = (bf16[256,256]{1,0:T(8,128)(2,1)S(1)}, bf16[256,256]{1,0:T(8,128)(2,1)S(1)}, u32[]{:S(2)}, u32[]{:S(2)}) collective-permute-start(bf16[256,256]{1,0:T(8,128)(2,1)S(1)} %constant_dynamic-slice_fusion), channel_id=1, source_target_pairs={{0,1},{1,0},{2,3},{3,2},{4,5},{5,4},{6,7},{7,6},{8,9},{9,8},{10,11... | collective-permute-start | bytes 393224 | tf_op jit(solution)/shard_map/ppermute | solution.py:21
  6.5 1.6 %collective-permute-start.2 = (bf16[256,256]{1,0:T(8,128)(2,1)S(1)}, bf16[256,256]{1,0:T(8,128)(2,1)S(1)}, u32[]{:S(2)}, u32[]{:S(2)}) collective-permute-start(bf16[256,256]{1,0:T(8,128)(2,1)S(1)} %constant_dynamic-slice_fusion), channel_id=1, source_target_pairs={{0,2},{1,3},{2,0},{3,1},{4,6},{5,7},{6,4},{7,5},{8,10},{9,11},{10,... | collective-permute-start | bytes 393224 | tf_op jit(solution)/shard_map/ppermute | solution.py:21
  8.1 1.0 %dynamic-slice_bitcast_fusion = bf16[256,512]{1,0:T(8,128)(2,1)S(1)} fusion(bf16[1,256,4096]{2,1,0:T(8,128)(2,1)} %param.3, s32[]{:T(128)S(6)} %select_n.7), kind=kLoop, calls=%fused_computation | loop fusion | bytes 524292 | tf_op jit(solution)/shard_map/dynamic_slice | solution.py:150
  9.1 0.0 copy-start
  9.1 0.0 copy-start.1
  9.1 0.0 copy-start.2
  9.1 0.6 collective-permute-start.9
  9.7 1.7 %collective-permute-done.6.refs_6_ = bf16[256,256]{1,0:T(8,128)(2,1)S(1)} collective-permute-done((bf16[256,256]{1,0:T(8,128)(2,1)S(1)}, bf16[256,256]{1,0:T(8,128)(2,1)S(1)}, u32[]{:S(2)}, u32[]{:S(2)}) %collective-permute-start.6) | collective-permute-done | bytes 131104 | tf_op jit(solution)/shard_map/ppermute | solution.py:146
  11.4 0.7 %collective-permute-start.8 = (bf16[256,256]{1,0:T(8,128)(2,1)S(1)}, bf16[256,256]{1,0:T(8,128)(2,1)S(1)}, u32[]{:S(2)}, u32[]{:S(2)}) collective-permute-start(bf16[256,256]{1,0:T(8,128)(2,1)S(1)} %collective-permute-done.6.refs_6_), channel_id=1, source_target_pairs={{0,16},{8,24},{16,0},{24,8},{1,17},{9,25},{17,1},{25,9},{2,18},{10... | collective-permute-start | bytes 393224 | tf_op jit(solution)/shard_map/ppermute | solution.py:21
  12.1 0.0 collective-permute-done.piece.refs_0_
  12.1 1.5 %collective-permute-start.4 = (bf16[256,256]{1,0:T(8,128)(2,1)S(1)}, bf16[256,256]{1,0:T(8,128)(2,1)S(1)}, u32[]{:S(2)}, u32[]{:S(2)}) collective-permute-start(bf16[256,256]{1,0:T(8,128)(2,1)S(1)} %shard_map.37), channel_id=1, source_target_pairs={{0,2},{1,3},{2,0},{3,1},{4,6},{5,7},{6,4},{7,5},{8,10},{9,11},{10,... | collective-permute-start | bytes 393224 | tf_op jit(solution)/shard_map/ppermute | solution.py:21
  13.6 1.5 %collective-permute-start.11 = (bf16[256,256]{1,0:T(8,128)(2,1)S(1)}, bf16[256,256]{1,0:T(8,128)(2,1)S(1)}, u32[]{:S(2)}, u32[]{:S(2)}) collective-permute-start(bf16[256,256]{1,0:T(8,128)(2,1)S(1)} %collective-permute-done.6.refs_6_), channel_id=1, source_target_pairs={{0,1},{1,0},{2,3},{3,2},{4,5},{5,4},{6,7},{7,6},{8,9},{9,8},{10,11... | collective-permute-start | bytes 393224 | tf_op jit(solution)/shard_map/ppermute | solution.py:21
  15.1 0.0 collective-permute-done.2.refs_2_
  15.1 0.0 collective-permute-start.7
  15.2 1.2 %collective-permute-done.8.refs_8_ = bf16[256,256]{1,0:T(8,128)(2,1)S(1)} collective-permute-done((bf16[256,256]{1,0:T(8,128)(2,1)S(1)}, bf16[256,256]{1,0:T(8,128)(2,1)S(1)}, u32[]{:S(2)}, u32[]{:S(2)}) %collective-permute-start.8) | collective-permute-done | bytes 131104 | tf_op jit(solution)/shard_map/ppermute | solution.py:21
  16.4 0.0 collective-permute-start.3
  16.4 1.4 %collective-permute-done.9.other_a = bf16[256,512]{1,0:T(8,128)(2,1)S(1)} collective-permute-done((bf16[256,512]{1,0:T(8,128)(2,1)S(1)}, bf16[256,512]{1,0:T(8,128)(2,1)S(1)}, u32[]{:S(2)}, u32[]{:S(2)}) %collective-permute-start.9) | collective-permute-done | bytes 262176 | tf_op jit(solution)/shard_map/ppermute | solution.py:21
  17.8 0.2 collective-permute-start.13
  18.0 1.2 %collective-permute-done.11.refs_10_ = bf16[256,256]{1,0:T(8,128)(2,1)S(1)} collective-permute-done((bf16[256,256]{1,0:T(8,128)(2,1)S(1)}, bf16[256,256]{1,0:T(8,128)(2,1)S(1)}, u32[]{:S(2)}, u32[]{:S(2)}) %collective-permute-start.11) | collective-permute-done | bytes 131104 | tf_op jit(solution)/shard_map/ppermute | solution.py:21
  19.2 0.0 collective-permute-start.1
  19.2 0.0 collective-permute-done.7.refs_7_
  19.2 0.5 collective-permute-start.10
  19.7 0.0 collective-permute-done.3.refs_3_
  19.7 0.1 collective-permute-start.12
  19.8 0.0 collective-permute-done.4.refs_4_
  19.8 0.4 collective-permute-start.5
  20.2 2.5 %collective-permute-done.13.refs_12_ = bf16[256,256]{1,0:T(8,128)(2,1)S(1)} collective-permute-done((bf16[256,256]{1,0:T(8,128)(2,1)S(1)}, bf16[256,256]{1,0:T(8,128)(2,1)S(1)}, u32[]{:S(2)}, u32[]{:S(2)}) %collective-permute-start.13) | collective-permute-done | bytes 131104 | tf_op jit(solution)/shard_map/ppermute | solution.py:21
  22.8 0.0 collective-permute-start.14
  22.8 0.0 collective-permute-done.1.refs_1_
  22.8 0.0 collective-permute-done.12.refs_11_
  22.8 0.0 collective-permute-done.5.refs_5_
  22.8 0.0 collective-permute-done.10.refs_9_
  22.8 1.3 %collective-permute-done.14.refs_13_ = bf16[256,256]{1,0:T(8,128)(2,1)S(1)} collective-permute-done((bf16[256,256]{1,0:T(8,128)(2,1)S(1)}, bf16[256,256]{1,0:T(8,128)(2,1)S(1)}, u32[]{:S(2)}, u32[]{:S(2)}) %collective-permute-start.14) | collective-permute-done | bytes 131104 | tf_op jit(solution)/shard_map/ppermute | solution.py:21
  24.1 1.1 %shard_map.38 = (bf16[256,512]{1,0:T(8,128)(2,1)S(1)}, bf16[256,256]{1,0:T(8,128)(2,1)S(1)}) custom-call(bf16[256,4096]{1,0:T(8,128)(2,1)S(1)} %bitcast.5, bf16[256,256]{1,0:T(8,128)(2,1)S(1)} %bitcast.10, bf16[512,256]{1,0:T(8,128)(2,1)S(1)} %copy-done.1, bf16[256,256]{1,0:T(8,128)(2,1)S(1)} %collective-permute-done.piece.refs_0_, ...), custom_call_target="tpu_custom_call" | custom-call | flops 20000000000 | bytes 4718592 | tf_op jit(solution)/shard_map/pallas_call | solution.py:35
  25.3 1.2 %collective-permute-start.17 = (bf16[256,256]{1,0:T(8,128)(2,1)S(1)}, bf16[256,256]{1,0:T(8,128)(2,1)S(1)}, u32[]{:S(2)}, u32[]{:S(2)}) collective-permute-start(bf16[256,256]{1,0:T(8,128)(2,1)S(1)} %get-tuple-element.17.local_t), channel_id=1, source_target_pairs={{0,1},{1,0},{2,3},{3,2},{4,5},{5,4},{6,7},{7,6},{8,9},{9,8},{10,11... | collective-permute-start | bytes 393224 | tf_op jit(solution)/shard_map/ppermute | solution.py:21
  26.4 0.9 %collective-permute-start.15 = (bf16[256,512]{1,0:T(8,128)(2,1)S(1)}, bf16[256,512]{1,0:T(8,128)(2,1)S(1)}, u32[]{:S(2)}, u32[]{:S(2)}) collective-permute-start(bf16[256,512]{1,0:T(8,128)(2,1)S(1)} %get-tuple-element.18), channel_id=1, source_target_pairs={{0,1},{1,0},{2,3},{3,2},{4,5},{5,4},{6,7},{7,6},{8,9},{9,8},{10,11... | collective-permute-start | bytes 786440 | tf_op jit(solution)/shard_map/ppermute | solution.py:21
  27.3 4.3 %collective-permute-done.17.other_t = bf16[256,256]{1,0:T(8,128)(2,1)S(1)} collective-permute-done((bf16[256,256]{1,0:T(8,128)(2,1)S(1)}, bf16[256,256]{1,0:T(8,128)(2,1)S(1)}, u32[]{:S(2)}, u32[]{:S(2)}) %collective-permute-start.17) | collective-permute-done | bytes 131104 | tf_op jit(solution)/shard_map/ppermute | solution.py:21
  31.7 0.4 shard_map.40
  32.1 2.7 %collective-permute-start.19 = (bf16[256,512]{1,0:T(8,128)(2,1)S(1)}, bf16[256,512]{1,0:T(8,128)(2,1)S(1)}, u32[]{:S(2)}, u32[]{:S(2)}) collective-permute-start(bf16[256,512]{1,0:T(8,128)(2,1)S(1)} %get-tuple-element.20), channel_id=1, source_target_pairs={{0,2},{1,3},{6,4},{7,5},{8,10},{9,11},{14,12},{15,13},{16,18},{17,... | collective-permute-start | bytes 786440 | tf_op jit(solution)/shard_map/ppermute | solution.py:25
  34.8 0.7 %collective-permute-start.18 = (bf16[256,512]{1,0:T(8,128)(2,1)S(1)}, bf16[256,512]{1,0:T(8,128)(2,1)S(1)}, u32[]{:S(2)}, u32[]{:S(2)}) collective-permute-start(bf16[256,512]{1,0:T(8,128)(2,1)S(1)} %get-tuple-element.20), channel_id=1, source_target_pairs={{2,4},{3,5},{4,2},{5,3},{10,12},{11,13},{12,10},{13,11},{18,20},{1... | collective-permute-start | bytes 786440 | tf_op jit(solution)/shard_map/ppermute | solution.py:25
  35.5 1.5 %collective-permute-start.21 = (bf16[256,512]{1,0:T(8,128)(2,1)S(1)}, bf16[256,512]{1,0:T(8,128)(2,1)S(1)}, u32[]{:S(2)}, u32[]{:S(2)}) collective-permute-start(bf16[256,512]{1,0:T(8,128)(2,1)S(1)} %get-tuple-element.22), channel_id=1, source_target_pairs={{0,1},{1,0},{2,3},{3,2},{4,5},{5,4},{6,7},{7,6},{8,9},{9,8},{10,11... | collective-permute-start | bytes 786440 | tf_op jit(solution)/shard_map/ppermute | solution.py:21
  37.0 0.0 collective-permute-done.15.refs_0_
  37.0 0.4 shard_map.39
  37.4 0.7 %collective-permute-start.16 = (bf16[256,512]{1,0:T(8,128)(2,1)S(1)}, bf16[256,512]{1,0:T(8,128)(2,1)S(1)}, u32[]{:S(2)}, u32[]{:S(2)}) collective-permute-start(bf16[256,512]{1,0:T(8,128)(2,1)S(1)} %get-tuple-element.19), channel_id=1, source_target_pairs={{0,1},{1,0},{2,3},{3,2},{4,5},{5,4},{6,7},{7,6},{8,9},{9,8},{10,11... | collective-permute-start | bytes 786440 | tf_op jit(solution)/shard_map/ppermute | solution.py:21
  38.1 0.9 %collective-permute-done.19.refs_0_ = bf16[256,512]{1,0:T(8,128)(2,1)S(1)} collective-permute-done((bf16[256,512]{1,0:T(8,128)(2,1)S(1)}, bf16[256,512]{1,0:T(8,128)(2,1)S(1)}, u32[]{:S(2)}, u32[]{:S(2)}) %collective-permute-start.19) | collective-permute-done | bytes 262176 | tf_op jit(solution)/shard_map/ppermute | solution.py:25
  39.0 0.3 shard_map.41
  39.2 3.5 %collective-permute-start.20 = (bf16[256,512]{1,0:T(8,128)(2,1)S(1)}, bf16[256,512]{1,0:T(8,128)(2,1)S(1)}, u32[]{:S(2)}, u32[]{:S(2)}) collective-permute-start(bf16[256,512]{1,0:T(8,128)(2,1)S(1)} %shard_map.41), channel_id=1, source_target_pairs={{0,4},{1,5},{2,6},{3,7},{4,0},{5,1},{6,2},{7,3},{8,12},{9,13},{10,... | collective-permute-start | bytes 786440 | tf_op jit(solution)/shard_map/ppermute | solution.py:21
  42.7 2.1 %collective-permute-done.21.refs_0_ = bf16[256,512]{1,0:T(8,128)(2,1)S(1)} collective-permute-done((bf16[256,512]{1,0:T(8,128)(2,1)S(1)}, bf16[256,512]{1,0:T(8,128)(2,1)S(1)}, u32[]{:S(2)}, u32[]{:S(2)}) %collective-permute-start.21) | collective-permute-done | bytes 262176 | tf_op jit(solution)/shard_map/ppermute | solution.py:21
  44.8 0.4 shard_map.43
  45.1 1.8 %collective-permute-start.22 = (bf16[256,512]{1,0:T(8,128)(2,1)S(1)}, bf16[256,512]{1,0:T(8,128)(2,1)S(1)}, u32[]{:S(2)}, u32[]{:S(2)}) collective-permute-start(bf16[256,512]{1,0:T(8,128)(2,1)S(1)} %shard_map.43), channel_id=1, source_target_pairs={{0,2},{1,3},{2,0},{3,1},{4,6},{5,7},{6,4},{7,5},{8,10},{9,11},{10,... | collective-permute-start | bytes 786440 | tf_op jit(solution)/shard_map/ppermute | solution.py:21
  46.9 0.0 collective-permute-done.18.refs_1_
  46.9 0.8 %collective-permute-done.16.refs_0_ = bf16[256,512]{1,0:T(8,128)(2,1)S(1)} collective-permute-done((bf16[256,512]{1,0:T(8,128)(2,1)S(1)}, bf16[256,512]{1,0:T(8,128)(2,1)S(1)}, u32[]{:S(2)}, u32[]{:S(2)}) %collective-permute-start.16) | collective-permute-done | bytes 262176 | tf_op jit(solution)/shard_map/ppermute | solution.py:21
  47.7 5.8 %collective-permute-done.20.refs_2_ = bf16[256,512]{1,0:T(8,128)(2,1)S(1)} collective-permute-done((bf16[256,512]{1,0:T(8,128)(2,1)S(1)}, bf16[256,512]{1,0:T(8,128)(2,1)S(1)}, u32[]{:S(2)}, u32[]{:S(2)}) %collective-permute-start.20) | collective-permute-done | bytes 262176 | tf_op jit(solution)/shard_map/ppermute | solution.py:21
  53.5 0.8 %shard_map.42.grad = f32[256,512]{1,0:T(8,128)S(1)} custom-call(bf16[256,4096]{1,0:T(8,128)(2,1)S(1)} %bitcast.9, bf16[256,256]{1,0:T(8,128)(2,1)S(1)} %get-tuple-element.17.local_t, bf16[256,512]{1,0:T(8,128)(2,1)S(1)} %collective-permute-done.16.refs_0_, bf16[256,512]{1,0:T(8,128)(2,1)S(1)} %collective-permute-done.18.refs_1_, ...), custom_call_target="tpu_custom_call" | custom-call | flops 20000000000 | bytes 3538944 | tf_op jit(solution)/shard_map/pallas_call | solution.py:35
  54.2 0.7 %collective-permute-done.22.last = bf16[256,512]{1,0:T(8,128)(2,1)S(1)} collective-permute-done((bf16[256,512]{1,0:T(8,128)(2,1)S(1)}, bf16[256,512]{1,0:T(8,128)(2,1)S(1)}, u32[]{:S(2)}, u32[]{:S(2)}) %collective-permute-start.22) | collective-permute-done | bytes 262176 | tf_op jit(solution)/shard_map/ppermute | solution.py:21
  55.0 0.2 shard_map.44
  55.2 0.1 collective-permute-start.23
  55.3 2.2 %collective-permute-start.24 = (bf16[64,512]{1,0:T(8,128)(2,1)S(1)}, bf16[64,512]{1,0:T(8,128)(2,1)S(1)}, u32[]{:S(2)}, u32[]{:S(2)}) collective-permute-start(bf16[64,512]{1,0:T(8,128)(2,1)S(1)} %get-tuple-element.25), channel_id=1, source_target_pairs={{0,16},{8,24},{16,0},{24,8},{1,17},{9,25},{17,1},{25,9},{2,18},{10... | collective-permute-start | bytes 196616 | tf_op jit(solution)/shard_map/ppermute | solution.py:21
  57.5 0.0 collective-permute-start.25
  57.5 1.5 %collective-permute-done.23.refs_0_ = bf16[64,512]{1,0:T(8,128)(2,1)S(1)} collective-permute-done((bf16[64,512]{1,0:T(8,128)(2,1)S(1)}, bf16[64,512]{1,0:T(8,128)(2,1)S(1)}, u32[]{:S(2)}, u32[]{:S(2)}) %collective-permute-start.23) | collective-permute-done | bytes 65568 | tf_op jit(solution)/shard_map/ppermute | solution.py:21
  59.1 1.6 %collective-permute-done.24.refs_1_ = bf16[64,512]{1,0:T(8,128)(2,1)S(1)} collective-permute-done((bf16[64,512]{1,0:T(8,128)(2,1)S(1)}, bf16[64,512]{1,0:T(8,128)(2,1)S(1)}, u32[]{:S(2)}, u32[]{:S(2)}) %collective-permute-start.24) | collective-permute-done | bytes 65568 | tf_op jit(solution)/shard_map/ppermute | solution.py:21
  60.6 0.7 %shard_map.45 = f32[64,512]{1,0:T(8,128)} custom-call(f32[64,512]{1,0:T(8,128)S(1)} %get-tuple-element.23.own, bf16[64,512]{1,0:T(8,128)(2,1)S(1)} %collective-permute-done.23.refs_0_, bf16[64,512]{1,0:T(8,128)(2,1)S(1)} %collective-permute-done.24.refs_1_, bf16[64,512]{1,0:T(8,128)(2,1)S(1)} %collective-permute-done.25.refs_2_), custom_call_target="tpu_custom_call" | custom-call | flops 20000000000 | bytes 458752 | tf_op jit(solution)/shard_map/pallas_call | solution.py:35
  (5 shorter events, 0.0 us)
Async XLA Ops:
  0.9 10.5 %collective-permute-start.6 = (bf16[256,256]{1,0:T(8,128)(2,1)S(1)}, bf16[256,256]{1,0:T(8,128)(2,1)S(1)}, u32[]{:S(2)}, u32[]{:S(2)}) collective-permute-start(bf16[256,256]{1,0:T(8,128)(2,1)S(1)} %constant_dynamic-slice_fusion), channel_id=1, source_target_pairs={{0,4},{1,5},{2,6},{3,7},{4,0},{5,1},{6,2},{7,3},{8,12},{9,13},{10,... | collective-permute-start | bytes 393224 | tf_op jit(solution)/shard_map/ppermute | solution.py:146
  5.0 7.1 %collective-permute-start = (bf16[256,256]{1,0:T(8,128)(2,1)S(1)}, bf16[256,256]{1,0:T(8,128)(2,1)S(1)}, u32[]{:S(2)}, u32[]{:S(2)}) collective-permute-start(bf16[256,256]{1,0:T(8,128)(2,1)S(1)} %constant_dynamic-slice_fusion), channel_id=1, source_target_pairs={{0,1},{1,0},{2,3},{3,2},{4,5},{5,4},{6,7},{7,6},{8,9},{9,8},{10,11... | collective-permute-start | bytes 393224 | tf_op jit(solution)/shard_map/ppermute | solution.py:21
  6.5 8.6 %collective-permute-start.2 = (bf16[256,256]{1,0:T(8,128)(2,1)S(1)}, bf16[256,256]{1,0:T(8,128)(2,1)S(1)}, u32[]{:S(2)}, u32[]{:S(2)}) collective-permute-start(bf16[256,256]{1,0:T(8,128)(2,1)S(1)} %constant_dynamic-slice_fusion), channel_id=1, source_target_pairs={{0,2},{1,3},{2,0},{3,1},{4,6},{5,7},{6,4},{7,5},{8,10},{9,11},{10,... | collective-permute-start | bytes 393224 | tf_op jit(solution)/shard_map/ppermute | solution.py:21
  9.1 15.0 %copy-start = (bf16[1,256,4096]{2,1,0:T(8,128)(2,1)S(1)}, bf16[1,256,4096]{2,1,0:T(8,128)(2,1)}, u32[]{:S(2)}) copy-start(bf16[1,256,4096]{2,1,0:T(8,128)(2,1)} %param.3) | copy-start | bytes 6291460
  9.1 15.0 %copy-start.1 = (bf16[512,256]{1,0:T(8,128)(2,1)S(1)}, bf16[512,256]{1,0:T(8,128)(2,1)}, u32[]{:S(2)}) copy-start(bf16[512,256]{1,0:T(8,128)(2,1)} %own.1) | copy-start | bytes 786436
  9.1 15.0 %copy-start.2 = (bf16[1,256,256]{2,1,0:T(8,128)(2,1)S(1)}, bf16[1,256,256]{2,1,0:T(8,128)(2,1)}, u32[]{:S(2)}) copy-start(bf16[1,256,256]{2,1,0:T(8,128)(2,1)} %param.5) | copy-start | bytes 393220
  9.1 8.7 %collective-permute-start.9 = (bf16[256,512]{1,0:T(8,128)(2,1)S(1)}, bf16[256,512]{1,0:T(8,128)(2,1)S(1)}, u32[]{:S(2)}, u32[]{:S(2)}) collective-permute-start(bf16[256,512]{1,0:T(8,128)(2,1)S(1)} %dynamic-slice_bitcast_fusion), channel_id=1, source_target_pairs={{0,1},{1,0},{2,3},{3,2},{4,5},{5,4},{6,7},{7,6},{8,9},{9,8},{10,11... | collective-permute-start | bytes 786440 | tf_op jit(solution)/shard_map/ppermute | solution.py:21
  11.4 5.0 %collective-permute-start.8 = (bf16[256,256]{1,0:T(8,128)(2,1)S(1)}, bf16[256,256]{1,0:T(8,128)(2,1)S(1)}, u32[]{:S(2)}, u32[]{:S(2)}) collective-permute-start(bf16[256,256]{1,0:T(8,128)(2,1)S(1)} %collective-permute-done.6.refs_6_), channel_id=1, source_target_pairs={{0,16},{8,24},{16,0},{24,8},{1,17},{9,25},{17,1},{25,9},{2,18},{10... | collective-permute-start | bytes 393224 | tf_op jit(solution)/shard_map/ppermute | solution.py:21
  12.1 7.7 %collective-permute-start.4 = (bf16[256,256]{1,0:T(8,128)(2,1)S(1)}, bf16[256,256]{1,0:T(8,128)(2,1)S(1)}, u32[]{:S(2)}, u32[]{:S(2)}) collective-permute-start(bf16[256,256]{1,0:T(8,128)(2,1)S(1)} %shard_map.37), channel_id=1, source_target_pairs={{0,2},{1,3},{2,0},{3,1},{4,6},{5,7},{6,4},{7,5},{8,10},{9,11},{10,... | collective-permute-start | bytes 393224 | tf_op jit(solution)/shard_map/ppermute | solution.py:21
  13.6 5.6 %collective-permute-start.11 = (bf16[256,256]{1,0:T(8,128)(2,1)S(1)}, bf16[256,256]{1,0:T(8,128)(2,1)S(1)}, u32[]{:S(2)}, u32[]{:S(2)}) collective-permute-start(bf16[256,256]{1,0:T(8,128)(2,1)S(1)} %collective-permute-done.6.refs_6_), channel_id=1, source_target_pairs={{0,1},{1,0},{2,3},{3,2},{4,5},{5,4},{6,7},{7,6},{8,9},{9,8},{10,11... | collective-permute-start | bytes 393224 | tf_op jit(solution)/shard_map/ppermute | solution.py:21
  15.1 4.1 %collective-permute-start.7 = (bf16[256,256]{1,0:T(8,128)(2,1)S(1)}, bf16[256,256]{1,0:T(8,128)(2,1)S(1)}, u32[]{:S(2)}, u32[]{:S(2)}) collective-permute-start(bf16[256,256]{1,0:T(8,128)(2,1)S(1)} %collective-permute-done.6.refs_6_), channel_id=1, source_target_pairs={{0,8},{8,0},{16,24},{24,16},{1,9},{9,1},{17,25},{25,17},{2,10},{10... | collective-permute-start | bytes 393224 | tf_op jit(solution)/shard_map/ppermute | solution.py:21
  16.4 3.3 %collective-permute-start.3 = (bf16[256,256]{1,0:T(8,128)(2,1)S(1)}, bf16[256,256]{1,0:T(8,128)(2,1)S(1)}, u32[]{:S(2)}, u32[]{:S(2)}) collective-permute-start(bf16[256,256]{1,0:T(8,128)(2,1)S(1)} %collective-permute-done.2.refs_2_), channel_id=1, source_target_pairs={{0,8},{8,0},{16,24},{24,16},{1,9},{9,1},{17,25},{25,17},{2,10},{10... | collective-permute-start | bytes 393224 | tf_op jit(solution)/shard_map/ppermute | solution.py:21
  17.8 5.0 %collective-permute-start.13 = (bf16[256,256]{1,0:T(8,128)(2,1)S(1)}, bf16[256,256]{1,0:T(8,128)(2,1)S(1)}, u32[]{:S(2)}, u32[]{:S(2)}) collective-permute-start(bf16[256,256]{1,0:T(8,128)(2,1)S(1)} %collective-permute-done.8.refs_8_), channel_id=1, source_target_pairs={{0,1},{1,0},{2,3},{3,2},{4,5},{5,4},{6,7},{7,6},{8,9},{9,8},{10,11... | collective-permute-start | bytes 393224 | tf_op jit(solution)/shard_map/ppermute | solution.py:21
  19.2 3.6 %collective-permute-start.1 = (bf16[256,256]{1,0:T(8,128)(2,1)S(1)}, bf16[256,256]{1,0:T(8,128)(2,1)S(1)}, u32[]{:S(2)}, u32[]{:S(2)}) collective-permute-start(bf16[256,256]{1,0:T(8,128)(2,1)S(1)} %collective-permute-done.piece.refs_0_), channel_id=1, source_target_pairs={{0,8},{8,0},{16,24},{24,16},{1,9},{9,1},{17,25},{25,17},{2,10},{10... | collective-permute-start | bytes 393224 | tf_op jit(solution)/shard_map/ppermute | solution.py:21
  19.2 3.6 %collective-permute-start.10 = (bf16[256,256]{1,0:T(8,128)(2,1)S(1)}, bf16[256,256]{1,0:T(8,128)(2,1)S(1)}, u32[]{:S(2)}, u32[]{:S(2)}) collective-permute-start(bf16[256,256]{1,0:T(8,128)(2,1)S(1)} %collective-permute-done.8.refs_8_), channel_id=1, source_target_pairs={{0,8},{8,0},{16,24},{24,16},{1,9},{9,1},{17,25},{25,17},{2,10},{10... | collective-permute-start | bytes 393224 | tf_op jit(solution)/shard_map/ppermute | solution.py:21
  19.7 3.1 %collective-permute-start.12 = (bf16[256,256]{1,0:T(8,128)(2,1)S(1)}, bf16[256,256]{1,0:T(8,128)(2,1)S(1)}, u32[]{:S(2)}, u32[]{:S(2)}) collective-permute-start(bf16[256,256]{1,0:T(8,128)(2,1)S(1)} %collective-permute-done.11.refs_10_), channel_id=1, source_target_pairs={{0,8},{8,0},{16,24},{24,16},{1,9},{9,1},{17,25},{25,17},{2,10},{10... | collective-permute-start | bytes 393224 | tf_op jit(solution)/shard_map/ppermute | solution.py:21
  19.8 3.0 %collective-permute-start.5 = (bf16[256,256]{1,0:T(8,128)(2,1)S(1)}, bf16[256,256]{1,0:T(8,128)(2,1)S(1)}, u32[]{:S(2)}, u32[]{:S(2)}) collective-permute-start(bf16[256,256]{1,0:T(8,128)(2,1)S(1)} %collective-permute-done.4.refs_4_), channel_id=1, source_target_pairs={{0,8},{8,0},{16,24},{24,16},{1,9},{9,1},{17,25},{25,17},{2,10},{10... | collective-permute-start | bytes 393224 | tf_op jit(solution)/shard_map/ppermute | solution.py:21
  22.8 1.3 %collective-permute-start.14 = (bf16[256,256]{1,0:T(8,128)(2,1)S(1)}, bf16[256,256]{1,0:T(8,128)(2,1)S(1)}, u32[]{:S(2)}, u32[]{:S(2)}) collective-permute-start(bf16[256,256]{1,0:T(8,128)(2,1)S(1)} %collective-permute-done.13.refs_12_), channel_id=1, source_target_pairs={{0,8},{8,0},{16,24},{24,16},{1,9},{9,1},{17,25},{25,17},{2,10},{10... | collective-permute-start | bytes 393224 | tf_op jit(solution)/shard_map/ppermute | solution.py:21
  25.3 6.4 %collective-permute-start.17 = (bf16[256,256]{1,0:T(8,128)(2,1)S(1)}, bf16[256,256]{1,0:T(8,128)(2,1)S(1)}, u32[]{:S(2)}, u32[]{:S(2)}) collective-permute-start(bf16[256,256]{1,0:T(8,128)(2,1)S(1)} %get-tuple-element.17.local_t), channel_id=1, source_target_pairs={{0,1},{1,0},{2,3},{3,2},{4,5},{5,4},{6,7},{7,6},{8,9},{9,8},{10,11... | collective-permute-start | bytes 393224 | tf_op jit(solution)/shard_map/ppermute | solution.py:21
  26.4 10.6 %collective-permute-start.15 = (bf16[256,512]{1,0:T(8,128)(2,1)S(1)}, bf16[256,512]{1,0:T(8,128)(2,1)S(1)}, u32[]{:S(2)}, u32[]{:S(2)}) collective-permute-start(bf16[256,512]{1,0:T(8,128)(2,1)S(1)} %get-tuple-element.18), channel_id=1, source_target_pairs={{0,1},{1,0},{2,3},{3,2},{4,5},{5,4},{6,7},{7,6},{8,9},{9,8},{10,11... | collective-permute-start | bytes 786440 | tf_op jit(solution)/shard_map/ppermute | solution.py:21
  32.1 6.9 %collective-permute-start.19 = (bf16[256,512]{1,0:T(8,128)(2,1)S(1)}, bf16[256,512]{1,0:T(8,128)(2,1)S(1)}, u32[]{:S(2)}, u32[]{:S(2)}) collective-permute-start(bf16[256,512]{1,0:T(8,128)(2,1)S(1)} %get-tuple-element.20), channel_id=1, source_target_pairs={{0,2},{1,3},{6,4},{7,5},{8,10},{9,11},{14,12},{15,13},{16,18},{17,... | collective-permute-start | bytes 786440 | tf_op jit(solution)/shard_map/ppermute | solution.py:25
  34.8 12.2 %collective-permute-start.18 = (bf16[256,512]{1,0:T(8,128)(2,1)S(1)}, bf16[256,512]{1,0:T(8,128)(2,1)S(1)}, u32[]{:S(2)}, u32[]{:S(2)}) collective-permute-start(bf16[256,512]{1,0:T(8,128)(2,1)S(1)} %get-tuple-element.20), channel_id=1, source_target_pairs={{2,4},{3,5},{4,2},{5,3},{10,12},{11,13},{12,10},{13,11},{18,20},{1... | collective-permute-start | bytes 786440 | tf_op jit(solution)/shard_map/ppermute | solution.py:25
  35.5 9.3 %collective-permute-start.21 = (bf16[256,512]{1,0:T(8,128)(2,1)S(1)}, bf16[256,512]{1,0:T(8,128)(2,1)S(1)}, u32[]{:S(2)}, u32[]{:S(2)}) collective-permute-start(bf16[256,512]{1,0:T(8,128)(2,1)S(1)} %get-tuple-element.22), channel_id=1, source_target_pairs={{0,1},{1,0},{2,3},{3,2},{4,5},{5,4},{6,7},{7,6},{8,9},{9,8},{10,11... | collective-permute-start | bytes 786440 | tf_op jit(solution)/shard_map/ppermute | solution.py:21
  37.4 10.3 %collective-permute-start.16 = (bf16[256,512]{1,0:T(8,128)(2,1)S(1)}, bf16[256,512]{1,0:T(8,128)(2,1)S(1)}, u32[]{:S(2)}, u32[]{:S(2)}) collective-permute-start(bf16[256,512]{1,0:T(8,128)(2,1)S(1)} %get-tuple-element.19), channel_id=1, source_target_pairs={{0,1},{1,0},{2,3},{3,2},{4,5},{5,4},{6,7},{7,6},{8,9},{9,8},{10,11... | collective-permute-start | bytes 786440 | tf_op jit(solution)/shard_map/ppermute | solution.py:21
  39.2 14.2 %collective-permute-start.20 = (bf16[256,512]{1,0:T(8,128)(2,1)S(1)}, bf16[256,512]{1,0:T(8,128)(2,1)S(1)}, u32[]{:S(2)}, u32[]{:S(2)}) collective-permute-start(bf16[256,512]{1,0:T(8,128)(2,1)S(1)} %shard_map.41), channel_id=1, source_target_pairs={{0,4},{1,5},{2,6},{3,7},{4,0},{5,1},{6,2},{7,3},{8,12},{9,13},{10,... | collective-permute-start | bytes 786440 | tf_op jit(solution)/shard_map/ppermute | solution.py:21
  45.1 9.8 %collective-permute-start.22 = (bf16[256,512]{1,0:T(8,128)(2,1)S(1)}, bf16[256,512]{1,0:T(8,128)(2,1)S(1)}, u32[]{:S(2)}, u32[]{:S(2)}) collective-permute-start(bf16[256,512]{1,0:T(8,128)(2,1)S(1)} %shard_map.43), channel_id=1, source_target_pairs={{0,2},{1,3},{2,0},{3,1},{4,6},{5,7},{6,4},{7,5},{8,10},{9,11},{10,... | collective-permute-start | bytes 786440 | tf_op jit(solution)/shard_map/ppermute | solution.py:21
  55.2 3.8 %collective-permute-start.23 = (bf16[64,512]{1,0:T(8,128)(2,1)S(1)}, bf16[64,512]{1,0:T(8,128)(2,1)S(1)}, u32[]{:S(2)}, u32[]{:S(2)}) collective-permute-start(bf16[64,512]{1,0:T(8,128)(2,1)S(1)} %get-tuple-element.24), channel_id=1, source_target_pairs={{0,24},{8,16},{16,8},{24,0},{1,25},{9,17},{17,9},{25,1},{2,26},{10... | collective-permute-start | bytes 196616 | tf_op jit(solution)/shard_map/ppermute | solution.py:21
  55.3 5.3 %collective-permute-start.24 = (bf16[64,512]{1,0:T(8,128)(2,1)S(1)}, bf16[64,512]{1,0:T(8,128)(2,1)S(1)}, u32[]{:S(2)}, u32[]{:S(2)}) collective-permute-start(bf16[64,512]{1,0:T(8,128)(2,1)S(1)} %get-tuple-element.25), channel_id=1, source_target_pairs={{0,16},{8,24},{16,0},{24,8},{1,17},{9,25},{17,1},{25,9},{2,18},{10... | collective-permute-start | bytes 196616 | tf_op jit(solution)/shard_map/ppermute | solution.py:21
  57.5 3.2 %collective-permute-start.25 = (bf16[64,512]{1,0:T(8,128)(2,1)S(1)}, bf16[64,512]{1,0:T(8,128)(2,1)S(1)}, u32[]{:S(2)}, u32[]{:S(2)}) collective-permute-start(bf16[64,512]{1,0:T(8,128)(2,1)S(1)} %get-tuple-element.26), channel_id=1, source_target_pairs={{0,8},{8,0},{16,24},{24,16},{1,9},{9,1},{17,25},{25,17},{2,10},{10... | collective-permute-start | bytes 196616 | tf_op jit(solution)/shard_map/ppermute | solution.py:21
